TPU v7x, 32 devices: a whole 2x2x4 slice. The times are simulated.
32 devices in a mesh: gx: 4 (over y, x), gy: 8 (over z, core).
Axes of the slice: x: 2, y: 2, z: 4, core: 2. Of those that a mesh axis runs over, the one named last changes fastest.
Arguments:
- ice_displacement: float32 [2, 32, 64, 128], P(None, 'gx', 'gy'), may hold values from -1.8 to 1.8
- ice_velocity: float32 [2, 32, 64, 128], P(None, 'gx', 'gy'), may hold values from -6 to 6
- jitter: float32 [2, 32, 64, 128], P(None, 'gx', 'gy'), may hold values from -0.2 to 0.2
- bond_mask: int32 [32, 64, 9], P('gx', 'gy'), may hold values from -2147483648 to 2147483647, as said below
- contact_node: int32 [64, 128], P('gy'), may hold values from 0 to 2097151, as said below
- intersection: float32 [64, 128], P('gy'), may hold values from -0.5 to 1
- shell_deflection: float32 [512, 4096], P('gx', 'gy'), may hold values from -1.8 to 1.8
- shell_velocity: float32 [512, 4096], P('gx', 'gy'), may hold values from -6 to 6
Outputs:
- ice_moved: float32 [2, 32, 64, 128], P(None, 'gx', 'gy')
- ice_speed: float32 [2, 32, 64, 128], P(None, 'gx', 'gy')
- shell_moved: float32 [512, 4096], P('gx', 'gy')
- shell_speed: float32 [512, 4096], P('gx', 'gy')
Inputs may be any that keep to these rules, and one draw needn't show every extreme that they name: Bit 4 * i + k of bond_mask[a, b, s] (bit 31 being the sign bit) is 1 where the bonds from the points of lengthwise row i of tile (a, b) to the points q with 4 q // 128 == k of neighbouring tile s are intact. contact_node = r * 4096 + c for shell row r and column c; for point q of tile column t, c // 4 == t * 16 + q % 16 and r // 64 == q // 16.
All inputs are finite; a program needn't handle non-finite values.
Results may differ from a plain program's by a relative error of at most 0.0001.
Values sent between devices are 32-bit elements; how exact they have to be, the bound alone decides.
No kernel may reach another device: no remote copies, remote signals or barrier semaphores. Data moves between devices by JAX's collectives and lax.ppermute only.
A program may use at most 64 MiB of HBM per device.

v0:
```python
import jax
import jax.numpy as jnp
from jax import lax
from jax.sharding import PartitionSpec as P

TILE_X = 8
TILE_Y = 16
PTS = 128
STEPS = 2


BOND_C = 1.0
HORIZON = 3.5
DELTA_SQ = 0.25
PENALTY = 4.0
BEND = 0.5
STEP_DT = 0.2


def extended(cells, sides, width):
    for axis, dim in sides:
        count = lax.axis_size(axis)
        ends = count - 1
        head = lax.slice_in_dim(cells, 0, width, axis=dim)
        tail = lax.slice_in_dim(cells, cells.shape[dim] - width, cells.shape[dim], axis=dim)
        cells = jnp.concatenate(
            [
                lax.ppermute(tail, axis, [(i, (i + 1) % count) for i in range(ends)]),
                cells,
                lax.ppermute(head, axis, [((i + 1) % count, i) for i in range(ends)]),
            ],
            axis=dim,
        )
    return cells


def spread(array, axis, root):
    mine = lax.axis_index(axis) == root
    return lax.psum(jnp.where(mine, array, jnp.zeros_like(array)), axis)


def pair_force(center, nearby, words, shift_x, shift_y):
    points = jnp.arange(TILE_X * TILE_Y, dtype=jnp.int32)
    bit_index = 4 * (points // TILE_Y)[:, None] + (4 * points // PTS)[None, :]
    intact = jnp.right_shift(words[..., None, None], bit_index) & 1
    lengthwise = (points // TILE_Y).astype(jnp.float32)
    sideways = (points % TILE_Y).astype(jnp.float32)
    base_x = shift_x * TILE_X + lengthwise[None, :] - lengthwise[:, None]
    base_y = shift_y * TILE_Y + sideways[None, :] - sideways[:, None]
    rest_x = base_x + (nearby[2][..., None, :] - center[2][..., :, None])
    rest_y = base_y + (nearby[3][..., None, :] - center[3][..., :, None])
    now_x = rest_x + (nearby[0][..., None, :] - center[0][..., :, None])
    now_y = rest_y + (nearby[1][..., None, :] - center[1][..., :, None])
    radius = jnp.sqrt(rest_x * rest_x + rest_y * rest_y + DELTA_SQ)
    stretched = jnp.sqrt(now_x * now_x + now_y * now_y + DELTA_SQ)
    reach = jnp.maximum(1.0 - radius / HORIZON, 0.0)
    factor = (
        BOND_C
        * intact.astype(jnp.float32)
        * reach
        * reach
        * (stretched - radius)
        / (radius * stretched)
    )
    return jnp.stack([jnp.sum(factor * now_x, axis=-1), jnp.sum(factor * now_y, axis=-1)])


def ice_forces(displacement, jitter_padded, bond_mask):
    tiles_x = displacement.shape[1]
    tiles_y = displacement.shape[2]
    moved_padded = extended(displacement, (("gx", 1), ("gy", 2)), 1)
    padded = jnp.concatenate([moved_padded, jitter_padded], axis=0)
    row_ids = lax.axis_index("gx") * tiles_x + jnp.arange(-1, tiles_x + 1, dtype=jnp.int32)
    col_ids = lax.axis_index("gy") * tiles_y + jnp.arange(-1, tiles_y + 1, dtype=jnp.int32)
    rows_ok = ((row_ids >= 0) & (row_ids < tiles_x * lax.axis_size("gx"))).astype(jnp.float32)
    cols_ok = ((col_ids >= 0) & (col_ids < tiles_y * lax.axis_size("gy"))).astype(jnp.float32)
    present = rows_ok[:, None] * cols_ok[None, :]
    center = padded[:, 1 : 1 + tiles_x, 1 : 1 + tiles_y]
    totals = jnp.zeros((2, tiles_x, tiles_y, displacement.shape[3]), jnp.float32)
    for offset in range(9):
        shift_x = offset // 3 - 1
        shift_y = offset % 3 - 1
        nearby = padded[:, 1 + shift_x : 1 + shift_x + tiles_x, 1 + shift_y : 1 + shift_y + tiles_y]
        weight = present[1 + shift_x : 1 + shift_x + tiles_x, 1 + shift_y : 1 + shift_y + tiles_y]
        totals = (
            totals
            + pair_force(center, nearby, bond_mask[:, :, offset], shift_x, shift_y)
            * weight[None, :, :, None]
        )
    return totals


def laplace(field):
    return (
        field[2:, 1:-1]
        + field[:-2, 1:-1]
        + field[1:-1, 2:]
        + field[1:-1, :-2]
        - 4.0 * field[1:-1, 1:-1]
    )


def on_device(
    ice_displacement,
    ice_velocity,
    jitter,
    bond_mask,
    contact_node,
    intersection,
    shell_deflection,
    shell_velocity,
):
    shell_rows = shell_deflection.shape[0]
    shell_cols = shell_deflection.shape[1]
    node_count = shell_rows * shell_cols
    width_all = shell_cols * lax.axis_size("gy")
    row_of = contact_node // width_all
    col_of = contact_node % width_all
    owned = (row_of // shell_rows == lax.axis_index("gx")) & (
        col_of // shell_cols == lax.axis_index("gy")
    )
    local_ids = (row_of % shell_rows * shell_cols + col_of % shell_cols).reshape(-1)
    front_flag = (lax.axis_index("gx") == lax.axis_size("gx") - 1).astype(jnp.float32)
    jitter_padded = extended(jitter, (("gx", 1), ("gy", 2)), 1)
    for iteration in range(STEPS):
        forces = ice_forces(ice_displacement, jitter_padded, bond_mask)
        front_gap = ice_displacement[0, -1] + intersection
        gaps = spread(front_gap, "gx", lax.axis_size("gx") - 1)
        reached = shell_deflection.reshape(-1)[local_ids].reshape(gaps.shape)
        pushes = jnp.where(owned, PENALTY * jnp.maximum(gaps - reached, 0.0), 0.0)
        loading = jax.ops.segment_sum(pushes.reshape(-1), local_ids, num_segments=node_count)
        loading = loading.reshape(shell_rows, shell_cols)
        my_pushes = lax.psum(pushes, "gx") * front_flag
        forces = forces.at[0, -1].add(-my_pushes)
        shell_padded = extended(shell_deflection, (("gx", 0), ("gy", 1)), 2)
        bending = laplace(laplace(shell_padded))
        ice_velocity = ice_velocity + STEP_DT * forces
        ice_displacement = ice_displacement + STEP_DT * ice_velocity
        shell_velocity = shell_velocity + STEP_DT * (loading - BEND * bending)
        shell_deflection = shell_deflection + STEP_DT * shell_velocity
    return (ice_displacement, ice_velocity, shell_deflection, shell_velocity)


def solution(mesh):
    in_specs = (
        P(None, "gx", "gy", None),
        P(None, "gx", "gy", None),
        P(None, "gx", "gy", None),
        P("gx", "gy", None),
        P("gy", None),
        P("gy", None),
        P("gx", "gy"),
        P("gx", "gy"),
    )
    out_specs = (P(None, "gx", "gy", None), P(None, "gx", "gy", None), P("gx", "gy"), P("gx", "gy"))
    return jax.shard_map(
        on_device, mesh=mesh, in_specs=in_specs, out_specs=out_specs, check_vma=False
    )
```

profile of v0, /device:TPU:1, one launch (start us, length us, event | category | flops | bytes accessed | tf_op | source)
XLA Modules:
  0.0 344.3 jit_solution(6628506796407880037)
XLA Ops:
  1.4 3.9 %collective-permute-start.3 = (f32[2,1,8,128]{3,2,1,0:T(8,128)S(1)}, f32[2,1,8,128]{3,2,1,0:T(8,128)S(1)}, u32[]{:S(2)}, u32[]{:S(2)}) collective-permute-start(f32[2,1,8,128]{3,2,1,0:T(8,128)S(1)} %get-tuple-element.171), channel_id=1, source_target_pairs={{0,8},{8,16},{16,24},{1,9},{9,17},{17,25},{2,10},{10,18},{18,26},{... | collective-permute-start | bytes 24584 | tf_op jit(solution)/shard_map/ppermute | solution.py:28
  7.3 4.0 %collective-permute-start = (f32[2,1,8,128]{3,2,1,0:T(8,128)S(1)}, f32[2,1,8,128]{3,2,1,0:T(8,128)S(1)}, u32[]{:S(2)}, u32[]{:S(2)}) collective-permute-start(f32[2,1,8,128]{3,2,1,0:T(8,128)S(1)} %get-tuple-element.169), channel_id=1, source_target_pairs={{0,8},{8,16},{16,24},{1,9},{9,17},{17,25},{2,10},{10,18},{18,26},{... | collective-permute-start | bytes 24584 | tf_op jit(solution)/shard_map/ppermute | solution.py:28
  13.4 4.7 %collective-permute-start.12 = (f32[2,512]{1,0:T(2,128)S(1)}, f32[2,512]{1,0:T(2,128)S(1)}, u32[]{:S(2)}, u32[]{:S(2)}) collective-permute-start(f32[2,512]{1,0:T(2,128)S(1)} %get-tuple-element.94), channel_id=1, source_target_pairs={{0,8},{8,16},{16,24},{1,9},{9,17},{17,25},{2,10},{10,18},{18,26},{... | collective-permute-start | bytes 12296 | tf_op jit(solution)/shard_map/ppermute | solution.py:28
  20.5 8.1 %psum.28 = f32[8,128]{1,0:T(8,128)S(1)} all-reduce(f32[8,128]{1,0:T(8,128)S(1)} %fusion.96), channel_id=1, replica_groups=mesh['gx'=4,'gy'=8] {'gx'}, use_global_device_ids=true, to_apply=%region_19.20 | all-reduce | flops 1024 | bytes 8192 | tf_op jit(solution)/shard_map/psum | solution.py:39
  28.8 6.2 %gather_fusion = f32[1024]{0:T(1024)S(1)} fusion(f32[65536]{0:T(1024)S(1)} %bitcast.195, s32[1024]{0:T(1024)S(1)} %broadcast_clamp_fusion), kind=kCustom, calls=%fused_computation | custom fusion | bytes 12288 | tf_op jit(solution)/shard_map/gather | solution.py:129
  36.4 10.9 %multiply_reduce_fusion.27 = (f32[8,8,128]{2,1,0:T(8,128)S(1)}, f32[8,8,128]{2,1,0:T(8,128)S(1)}) fusion(f32[8,8,128]{2,1,0:T(8,128)S(1)} %get-tuple-element.167, f32[8,8,128]{2,1,0:T(8,128)S(1)} %get-tuple-element.165, f32[128,128]{1,0:T(8,128)S(1)} %get-tuple-element.200, f32[8,8,128]{2,1,0:T(8,128)S(1)} %get-tuple-element.166, ...), kind=kLoop, calls=%fused_computation.95 | loop fusion | flops 33538048 | bytes 393472 | tf_op jit(solution)/shard_map/reduce_sum | solution.py:65
  48.0 5.7 %psum.29 = f32[8,128]{1,0:T(8,128)S(1)} all-reduce(f32[8,128]{1,0:T(8,128)S(1)} %get-tuple-element.86), channel_id=1, replica_groups=mesh['gx'=4,'gy'=8] {'gx'}, use_global_device_ids=true, to_apply=%region_20.21 | all-reduce | flops 1024 | bytes 8192 | tf_op jit(solution)/shard_map/psum | solution.py:133
  53.8 7.7 %collective-permute-start.15 = (f32[132,2]{1,0:T(8,128)S(1)}, f32[132,2]{1,0:T(8,128)S(1)}, u32[]{:S(2)}, u32[]{:S(2)}) collective-permute-start(f32[132,2]{1,0:T(8,128)S(1)} %get-tuple-element.91), channel_id=1, source_target_pairs={{1,0},{2,1},{3,2},{4,3},{5,4},{6,5},{7,6},{9,8},{10,9},{11,10},{12... | collective-permute-start | bytes 3176 | tf_op jit(solution)/shard_map/ppermute | solution.py:30
  61.6 3.1 collective-permute-start.14
  65.6 6.0 %scatter_custom_fusion = f32[65536]{0:T(1024)S(1)} fusion(s32[1024]{0:T(1024)S(1)} %fusion.119, f32[1024]{0:T(1024)S(1)} %bitcast.238, f32[]{:T(128)} %constant.364.clone.1), kind=kCustom, calls=%fused_computation.227 | custom fusion | flops 1024 | bytes 262148 | tf_op jit(solution)/shard_map/scatter-add | solution.py:131
  74.5 6.2 %gather_fusion.1 = f32[1024]{0:T(1024)S(1)} fusion(f32[65536]{0:T(1024)S(1)} %bitcast.196, s32[1024]{0:T(1024)S(1)} %broadcast_clamp_fusion), kind=kCustom, calls=%fused_computation.1 | custom fusion | bytes 12288 | tf_op jit(solution)/shard_map/gather | solution.py:129
  82.2 4.9 %collective-permute-start.16 = (f32[2,512]{1,0:T(2,128)S(1)}, f32[2,512]{1,0:T(2,128)S(1)}, u32[]{:S(2)}, u32[]{:S(2)}) collective-permute-start(f32[2,512]{1,0:T(2,128)S(1)} %get-tuple-element.92), channel_id=1, source_target_pairs={{0,8},{8,16},{16,24},{1,9},{9,17},{17,25},{2,10},{10,18},{18,26},{... | collective-permute-start | bytes 12296 | tf_op jit(solution)/shard_map/ppermute | solution.py:28
  91.1 3.6 %collective-permute-start.5 = (f32[2,10,1,128]{3,2,1,0:T(1,128)S(1)}, f32[2,10,1,128]{3,2,1,0:T(1,128)S(1)}, u32[]{:S(2)}, u32[]{:S(2)}) collective-permute-start(f32[2,10,1,128]{3,2,1,0:T(1,128)S(1)} %get-tuple-element.138), channel_id=1, source_target_pairs={{0,1},{1,2},{2,3},{3,4},{4,5},{5,6},{6,7},{8,9},{9,10},{10,11},{11... | collective-permute-start | bytes 30728 | tf_op jit(solution)/shard_map/ppermute | solution.py:28
  96.9 3.9 %collective-permute-start.18 = (f32[132,2]{1,0:T(8,128)S(1)}, f32[132,2]{1,0:T(8,128)S(1)}, u32[]{:S(2)}, u32[]{:S(2)}) collective-permute-start(f32[132,2]{1,0:T(8,128)S(1)} %get-tuple-element.88), channel_id=1, source_target_pairs={{0,1},{1,2},{2,3},{3,4},{4,5},{5,6},{6,7},{8,9},{9,10},{10,11},{11... | collective-permute-start | bytes 3176 | tf_op jit(solution)/shard_map/ppermute | solution.py:28
  100.7 21.8 %multiply_reduce_fusion.21 = (f32[8,8,128]{2,1,0:T(8,128)S(1)}, f32[8,8,128]{2,1,0:T(8,128)S(1)}, f32[8,8,128]{2,1,0:T(8,128)S(1)}, f32[8,8,128]{2,1,0:T(8,128)S(1)}) fusion(f32[8,8,128]{2,1,0:T(8,128)S(1)} %get-tuple-element.151, f32[8,8,128]{2,1,0:T(8,128)S(1)} %get-tuple-element.149, f32[128,128]{1,0:T(8,128)S(1)} %get-tuple-element.202, ...), kind=kLoop, calls=%fused_computation.68 | loop fusion | flops 67076096 | bytes 786944 | tf_op jit(solution)/shard_map/reduce_sum | solution.py:65
  122.6 2.2 collective-permute-start.2
  125.7 21.8 %multiply_reduce_fusion.23 = (f32[8,8,128]{2,1,0:T(8,128)S(1)}, f32[8,8,128]{2,1,0:T(8,128)S(1)}, f32[8,8,128]{2,1,0:T(8,128)S(1)}, f32[8,8,128]{2,1,0:T(8,128)S(1)}) fusion(f32[8,8,128]{2,1,0:T(8,128)S(1)} %get-tuple-element.131, f32[8,8,128]{2,1,0:T(8,128)S(1)} %get-tuple-element.125, f32[128,128]{1,0:T(8,128)S(1)} %get-tuple-element.202, ...), kind=kLoop, calls=%fused_computation.77 | loop fusion | flops 67076096 | bytes 786944 | tf_op jit(solution)/shard_map/reduce_sum | solution.py:65
  147.6 21.8 %multiply_reduce_fusion.31 = (f32[8,8,128]{2,1,0:T(8,128)S(1)}, f32[8,8,128]{2,1,0:T(8,128)S(1)}, f32[8,8,128]{2,1,0:T(8,128)S(1)}, f32[8,8,128]{2,1,0:T(8,128)S(1)}) fusion(f32[8,8,128]{2,1,0:T(8,128)S(1)} %get-tuple-element.115, f32[8,8,128]{2,1,0:T(8,128)S(1)} %get-tuple-element.109, f32[8,8,128]{2,1,0:T(8,128)S(1)} %get-tuple-element.167, ...), kind=kLoop, calls=%fused_computation.113 | loop fusion | flops 67076096 | bytes 786944 | tf_op jit(solution)/shard_map/reduce_sum | solution.py:65
  169.4 32.4 %multiply_reduce_fusion.19 = (f32[8,8,128]{2,1,0:T(8,128)S(1)}, f32[8,8,128]{2,1,0:T(8,128)S(1)}, f32[8,8,128]{2,1,0:T(8,128)S(1)}, f32[8,8,128]{2,1,0:T(8,128)S(1)}) fusion(f32[8,8,128]{2,1,0:T(8,128)S(1)} %get-tuple-element.119, f32[8,8,128]{2,1,0:T(8,128)S(1)} %get-tuple-element.113, f32[128,128]{1,0:T(8,128)S(1)} %get-tuple-element.202, ...), kind=kLoop, calls=%fused_computation.59 | loop fusion | flops 67076096 | bytes 786944 | tf_op jit(solution)/shard_map/reduce_sum | solution.py:65
  201.9 2.0 fusion.86
  205.3 4.9 %collective-permute-start.8 = (f32[2,1,8,128]{3,2,1,0:T(8,128)S(1)}, f32[2,1,8,128]{3,2,1,0:T(8,128)S(1)}, u32[]{:S(2)}, u32[]{:S(2)}) collective-permute-start(f32[2,1,8,128]{3,2,1,0:T(8,128)S(1)} %get-tuple-element.156), channel_id=1, source_target_pairs={{0,8},{8,16},{16,24},{1,9},{9,17},{17,25},{2,10},{10,18},{18,26},{... | collective-permute-start | bytes 24584 | tf_op jit(solution)/shard_map/ppermute | solution.py:28
  210.2 8.1 %psum.30 = f32[8,128]{1,0:T(8,128)S(1)} all-reduce(f32[8,128]{1,0:T(8,128)S(1)} %fusion.89), channel_id=1, replica_groups=mesh['gx'=4,'gy'=8] {'gx'}, use_global_device_ids=true, to_apply=%region_39.40 | all-reduce | flops 1024 | bytes 8192 | tf_op jit(solution)/shard_map/psum | solution.py:39
  218.3 6.0 %scatter_custom_fusion.1 = f32[65536]{0:T(1024)S(1)} fusion(s32[1024]{0:T(1024)S(1)} %fusion.119, f32[1024]{0:T(1024)S(1)} %bitcast.236, f32[]{:T(128)} %constant.364.clone.1), kind=kCustom, calls=%fused_computation.225 | custom fusion | flops 1024 | bytes 262148 | tf_op jit(solution)/shard_map/scatter-add | solution.py:131
  225.5 6.4 %psum.31 = f32[8,128]{1,0:T(8,128)S(1)} all-reduce(f32[8,128]{1,0:T(8,128)S(1)} %fusion.92), channel_id=1, replica_groups=mesh['gx'=4,'gy'=8] {'gx'}, use_global_device_ids=true, to_apply=%region_41.42 | all-reduce | flops 1024 | bytes 8192 | tf_op jit(solution)/shard_map/psum | solution.py:133
  231.9 6.8 %collective-permute-start.11 = (f32[2,10,1,128]{3,2,1,0:T(1,128)S(1)}, f32[2,10,1,128]{3,2,1,0:T(1,128)S(1)}, u32[]{:S(2)}, u32[]{:S(2)}) collective-permute-start(f32[2,10,1,128]{3,2,1,0:T(1,128)S(1)} %get-tuple-element.134), channel_id=1, source_target_pairs={{1,0},{2,1},{3,2},{4,3},{5,4},{6,5},{7,6},{9,8},{10,9},{11,10},{12... | collective-permute-start | bytes 30728 | tf_op jit(solution)/shard_map/ppermute | solution.py:30
  238.8 3.5 %collective-permute-start.10 = (f32[2,10,1,128]{3,2,1,0:T(1,128)S(1)}, f32[2,10,1,128]{3,2,1,0:T(1,128)S(1)}, u32[]{:S(2)}, u32[]{:S(2)}) collective-permute-start(f32[2,10,1,128]{3,2,1,0:T(1,128)S(1)} %get-tuple-element.135), channel_id=1, source_target_pairs={{0,1},{1,2},{2,3},{3,4},{4,5},{5,6},{6,7},{8,9},{9,10},{10,11},{11... | collective-permute-start | bytes 30728 | tf_op jit(solution)/shard_map/ppermute | solution.py:28
  242.3 21.7 %multiply_reduce_fusion.9 = (f32[8,8,128]{2,1,0:T(8,128)S(1)}, f32[8,8,128]{2,1,0:T(8,128)S(1)}, f32[8,8,128]{2,1,0:T(8,128)S(1)}, f32[8,8,128]{2,1,0:T(8,128)S(1)}) fusion(f32[8,8,128]{2,1,0:T(8,128)S(1)} %get-tuple-element.155, f32[8,8,128]{2,1,0:T(8,128)S(1)} %get-tuple-element.165, f32[128,128]{1,0:T(8,128)S(1)} %get-tuple-element.200, ...), kind=kLoop, calls=%fused_computation.34 | loop fusion | flops 67076096 | bytes 655872 | tf_op jit(solution)/shard_map/reduce_sum | solution.py:65
  264.1 11.1 %multiply_reduce_fusion.17 = (f32[8,8,128]{2,1,0:T(8,128)S(1)}, f32[8,8,128]{2,1,0:T(8,128)S(1)}) fusion(f32[8,8,128]{2,1,0:T(8,128)S(1)} %get-tuple-element.155, f32[8,8,128]{2,1,0:T(8,128)S(1)} %get-tuple-element.107, f32[8,8,128]{2,1,0:T(8,128)S(1)} %get-tuple-element.165, f32[8,8,128]{2,1,0:T(8,128)S(1)} %get-tuple-element.121, ...), kind=kLoop, calls=%fused_computation.54 | loop fusion | flops 33538048 | bytes 524544 | tf_op jit(solution)/shard_map/reduce_sum | solution.py:65
  275.2 22.0 %multiply_reduce_fusion.7 = (f32[8,8,128]{2,1,0:T(8,128)S(1)}, f32[8,8,128]{2,1,0:T(8,128)S(1)}, f32[8,8,128]{2,1,0:T(8,128)S(1)}, f32[8,8,128]{2,1,0:T(8,128)S(1)}) fusion(f32[8,8,128]{2,1,0:T(8,128)S(1)} %get-tuple-element.99, f32[8,8,128]{2,1,0:T(8,128)S(1)} %get-tuple-element.155, f32[8,8,128]{2,1,0:T(8,128)S(1)} %get-tuple-element.108, ...), kind=kLoop, calls=%fused_computation.29 | loop fusion | flops 67076096 | bytes 786944 | tf_op jit(solution)/shard_map/reduce_sum | solution.py:65
  297.2 21.8 %multiply_reduce_fusion.5 = (f32[8,8,128]{2,1,0:T(8,128)S(1)}, f32[8,8,128]{2,1,0:T(8,128)S(1)}, f32[8,8,128]{2,1,0:T(8,128)S(1)}, f32[8,8,128]{2,1,0:T(8,128)S(1)}) fusion(f32[8,8,128]{2,1,0:T(8,128)S(1)} %get-tuple-element.104, f32[8,8,128]{2,1,0:T(8,128)S(1)} %get-tuple-element.155, f32[8,8,128]{2,1,0:T(8,128)S(1)} %get-tuple-element.125, ...), kind=kLoop, calls=%fused_computation.24 | loop fusion | flops 67076096 | bytes 786944 | tf_op jit(solution)/shard_map/reduce_sum | solution.py:65
  319.0 22.0 %multiply_reduce_fusion.1 = (f32[8,8,128]{2,1,0:T(8,128)S(1)}, f32[8,8,128]{2,1,0:T(8,128)S(1)}, f32[8,8,128]{2,1,0:T(8,128)S(1)}, f32[8,8,128]{2,1,0:T(8,128)S(1)}) fusion(f32[8,8,128]{2,1,0:T(8,128)S(1)} %get-tuple-element.97, f32[8,8,128]{2,1,0:T(8,128)S(1)} %get-tuple-element.155, f32[8,8,128]{2,1,0:T(8,128)S(1)} %get-tuple-element.113, ...), kind=kLoop, calls=%fused_computation.14 | loop fusion | flops 67076096 | bytes 786944 | tf_op jit(solution)/shard_map/reduce_sum | solution.py:65
  341.2 2.0 fusion.87
  (121 shorter events, 25.2 us)
Async XLA Ops:
  0.6 19.0 %copy-start.6 = (s32[8,128]{1,0:T(8,128)S(1)}, s32[8,128]{1,0:T(8,128)}, u32[]{:S(2)}) copy-start(s32[8,128]{1,0:T(8,128)} %param.16) | copy-start | bytes 12292
  0.6 19.1 %copy-start.1 = (s32[8,8,9]{2,1,0:T(8,128)S(1)}, s32[8,8,9]{2,1,0:T(8,128)}, u32[]{:S(2)}) copy-start(s32[8,8,9]{2,1,0:T(8,128)} %param.15) | copy-start | bytes 6916
  1.4 80.8 %collective-permute-start.3 = (f32[2,1,8,128]{3,2,1,0:T(8,128)S(1)}, f32[2,1,8,128]{3,2,1,0:T(8,128)S(1)}, u32[]{:S(2)}, u32[]{:S(2)}) collective-permute-start(f32[2,1,8,128]{3,2,1,0:T(8,128)S(1)} %get-tuple-element.171), channel_id=1, source_target_pairs={{0,8},{8,16},{16,24},{1,9},{9,17},{17,25},{2,10},{10,18},{18,26},{... | collective-permute-start | bytes 24584 | tf_op jit(solution)/shard_map/ppermute | solution.py:28
  5.3 81.8 %collective-permute-start.4 = (f32[2,1,8,128]{3,2,1,0:T(8,128)S(1)}, f32[2,1,8,128]{3,2,1,0:T(8,128)S(1)}, u32[]{:S(2)}, u32[]{:S(2)}) collective-permute-start(f32[2,1,8,128]{3,2,1,0:T(8,128)S(1)} %get-tuple-element.170), channel_id=1, source_target_pairs={{8,0},{16,8},{24,16},{9,1},{17,9},{25,17},{10,2},{18,10},{26,18},{... | collective-permute-start | bytes 24584 | tf_op jit(solution)/shard_map/ppermute | solution.py:30
  7.3 81.7 %collective-permute-start = (f32[2,1,8,128]{3,2,1,0:T(8,128)S(1)}, f32[2,1,8,128]{3,2,1,0:T(8,128)S(1)}, u32[]{:S(2)}, u32[]{:S(2)}) collective-permute-start(f32[2,1,8,128]{3,2,1,0:T(8,128)S(1)} %get-tuple-element.169), channel_id=1, source_target_pairs={{0,8},{8,16},{16,24},{1,9},{9,17},{17,25},{2,10},{10,18},{18,26},{... | collective-permute-start | bytes 24584 | tf_op jit(solution)/shard_map/ppermute | solution.py:28
  12.1 41.6 %collective-permute-start.13 = (f32[2,512]{1,0:T(2,128)S(1)}, f32[2,512]{1,0:T(2,128)S(1)}, u32[]{:S(2)}, u32[]{:S(2)}) collective-permute-start(f32[2,512]{1,0:T(2,128)S(1)} %get-tuple-element.95), channel_id=1, source_target_pairs={{8,0},{16,8},{24,16},{9,1},{17,9},{25,17},{10,2},{18,10},{26,18},{... | collective-permute-start | bytes 12296 | tf_op jit(solution)/shard_map/ppermute | solution.py:30
  13.4 40.3 %collective-permute-start.12 = (f32[2,512]{1,0:T(2,128)S(1)}, f32[2,512]{1,0:T(2,128)S(1)}, u32[]{:S(2)}, u32[]{:S(2)}) collective-permute-start(f32[2,512]{1,0:T(2,128)S(1)} %get-tuple-element.94), channel_id=1, source_target_pairs={{0,8},{8,16},{16,24},{1,9},{9,17},{17,25},{2,10},{10,18},{18,26},{... | collective-permute-start | bytes 12296 | tf_op jit(solution)/shard_map/ppermute | solution.py:28
  19.7 0.8 copy-start.2
  19.7 0.8 copy-start.7
  19.7 8.9 %copy-start = (f32[128,512]{1,0:T(8,128)S(1)}, f32[128,512]{1,0:T(8,128)}, u32[]{:S(2)}) copy-start(f32[128,512]{1,0:T(8,128)} %param.18) | copy-start | bytes 786436
  35.0 0.7 copy-start.8
  53.8 17.9 %collective-permute-start.15 = (f32[132,2]{1,0:T(8,128)S(1)}, f32[132,2]{1,0:T(8,128)S(1)}, u32[]{:S(2)}, u32[]{:S(2)}) collective-permute-start(f32[132,2]{1,0:T(8,128)S(1)} %get-tuple-element.91), channel_id=1, source_target_pairs={{1,0},{2,1},{3,2},{4,3},{5,4},{6,5},{7,6},{9,8},{10,9},{11,10},{12... | collective-permute-start | bytes 3176 | tf_op jit(solution)/shard_map/ppermute | solution.py:30
  61.6 11.3 %collective-permute-start.14 = (f32[132,2]{1,0:T(8,128)S(1)}, f32[132,2]{1,0:T(8,128)S(1)}, u32[]{:S(2)}, u32[]{:S(2)}) collective-permute-start(f32[132,2]{1,0:T(8,128)S(1)} %get-tuple-element.90), channel_id=1, source_target_pairs={{0,1},{1,2},{2,3},{3,4},{4,5},{5,6},{6,7},{8,9},{9,10},{10,11},{11... | collective-permute-start | bytes 3176 | tf_op jit(solution)/shard_map/ppermute | solution.py:28
  71.6 17.5 %collective-permute-start.1 = (f32[2,1,8,128]{3,2,1,0:T(8,128)S(1)}, f32[2,1,8,128]{3,2,1,0:T(8,128)S(1)}, u32[]{:S(2)}, u32[]{:S(2)}) collective-permute-start(f32[2,1,8,128]{3,2,1,0:T(8,128)S(1)} %get-tuple-element.168), channel_id=1, source_target_pairs={{8,0},{16,8},{24,16},{9,1},{17,9},{25,17},{10,2},{18,10},{26,18},{... | collective-permute-start | bytes 24584 | tf_op jit(solution)/shard_map/ppermute | solution.py:30
  73.2 1.0 copy-start.4
  80.7 8.4 %copy-start.3 = (f32[2,8,8,128]{3,2,1,0:T(8,128)S(1)}, f32[2,8,8,128]{3,2,1,0:T(8,128)}, u32[]{:S(2)}) copy-start(f32[2,8,8,128]{3,2,1,0:T(8,128)} %param.14) | copy-start | bytes 196612
  80.7 14.1 %collective-permute-start.17 = (f32[2,512]{1,0:T(2,128)S(1)}, f32[2,512]{1,0:T(2,128)S(1)}, u32[]{:S(2)}, u32[]{:S(2)}) collective-permute-start(f32[2,512]{1,0:T(2,128)S(1)} %get-tuple-element.93), channel_id=1, source_target_pairs={{8,0},{16,8},{24,16},{9,1},{17,9},{25,17},{10,2},{18,10},{26,18},{... | collective-permute-start | bytes 12296 | tf_op jit(solution)/shard_map/ppermute | solution.py:30
  82.2 12.7 %collective-permute-start.16 = (f32[2,512]{1,0:T(2,128)S(1)}, f32[2,512]{1,0:T(2,128)S(1)}, u32[]{:S(2)}, u32[]{:S(2)}) collective-permute-start(f32[2,512]{1,0:T(2,128)S(1)} %get-tuple-element.92), channel_id=1, source_target_pairs={{0,8},{8,16},{16,24},{1,9},{9,17},{17,25},{2,10},{10,18},{18,26},{... | collective-permute-start | bytes 12296 | tf_op jit(solution)/shard_map/ppermute | solution.py:28
  87.2 60.4 %collective-permute-start.7 = (f32[2,10,1,128]{3,2,1,0:T(1,128)S(1)}, f32[2,10,1,128]{3,2,1,0:T(1,128)S(1)}, u32[]{:S(2)}, u32[]{:S(2)}) collective-permute-start(f32[2,10,1,128]{3,2,1,0:T(1,128)S(1)} %get-tuple-element.139), channel_id=1, source_target_pairs={{1,0},{2,1},{3,2},{4,3},{5,4},{6,5},{7,6},{9,8},{10,9},{11,10},{12... | collective-permute-start | bytes 30728 | tf_op jit(solution)/shard_map/ppermute | solution.py:30
  89.2 58.4 %collective-permute-start.6 = (f32[2,10,1,128]{3,2,1,0:T(1,128)S(1)}, f32[2,10,1,128]{3,2,1,0:T(1,128)S(1)}, u32[]{:S(2)}, u32[]{:S(2)}) collective-permute-start(f32[2,10,1,128]{3,2,1,0:T(1,128)S(1)} %get-tuple-element.137), channel_id=1, source_target_pairs={{1,0},{2,1},{3,2},{4,3},{5,4},{6,5},{7,6},{9,8},{10,9},{11,10},{12... | collective-permute-start | bytes 30728 | tf_op jit(solution)/shard_map/ppermute | solution.py:30
  91.1 34.4 %collective-permute-start.5 = (f32[2,10,1,128]{3,2,1,0:T(1,128)S(1)}, f32[2,10,1,128]{3,2,1,0:T(1,128)S(1)}, u32[]{:S(2)}, u32[]{:S(2)}) collective-permute-start(f32[2,10,1,128]{3,2,1,0:T(1,128)S(1)} %get-tuple-element.138), channel_id=1, source_target_pairs={{0,1},{1,2},{2,3},{3,4},{4,5},{5,6},{6,7},{8,9},{9,10},{10,11},{11... | collective-permute-start | bytes 30728 | tf_op jit(solution)/shard_map/ppermute | solution.py:28
  94.9 27.6 %collective-permute-start.19 = (f32[132,2]{1,0:T(8,128)S(1)}, f32[132,2]{1,0:T(8,128)S(1)}, u32[]{:S(2)}, u32[]{:S(2)}) collective-permute-start(f32[132,2]{1,0:T(8,128)S(1)} %get-tuple-element.89), channel_id=1, source_target_pairs={{1,0},{2,1},{3,2},{4,3},{5,4},{6,5},{7,6},{9,8},{10,9},{11,10},{12... | collective-permute-start | bytes 3176 | tf_op jit(solution)/shard_map/ppermute | solution.py:30
  96.9 28.0 %collective-permute-start.18 = (f32[132,2]{1,0:T(8,128)S(1)}, f32[132,2]{1,0:T(8,128)S(1)}, u32[]{:S(2)}, u32[]{:S(2)}) collective-permute-start(f32[132,2]{1,0:T(8,128)S(1)} %get-tuple-element.88), channel_id=1, source_target_pairs={{0,1},{1,2},{2,3},{3,4},{4,5},{5,6},{6,7},{8,9},{9,10},{10,11},{11... | collective-permute-start | bytes 3176 | tf_op jit(solution)/shard_map/ppermute | solution.py:28
  122.6 3.1 collective-permute-start.2
  201.8 2.2 copy-start.5
  204.0 27.9 %collective-permute-start.9 = (f32[2,1,8,128]{3,2,1,0:T(8,128)S(1)}, f32[2,1,8,128]{3,2,1,0:T(8,128)S(1)}, u32[]{:S(2)}, u32[]{:S(2)}) collective-permute-start(f32[2,1,8,128]{3,2,1,0:T(8,128)S(1)} %get-tuple-element.157), channel_id=1, source_target_pairs={{8,0},{16,8},{24,16},{9,1},{17,9},{25,17},{10,2},{18,10},{26,18},{... | collective-permute-start | bytes 24584 | tf_op jit(solution)/shard_map/ppermute | solution.py:30
  205.3 26.6 %collective-permute-start.8 = (f32[2,1,8,128]{3,2,1,0:T(8,128)S(1)}, f32[2,1,8,128]{3,2,1,0:T(8,128)S(1)}, u32[]{:S(2)}, u32[]{:S(2)}) collective-permute-start(f32[2,1,8,128]{3,2,1,0:T(8,128)S(1)} %get-tuple-element.156), channel_id=1, source_target_pairs={{0,8},{8,16},{16,24},{1,9},{9,17},{17,25},{2,10},{10,18},{18,26},{... | collective-permute-start | bytes 24584 | tf_op jit(solution)/shard_map/ppermute | solution.py:28
  231.9 32.1 %collective-permute-start.11 = (f32[2,10,1,128]{3,2,1,0:T(1,128)S(1)}, f32[2,10,1,128]{3,2,1,0:T(1,128)S(1)}, u32[]{:S(2)}, u32[]{:S(2)}) collective-permute-start(f32[2,10,1,128]{3,2,1,0:T(1,128)S(1)} %get-tuple-element.134), channel_id=1, source_target_pairs={{1,0},{2,1},{3,2},{4,3},{5,4},{6,5},{7,6},{9,8},{10,9},{11,10},{12... | collective-permute-start | bytes 30728 | tf_op jit(solution)/shard_map/ppermute | solution.py:30
  238.8 25.3 %collective-permute-start.10 = (f32[2,10,1,128]{3,2,1,0:T(1,128)S(1)}, f32[2,10,1,128]{3,2,1,0:T(1,128)S(1)}, u32[]{:S(2)}, u32[]{:S(2)}) collective-permute-start(f32[2,10,1,128]{3,2,1,0:T(1,128)S(1)} %get-tuple-element.135), channel_id=1, source_target_pairs={{0,1},{1,2},{2,3},{3,4},{4,5},{5,6},{6,7},{8,9},{9,10},{10,11},{11... | collective-permute-start | bytes 30728 | tf_op jit(solution)/shard_map/ppermute | solution.py:28
where the time goes:
time: 350 us; the launch traced here: 344 us
  other arithmetic  229 us (65%)
  starting transfers between devices  65.6 us (19%)
  blocking collectives  28.3 us (8%)
  local copies, waits for them, and re-layouts  19.6 us (6%)
    reduce_sum x10, other arithmetic, pair_force(): jnp.sum(factor * now_x, axis=-1)  207 us
    ppermute x10, starting transfers between devices, extended(): lax.ppermute(tail, axis, [(i, (i + 1) % count) for i in range(ends)])  38.6 us
    ppermute x10, starting transfers between devices, extended(): lax.ppermute(head, axis, [((i + 1) % count, i) for i in range(ends)])  26.9 us
    psum x2, blocking collectives, spread(): return lax.psum(jnp.where(mine, array, jnp.zeros_like(array)), axis)  16.2 us
    gather x2, local copies, waits for them, and re-layouts, on_device(): reached = shell_deflection.reshape(-1)[local_ids].reshape(gaps.shape)  12.3 us
    psum x2, blocking collectives, on_device(): my_pushes = lax.psum(pushes, 'gx') * front_flag  12.1 us
    scatter-add x2, other arithmetic, on_device(): jax.ops.segment_sum(pushes.reshape(-1), local_ids, num_segments=node_count)  12 us
  transfers between devices with their start and end apart: 20, of which 1 were waited for; matrix products, arithmetic and copies ran while one was open for 32% of the time, Pallas kernels for 0%

commit v1 on v0

v1 whole, which is shorter than its diff:
```python
import functools

import jax
import jax.numpy as jnp
from jax import lax
from jax.experimental import pallas as pl
from jax.experimental.pallas import tpu as pltpu
from jax.sharding import PartitionSpec as P

TILE_X = 8
TILE_Y = 16
PTS = 128
SPLIT = 4

HORIZON = 3.5
DELTA_SQ = 0.25
PENALTY = 4.0
BEND = 0.5
STEP_DT = 0.2

F32 = jnp.float32
I32 = jnp.int32

STRIDE = 24
WIDE = 640
PAD = 16


def bond_offsets():
    limit = HORIZON * HORIZON - DELTA_SQ
    found = []
    for oy in range(-4, 5):
        for ox in range(-4, 5):
            near = max(abs(ox) - 0.4, 0.0) ** 2 + max(abs(oy) - 0.4, 0.0) ** 2
            if near < limit and (ox or oy):
                found.append((ox, oy))
    return found


OFFSETS = bond_offsets()
SIDEWAYS = sorted({oy for _, oy in OFFSETS})


def sign(value):
    return (value > 0) - (value < 0)


def lanes():
    return lax.broadcasted_iota(I32, (8, PTS), 1)


def subs():
    return lax.broadcasted_iota(I32, (8, PTS), 0)


def turn(values, shift):
    size = values.shape[1]
    return pltpu.roll(values, shift % size, 1) if shift % size else values


def slot(dx, dy):
    return 3 * (dx + 1) + dy + 1


def lane_masks():
    lane = lanes()
    row, col = lane // TILE_Y, lane % TILE_Y
    masks = {}
    for o in (1, 2, 3):
        masks["col_at", o] = col < o
        masks["col_at", -o] = col >= TILE_Y - o
        masks["col_from", o] = col >= TILE_Y - o
        masks["col_from", -o] = col < o
        masks["row_at", o] = row < o
        masks["row_at", -o] = row >= TILE_X - o
        masks["row_from", o] = row >= TILE_X - o
        masks["row_from", -o] = row < o
    bits = {}
    for ox in range(-3, 4):
        bits[ox] = jnp.left_shift(jnp.int32(1), 4 * row + ((row + ox) & 7) // 2)
    return masks, bits


def moved(get, oy, masks):
    out = {}
    for dx in (-1, 0, 1):
        held = get(dx, 0)
        if oy:
            held = turn(jnp.where(masks["col_at", oy], get(dx, sign(oy)), held), -oy)
        out[dx] = held
    return out


def across(cells, ox, masks):
    if not ox:
        return cells[0]
    return turn(jnp.where(masks["row_at", ox], cells[sign(ox)], cells[0]), -TILE_Y * ox)


def first_forces(get_jx, get_jy, get_dx, get_dy, get_words, keep=None, both=True):
    masks, bits = lane_masks()
    jx0, jy0, dx0, dy0 = get_jx(0, 0), get_jy(0, 0), get_dx(0, 0), get_dy(0, 0)
    fx = jnp.zeros((8, PTS), F32)
    fy = jnp.zeros((8, PTS), F32)
    for oy in SIDEWAYS:
        jxs, jys = moved(get_jx, oy, masks), moved(get_jy, oy, masks)
        dxs, dys = moved(get_dx, oy, masks), moved(get_dy, oy, masks)
        words = {}
        for dx in (-1, 0, 1):
            words[dx] = get_words(dx, 0)
            if oy:
                words[dx] = jnp.where(masks["col_from", oy], get_words(dx, sign(oy)), words[dx])
        for number, (ox, other) in enumerate(OFFSETS):
            if other != oy:
                continue
            word = words[0]
            if ox:
                word = jnp.where(masks["row_from", ox], words[sign(ox)], word)
            intact = (word & bits[ox]) != 0
            rest_x = across(jxs, ox, masks) - (jx0 - float(ox))
            rest_y = across(jys, ox, masks) - (jy0 - float(oy))
            now_x = across(dxs, ox, masks) - (dx0 - float(ox))
            now_y = across(dys, ox, masks) - (dy0 - float(oy))
            rest_sq = rest_x * rest_x + rest_y * rest_y + DELTA_SQ
            now_sq = now_x * now_x + now_y * now_y + DELTA_SQ
            rest_inv = lax.rsqrt(rest_sq)
            reach = jnp.maximum(1.0 - rest_sq * rest_inv * (1.0 / HORIZON), 0.0)
            weight = jnp.where(intact, reach * reach, 0.0)
            level = weight * rest_inv
            if keep is not None:
                keep(number, weight, level)
            factor = level - weight * lax.rsqrt(now_sq)
            fx = fx + factor * now_x
            if both:
                fy = fy + factor * now_y
    return fx, fy


def second_forces(get_dx, get_dy, kept):
    masks, _ = lane_masks()
    dx0, dy0 = get_dx(0, 0), get_dy(0, 0)
    fx = jnp.zeros((8, PTS), F32)
    fy = jnp.zeros((8, PTS), F32)
    for oy in SIDEWAYS:
        dxs, dys = moved(get_dx, oy, masks), moved(get_dy, oy, masks)
        for number, (ox, other) in enumerate(OFFSETS):
            if other != oy:
                continue
            now_x = across(dxs, ox, masks) - (dx0 - float(ox))
            now_y = across(dys, ox, masks) - (dy0 - float(oy))
            now_sq = now_x * now_x + now_y * now_y + DELTA_SQ
            weight, level = kept(number)
            factor = level - weight * lax.rsqrt(now_sq)
            fx = fx + factor * now_x
            fy = fy + factor * now_y
    return fx, fy


def widen(row_of, count):
    lane, sub = lanes(), subs()
    index = sub * TILE_Y + (lane % 64) // SPLIT
    out = []
    for j in range(count):
        left, right = (
            jnp.take_along_axis(jnp.broadcast_to(row_of(b), (8, PTS)), index, axis=1) for b in (2 * j, 2 * j + 1)
        )
        out.append(jnp.where(lane < 64, left, right))
    return out


def narrow(block_of, tiles):
    lane, sub = lanes(), subs()
    out = []
    for b in tiles:
        held = block_of(b // 2)
        held = held + turn(held, -1)
        held = held + turn(held, -2)
        picked = jnp.take_along_axis(held, 64 * (b % 2) + SPLIT * (lane % TILE_Y), axis=1)
        out.append(jnp.sum(jnp.where(sub == lane // TILE_Y, picked, 0.0), axis=0, keepdims=True))
    return out


def lay_out(ref, at, j, block):
    for row in range(TILE_X):
        ref[at + (row, slice(None), slice(j * PTS, (j + 1) * PTS))] = jnp.broadcast_to(block[row : row + 1], (8, PTS))


class Place:
    def __init__(self, nx, ny, shell_rows, shell_cols):
        self.nx, self.ny = nx, ny
        self.gx, self.gy = lax.axis_index("gx"), lax.axis_index("gy")
        self.shell_rows, self.shell_cols = shell_rows, shell_cols
        self.width = shell_cols * ny
        self.band = shell_rows * nx // TILE_X
        self.bands = shell_rows // self.band
        self.front = self.gx == nx - 1

    def sides(self, first, second):
        even = self.gy % 2 == 0
        right = jnp.where(even, first, second)
        left = jnp.where(even, second, first)
        right = jnp.where(self.gy < self.ny - 1, right, 0.0)
        left = jnp.where(self.gy > 0, left, 0.0)
        return right, left

    def nodes(self, row, columns):
        shape = (8, columns)
        col = lax.broadcasted_iota(I32, shape, 1)
        if columns > self.shell_cols:
            col = jnp.where(col >= self.shell_cols + 64, col - columns, col)
        first = (self.gx * self.shell_rows + row) * self.width + self.gy * self.shell_cols
        return (first + lax.broadcasted_iota(I32, shape, 0) * self.width + col).astype(F32)

    def band_of(self, row):
        return jnp.clip((self.gx * self.shell_rows + row + self.band) // self.band - 1, 0, TILE_X - 1)


Y_ROWS = 88


def pack_sides(place_args, disp, vel, jit, words, node, inter, shell, speed, first, second, wide_ref):
    place = Place(*place_args)
    tiles = disp.shape[2]
    even = place.gy % 2 == 0
    blocks = place.shell_cols // PTS
    numbers = node[...].astype(F32)
    edge_blocks = (0, blocks - 1)
    for j in edge_blocks:
        lay_out(wide_ref, (), j, widen(lambda b: numbers[b : b + 1], blocks)[j])
    held = {}
    for j in edge_blocks:
        total = jnp.zeros((8, PTS), F32)
        for part in range(place.bands):
            summed = jnp.zeros((8, PTS), F32)
            for row in range(part * place.band, (part + 1) * place.band, 8):
                wanted = wide_ref[place.band_of(row), :, j * PTS : (j + 1) * PTS]
                ids = place.nodes(row, PTS) + float(j * PTS)
                summed = summed + jnp.where(wanted == ids, shell[row : row + 8, j * PTS : (j + 1) * PTS], 0.0)
            summed = jnp.sum(summed, axis=0, keepdims=True)
            total = total + jnp.where(subs() == place.band_of(part * place.band), summed, 0.0)
        held[j] = total
    met = narrow(lambda j: held[j], (0, tiles - 1))

    def send(ref, to_right):
        edge = jnp.where(to_right, tiles - 1, 0)
        for f, source in enumerate((disp, disp, vel, vel, jit, jit)):
            ref[8 * f : 8 * f + 8, :] = jnp.where(
                to_right, source[f % 2, :, tiles - 1, :], source[f % 2, :, 0, :]
            )
        ref[48:Y_ROWS, :] = jnp.zeros((Y_ROWS - 48, PTS), F32)
        edge_words = jnp.where(to_right, words[:, tiles - 1, :], words[:, 0, :])
        ref[48:56, 0:9] = (edge_words & 65535).astype(F32)
        ref[56:64, 0:9] = jnp.right_shift(edge_words, 16).astype(F32)
        ref[64:65, :] = jnp.where(to_right, numbers[tiles - 1 : tiles], numbers[0:1])
        ref[65:66, :] = jnp.where(to_right, inter[tiles - 1 : tiles, :], inter[0:1, :])
        ref[66:67, :] = jnp.where(to_right, met[1], met[0])
        for f, source in enumerate((shell, speed)):
            last = jnp.transpose(source[:, place.shell_cols - PTS :])[PTS - 8 :]
            head = jnp.transpose(source[:, 0:PTS])[:8]
            ref[72 + 8 * f : 80 + 8 * f, :] = jnp.where(to_right, last, head)

    send(first, even)
    send(second, jnp.logical_not(even))


HALO_ROWS = 120
CONTACT_ROWS = 24


def shell_strip(right, left, at):
    middle = jnp.zeros((PTS - 16, PTS), F32)
    return jnp.transpose(jnp.concatenate([right[at : at + 8], middle, left[at : at + 8]], axis=0))


def laplace_pass(source, target, blocks):
    for k in blocks:
        row = 8 * k
        here = source[row : row + 8, :]
        around = source[row - 1 : row + 7, :] + source[row + 1 : row + 9, :] + turn(here, 1) + turn(here, -1)
        target[row : row + 8, :] = around - 4.0 * here


def laplace_of(source, k):
    row = 8 * k
    here = source[row : row + 8, :]
    around = source[row - 1 : row + 7, :] + source[row + 1 : row + 9, :] + turn(here, 1) + turn(here, -1)
    return around - 4.0 * here


def pack_ends(
    place_args, shifts, disp, vel, jit, words, node, inter, shell, speed, first, second, *refs
):
    place = Place(*place_args)
    outs = refs[: len(shifts)]
    own, strip_d, strip_v, grid, tall, tall_v, bent, wide_ref = refs[len(shifts) :]
    rows_a, tiles = disp.shape[1], disp.shape[2]
    rows, cols = place.shell_rows, place.shell_cols
    right, left = place.sides(first[...], second[...])

    grid[...] = jnp.zeros_like(grid)
    for f, (source, at) in enumerate(((jit, 32), (jit, 40), (disp, 0), (disp, 8))):
        for level, a in enumerate((rows_a - 2, rows_a - 1)):
            base = (level + 1) * STRIDE
            values, from_right, from_left = source[f % 2, a], right[at + a : at + a + 1], left[at + a : at + a + 1]
            if f >= 2:
                far = 32 + 8 * (f % 2) + a
                values = values + jit[f % 2, a]
                from_right = from_right + right[far : far + 1]
                from_left = from_left + left[far : far + 1]
            grid[f, base + 8 : base + 16, :] = values
            grid[f, base + 16 : base + 17, :] = from_right
            grid[f, base + 7 : base + 8, :] = from_left

    def tile_getter(f):
        held = {}

        def get(dx, dy):
            if (dx, dy) not in held:
                base = (2 + dx) * STRIDE + 8 + dy
                held[dx, dy] = turn(grid[f, base : base + 8, :], TILE_Y * dy)
            return held[dx, dy]

        return get

    def words_getter():
        held = {}
        sub = subs()

        def get(dx, dy):
            if (dx, dy) not in held:
                s = slot(dx, dy)
                word = jnp.broadcast_to(words[rows_a - 1, :, s : s + 1], (8, PTS))
                if dx > 0:
                    word = jnp.zeros_like(word)
                if dy < 0:
                    word = jnp.where((sub == 0) & (place.gy == 0), 0, word)
                if dy > 0:
                    word = jnp.where((sub == tiles - 1) & (place.gy == place.ny - 1), 0, word)
                held[dx, dy] = word
            return held[dx, dy]

        return get

    force, _ = first_forces(
        tile_getter(0), tile_getter(1), tile_getter(2), tile_getter(3), words_getter(), both=False
    )
    gap = disp[0, rows_a - 1] + inter[...]
    last = rows_a - 1
    own[0:8, :] = gap + STEP_DT * (vel[0, last] + STEP_DT * force)
    own[8:16, :] = gap
    own[16:24, :] = jnp.zeros((8, PTS), F32)
    own[16:17, :] = right[last : last + 1] + right[65:66]
    own[17:18, :] = left[last : last + 1] + left[65:66]

    halo_d = shell_strip(right, left, 72)
    halo_v = shell_strip(right, left, 80)
    strip_d[...] = halo_d
    strip_v[...] = halo_v
    tall[...] = jnp.zeros_like(tall)
    tall_v[...] = jnp.zeros_like(tall_v)
    tall[PAD : PAD + rows, 0:cols] = shell[...]
    tall[PAD : PAD + rows, cols:WIDE] = halo_d
    tall_v[PAD : PAD + rows, 0:cols] = speed[...]
    bent[...] = jnp.zeros_like(bent)
    span = range(PAD // 8 - 1, (PAD + rows) // 8 + 1)
    laplace_pass(tall, bent, span)
    numbers = node[...].astype(F32)
    for j, block in enumerate(widen(lambda b: numbers[b : b + 1], cols // PTS)):
        lay_out(wide_ref, (), j, block)
    sub_wide = lax.broadcasted_iota(I32, (8, cols), 0)
    ahead = jnp.zeros((8, cols), F32)
    met = jnp.zeros((8, cols), F32)
    parts = [[-8]] + [list(range(p * place.band, (p + 1) * place.band, 8)) for p in range(place.bands)] + [[rows]]
    for part in parts:
        soon = jnp.zeros((8, cols), F32)
        now = jnp.zeros((8, cols), F32)
        band = place.band_of(part[0])
        for row in part:
            k = (PAD + row) // 8
            hit = wide_ref[band] == place.nodes(row, cols)
            bending = laplace_of(bent, k)[:, 0:cols]
            here = tall[PAD + row : PAD + row + 8, 0:cols]
            later = here + STEP_DT * (tall_v[PAD + row : PAD + row + 8, 0:cols] - (STEP_DT * BEND) * bending)
            soon = soon + jnp.where(hit, later, 0.0)
            if 0 <= row < rows:
                now = now + jnp.where(hit, here, 0.0)
        ahead = ahead + jnp.where(sub_wide == band, jnp.sum(soon, axis=0, keepdims=True), 0.0)
        if 0 <= part[0] < rows:
            met = met + jnp.where(sub_wide == band, jnp.sum(now, axis=0, keepdims=True), 0.0)
    base = CONTACT_ROWS
    own[base + 16 : base + 24, :] = jnp.zeros((8, PTS), F32)
    for b, row in enumerate(narrow(lambda j: ahead[:, j * PTS : (j + 1) * PTS], range(tiles))):
        own[base + b : base + b + 1, :] = row
    for b, row in enumerate(narrow(lambda j: met[:, j * PTS : (j + 1) * PTS], range(tiles))):
        own[base + 8 + b : base + 9 + b, :] = row
    own[base + 16 : base + 17, :] = right[66:67]
    own[base + 17 : base + 18, :] = left[66:67]

    mine = jnp.where(place.front, own[0:CONTACT_ROWS, :], own[base : base + CONTACT_ROWS, :])
    for shift, out in zip(shifts, outs):
        at = 0
        if shift & (shift + 1) == 0:
            at = HALO_ROWS
            down = (place.gx ^ shift) > place.gx
            edge = jnp.where(down, rows_a - 1, 0)
            for f, source in enumerate((disp, disp, vel, vel, jit, jit)):
                out[8 * f : 8 * f + 8, :] = source[f % 2, edge]
            out[48:80, :] = jnp.zeros((32, PTS), F32)
            edge_words = words[edge]
            out[48:56, 0:9] = (edge_words & 65535).astype(F32)
            out[56:64, 0:9] = jnp.right_shift(edge_words, 16).astype(F32)
            for f in range(8):
                for side, values in ((64, right), (72, left)):
                    low, high = values[8 * f : 8 * f + 1], values[8 * f + rows_a - 1 : 8 * f + rows_a]
                    out[side + f : side + f + 1, :] = jnp.where(down, high, low)
            for j in range(WIDE // PTS):
                cut = slice(j * PTS, (j + 1) * PTS)
                if j < cols // PTS:
                    d_low, d_high = shell[0:4, cut], shell[rows - 4 : rows, cut]
                    v_low, v_high = speed[0:2, cut], speed[rows - 2 : rows, cut]
                else:
                    d_low, d_high = halo_d[0:4], halo_d[rows - 4 : rows]
                    v_low, v_high = halo_v[0:2], halo_v[rows - 2 : rows]
                out[80 + 8 * j : 84 + 8 * j, :] = jnp.where(down, d_high, d_low)
                out[84 + 8 * j : 86 + 8 * j, :] = jnp.where(down, v_high, v_low)
                out[86 + 8 * j : 88 + 8 * j, :] = jnp.zeros((2, PTS), F32)
        out[at : at + CONTACT_ROWS, :] = mine


def both_steps(
    place_args, shifts, disp, vel, jit, words, node, inter, shell, speed, first, second, own, strip_d, strip_v, *refs
):
    place = Place(*place_args)
    ends = refs[: len(shifts)]
    out_disp, out_vel, out_shell, out_speed = refs[len(shifts) : len(shifts) + 4]
    grid, near, vels, kinds, weights, levels, tall, tall_v, bent, pushed, gaps, trial, halo = refs[len(shifts) + 4 :]
    rows_a, tiles = disp.shape[1], disp.shape[2]
    rows, cols = place.shell_rows, place.shell_cols
    right, left = place.sides(first[...], second[...])

    halo[...] = jnp.zeros_like(halo)
    contact = jnp.where(place.front, own[0:CONTACT_ROWS, :], 0.0)
    owners = own[CONTACT_ROWS:, :]
    for shift, ref in zip(shifts, ends):
        partner = place.gx ^ shift
        at = 0
        if shift & (shift + 1) == 0:
            at = HALO_ROWS

            @pl.when(partner == place.gx - 1)
            def _():
                halo[0] = ref[0:HALO_ROWS, :]

            @pl.when(partner == place.gx + 1)
            def _():
                halo[1] = ref[0:HALO_ROWS, :]

        got = ref[at : at + CONTACT_ROWS, :]
        contact = jnp.where(partner == place.nx - 1, got, contact)
        owners = owners + got

    tall[...] = jnp.zeros_like(tall)
    tall_v[...] = jnp.zeros_like(tall_v)
    tall[PAD : PAD + rows, 0:cols] = shell[...]
    tall[PAD : PAD + rows, cols:WIDE] = strip_d[...]
    tall_v[PAD : PAD + rows, 0:cols] = speed[...]
    tall_v[PAD : PAD + rows, cols:WIDE] = strip_v[...]
    for j in range(WIDE // PTS):
        cut = slice(j * PTS, (j + 1) * PTS)
        tall[PAD - 4 : PAD, cut] = halo[0, 80 + 8 * j : 84 + 8 * j, :]
        tall_v[PAD - 2 : PAD, cut] = halo[0, 84 + 8 * j : 86 + 8 * j, :]
        tall[PAD + rows : PAD + rows + 4, cut] = halo[1, 80 + 8 * j : 84 + 8 * j, :]
        tall_v[PAD + rows : PAD + rows + 2, cut] = halo[1, 84 + 8 * j : 86 + 8 * j, :]
    numbers = node[...].astype(F32)
    node_rows = [numbers[b : b + 1] for b in range(tiles)] + [right[64:65], left[64:65]]
    gap_rows = [contact[8 + b : 9 + b] for b in range(tiles)] + [contact[16:17], contact[17:18]]
    soon_rows = [contact[b : b + 1] for b in range(tiles)]
    for j, (nodes, gap) in enumerate(zip(widen(node_rows.__getitem__, 5), widen(gap_rows.__getitem__, 5))):
        lay_out(gaps, (0,), j, nodes)
        lay_out(gaps, (1,), j, gap)
    for j, soon in enumerate(widen(soon_rows.__getitem__, 4)):
        lay_out(gaps, (2,), j, soon)
    bent[...] = jnp.zeros_like(bent)
    span = range(PAD // 8 - 1, (PAD + rows) // 8 + 1)
    laplace_pass(tall, bent, span)
    col = lax.broadcasted_iota(I32, (8, WIDE), 1)
    inside = jnp.where(col < cols, 1.0, 0.0)
    inside = jnp.where((col >= cols) & (col < cols + 64) & (place.gy < place.ny - 1), 1.0, inside)
    inside = jnp.where((col >= cols + 64) & (place.gy > 0), 1.0, inside)
    for k in span:
        row = 8 * k - PAD
        cut = slice(8 * k, 8 * k + 8)
        here = tall[cut, :]
        band = place.band_of(row)
        hit = gaps[0, band] == place.nodes(row, WIDE)
        push = jnp.where(hit, PENALTY * jnp.maximum(gaps[1, band] - here, 0.0), 0.0)
        fast = tall_v[cut, :] + STEP_DT * (push - BEND * laplace_of(bent, k))
        there = here + STEP_DT * fast
        keep = inside
        if row < 0:
            keep = inside * jnp.where(place.gx > 0, 1.0, 0.0)
        elif row >= rows:
            keep = inside * jnp.where(place.gx < place.nx - 1, 1.0, 0.0)
        tall[cut, :] = there * keep
        if 0 <= row < rows:
            tall_v[cut, :] = fast
            pushed[cut, :] = push
    laplace_pass(tall, bent, span)
    for k in range(PAD // 8, (PAD + rows) // 8):
        row = 8 * k - PAD
        cut = slice(8 * k, 8 * k + 8)
        here = tall[cut, 0:cols]
        band = place.band_of(row)
        hit = gaps[0, band, :, 0:cols] == place.nodes(row, cols)
        gap = gaps[2, band, :, 0:cols] - (STEP_DT * STEP_DT) * pushed[cut, 0:cols]
        push = jnp.where(hit, PENALTY * jnp.maximum(gap - here, 0.0), 0.0)
        fast = tall_v[cut, 0:cols] + STEP_DT * (push - BEND * laplace_of(bent, k)[:, 0:cols])
        out_speed[row : row + 8, :] = fast
        out_shell[row : row + 8, :] = here + STEP_DT * fast

    grid[...] = jnp.zeros_like(grid)
    top, low = STRIDE, (rows_a + 2) * STRIDE
    for f in range(4):
        source, at = ((jit, 32 + 8 * f), (disp, 8 * (f - 2)))[f >= 2]
        extra = 32 + 8 * (f - 2)

        def with_rest(values, rest):
            return values + rest if f >= 2 else values

        for a in range(rows_a):
            base = (a + 2) * STRIDE + 8
            grid[f, base : base + tiles, :] = with_rest(source[f % 2, a], jit[f % 2, a])
        for side, offset in ((right, 16), (left, 7)):
            grid[f, pl.ds(2 * STRIDE + offset, rows_a, stride=STRIDE), :] = with_rest(
                side[at : at + 8], side[extra : extra + 8]
            )
        for end, base in ((0, top), (1, low)):
            grid[f, base + 8 : base + 16, :] = with_rest(halo[end, at : at + 8, :], halo[end, extra : extra + 8, :])
            for part, offset in ((64, 16), (72, 7)):
                grid[f, base + offset : base + offset + 1, :] = with_rest(
                    halo[end, part + at // 8 : part + at // 8 + 1, :],
                    halo[end, part + extra // 8 : part + extra // 8 + 1, :],
                )

    blocks = rows_a + 5
    corner = 8 * (rows_a + 4)

    def spread_grid(f, row_blocks, edges):
        for dx in (-1, 0, 1):
            for dy in (-1, 0, 1):
                s = slot(dx, dy)
                for t in row_blocks:
                    a = t if t < rows_a else (-1, rows_a)[t - rows_a]
                    base = (a + 2 + dx) * STRIDE + 8 + dy
                    near[f, s, 8 * t : 8 * t + 8, :] = turn(grid[f, base : base + 8, :], TILE_Y * dy)
                if edges:
                    for t, offset in ((rows_a + 2, 7), (rows_a + 3, 16)):
                        near[f, s, 8 * t : 8 * t + 8, :] = turn(
                            grid[f, pl.ds((2 + dx) * STRIDE + offset + dy, 8, stride=STRIDE), :], TILE_Y * dy
                        )
                    near[f, s, corner : corner + 8, :] = jnp.zeros((8, PTS), F32)
                    for n, offset in enumerate((7, 16)):
                        for m, base in enumerate((top, low)):
                            start = base + dx * STRIDE + offset + dy
                            at = corner + 2 * n + m
                            near[f, s, at : at + 1, :] = turn(grid[f, start : start + 1, :], TILE_Y * dy)

    for f in range(4):
        spread_grid(f, range(rows_a + 2), True)

    for f in range(2):
        at = 16 + 8 * f
        for a in range(rows_a):
            vels[f, 8 * a : 8 * a + 8, :] = vel[f, a]
        for end in (0, 1):
            t = rows_a + end
            vels[f, 8 * t : 8 * t + 8, :] = halo[end, at : at + 8, :]
        vels[f, corner - 16 : corner - 8, :] = left[at : at + 8]
        vels[f, corner - 8 : corner, :] = right[at : at + 8]
        vels[f, corner : corner + 8, :] = jnp.zeros((8, PTS), F32)
        for n, part in enumerate((72, 64)):
            for end in (0, 1):
                vels[f, corner + 2 * n + end : corner + 2 * n + end + 1, :] = halo[
                    end, part + 2 + f : part + 3 + f, :
                ]

    def joined(low_part, high_part):
        return jnp.left_shift(high_part.astype(I32), 16) | low_part.astype(I32)

    sub = subs()
    west, east = place.gy == 0, place.gy == place.ny - 1
    north, south = place.gx == 0, place.gx == place.nx - 1
    for t in range(blocks):
        if t < rows_a:
            packed = words[t]
        elif t < rows_a + 2:
            packed = joined(halo[t - rows_a, 48:56, :], halo[t - rows_a, 56:64, :])
        elif t < rows_a + 4:
            side = (left, right)[t - rows_a - 2]
            packed = joined(side[48:56], side[56:64])
        else:
            zero = jnp.zeros((4, PTS), F32)
            lows = [halo[end, part + 6 : part + 7, :] for part in (72, 64) for end in (0, 1)]
            highs = [halo[end, part + 7 : part + 8, :] for part in (72, 64) for end in (0, 1)]
            packed = joined(jnp.concatenate(lows + [zero], axis=0), jnp.concatenate(highs + [zero], axis=0))
        for dx in (-1, 0, 1):
            for dy in (-1, 0, 1):
                s = slot(dx, dy)
                word = jnp.broadcast_to(packed[:, s : s + 1], (8, PTS))
                if t < rows_a + 2:
                    if dy < 0:
                        word = jnp.where((sub == 0) & west, 0, word)
                    if dy > 0:
                        word = jnp.where((sub == tiles - 1) & east, 0, word)
                    if dx < 0 and t == 0:
                        word = jnp.where(north, 0, word)
                    if dx > 0 and t == rows_a - 1:
                        word = jnp.where(south, 0, word)
                elif t < rows_a + 4:
                    if dx < 0:
                        word = jnp.where((sub == 0) & north, 0, word)
                    if dx > 0:
                        word = jnp.where((sub == rows_a - 1) & south, 0, word)
                kinds[s, 8 * t : 8 * t + 8, :] = word

    def getter(ref, f, at):
        held = {}

        def get(dx, dy):
            if (dx, dy) not in held:
                cut = (slot(dx, dy), pl.ds(at, 8), slice(None))
                held[dx, dy] = ref[cut] if f is None else ref[(f,) + cut]
            return held[dx, dy]

        return get

    @pl.loop(0, blocks)
    def _(t):
        at = pl.multiple_of(8 * t, 8)

        def keep(number, weight, level):
            weights[number, pl.ds(at, 8), :] = weight
            levels[number, pl.ds(at, 8), :] = level

        fx, fy = first_forces(
            getter(near, 0, at),
            getter(near, 1, at),
            getter(near, 2, at),
            getter(near, 3, at),
            getter(kinds, None, at),
            keep,
        )
        trial[0, pl.ds(at, 8), :] = fx
        trial[1, pl.ds(at, 8), :] = fy

    here = jnp.where(place.front, 1.0, 0.0)
    push = PENALTY * here * jnp.maximum(contact[8:18] - owners[8:18], 0.0)
    last = rows_a - 1
    trial[0, 8 * last : 8 * last + 8, :] -= push[0:8]
    at = 8 * (rows_a + 2) + last
    trial[0, at : at + 1, :] -= push[9:10]
    trial[0, at + 8 : at + 9, :] -= push[8:9]
    for f in range(2):
        vels[f] = vels[f] + STEP_DT * trial[f]
        trial[f] = near[2 + f, slot(0, 0)] + STEP_DT * vels[f]
        for t in range(rows_a + 2):
            a = t if t < rows_a else (-1, rows_a)[t - rows_a]
            grid[2 + f, (a + 2) * STRIDE + 8 : (a + 2) * STRIDE + 16, :] = trial[f, 8 * t : 8 * t + 8, :]
        for t, offset in ((rows_a + 2, 7), (rows_a + 3, 16)):
            grid[2 + f, pl.ds(2 * STRIDE + offset, 8, stride=STRIDE), :] = trial[f, 8 * t : 8 * t + 8, :]
        for n, offset in enumerate((7, 16)):
            for m, base in enumerate((top, low)):
                at = corner + 2 * n + m
                grid[2 + f, base + offset : base + offset + 1, :] = trial[f, at : at + 1, :]
        spread_grid(2 + f, range(rows_a), False)

    @pl.loop(0, rows_a)
    def _(t):
        at = pl.multiple_of(8 * t, 8)

        def kept(number):
            return weights[number, pl.ds(at, 8), :], levels[number, pl.ds(at, 8), :]

        fx, fy = second_forces(getter(near, 2, at), getter(near, 3, at), kept)
        out_vel[0, t] = vels[0, pl.ds(at, 8), :] + STEP_DT * fx
        out_vel[1, t] = vels[1, pl.ds(at, 8), :] + STEP_DT * fy

    gap = trial[0, 8 * last : 8 * last + 8, :] - jit[0, last] + inter[...]
    reached = owners[0:8] + (STEP_DT * STEP_DT) * push[0:8]
    out_vel[0, last] = out_vel[0, last] - (STEP_DT * PENALTY) * here * jnp.maximum(gap - reached, 0.0)
    for f in range(2):
        for a in range(rows_a):
            out_disp[f, a] = (trial[f, 8 * a : 8 * a + 8, :] - jit[f, a]) + STEP_DT * out_vel[f, a]


def on_device(nx, ny, disp, vel, jit, words, node, inter, shell, speed):
    rows_a = disp.shape[1]
    rows, cols = shell.shape
    place_args = (nx, ny, rows, cols)
    shifts = tuple(range(1, nx))
    base = (disp, vel, jit, words, node, inter, shell, speed)

    def call(body, out, scratch, *args):
        return pl.pallas_call(
            body,
            out_shape=out,
            scratch_shapes=scratch,
            compiler_params=pltpu.CompilerParams(vmem_limit_bytes=40 * 1024 * 1024),
        )(*args)

    side = jax.ShapeDtypeStruct((Y_ROWS, PTS), F32)
    first, second = call(
        functools.partial(pack_sides, place_args), (side, side), [pltpu.VMEM((TILE_X, 8, cols), F32)], *base
    )
    first = lax.ppermute(first, "gy", [(i, i ^ 1) for i in range(ny)])
    second = lax.ppermute(second, "gy", [(i, ((i - 1) ^ 1) + 1 if 0 < i < ny - 1 else ny - 1 - i) for i in range(ny)])

    tall = pltpu.VMEM((rows + 2 * PAD, WIDE), F32)
    outs = [
        jax.ShapeDtypeStruct((CONTACT_ROWS + (HALO_ROWS if s & (s + 1) == 0 else 0), PTS), F32) for s in shifts
    ]
    outs += [jax.ShapeDtypeStruct((2 * CONTACT_ROWS, PTS), F32)]
    outs += [jax.ShapeDtypeStruct((rows, PTS), F32)] * 2
    *ends, own, strip_d, strip_v = call(
        functools.partial(pack_ends, place_args, shifts),
        outs,
        [pltpu.VMEM((4, 4 * STRIDE, PTS), F32), tall, tall, tall, pltpu.VMEM((TILE_X, 8, cols), F32)],
        *base,
        first,
        second,
    )
    ends = [lax.ppermute(e, "gx", [(i, i ^ s) for i in range(nx)]) for s, e in zip(shifts, ends)]

    held = 8 * (rows_a + 5)
    scratch = [
        pltpu.VMEM((4, (rows_a + 4) * STRIDE, PTS), F32),
        pltpu.VMEM((4, 9, held, PTS), F32),
        pltpu.VMEM((2, held, PTS), F32),
        pltpu.VMEM((9, held, PTS), I32),
        pltpu.VMEM((len(OFFSETS), held, PTS), F32),
        pltpu.VMEM((len(OFFSETS), held, PTS), F32),
        tall,
        tall,
        tall,
        tall,
        pltpu.VMEM((3, TILE_X, 8, WIDE), F32),
        pltpu.VMEM((2, held, PTS), F32),
        pltpu.VMEM((2, HALO_ROWS, PTS), F32),
    ]
    out = [jax.ShapeDtypeStruct(x.shape, F32) for x in (disp, vel, shell, speed)]
    return tuple(
        call(functools.partial(both_steps, place_args, shifts), out, scratch, *base, first, second, own, strip_d, strip_v, *ends)
    )


def solution(mesh):
    in_specs = (
        P(None, "gx", "gy", None),
        P(None, "gx", "gy", None),
        P(None, "gx", "gy", None),
        P("gx", "gy", None),
        P("gy", None),
        P("gy", None),
        P("gx", "gy"),
        P("gx", "gy"),
    )
    out_specs = (P(None, "gx", "gy", None), P(None, "gx", "gy", None), P("gx", "gy"), P("gx", "gy"))
    body = functools.partial(on_device, mesh.shape["gx"], mesh.shape["gy"])
    return jax.shard_map(body, mesh=mesh, in_specs=in_specs, out_specs=out_specs, check_vma=False)
```

time: 350 us -> 34.8 us (0.10)
  the two profiles are of different devices: /device:TPU:1 before, /device:TPU:0 now
where the time goes in v1:
time: 34.8 us; the launch traced here: 34.3 us
  Pallas kernels  13.1 us (38%)
  starting transfers between devices  8.78 us (25%)
  local copies, waits for them, and re-layouts  6.54 us (19%)
  waiting for transfers between devices  5.23 us (15%)
  between operations  0.66 us (2%)
    pallas_call x3, Pallas kernels, call(): pl.pallas_call(body, out_shape=out, scratch_shapes=scratch, compiler_para...  13.1 us
    unnamed x16, local copies, waits for them, and re-layouts  6.54 us
    ppermute x1, starting transfers between devices, on_device(): lax.ppermute(second, 'gy', [(i, (i - 1 ^ 1) + 1 if 0 < i < ny - 1 else ny...  4.71 us
    ppermute x3, starting transfers between devices, on_device(): lax.ppermute(e, 'gx', [(i, i ^ s) for i in range(nx)])  3.55 us
    ppermute x3, waiting for transfers between devices, on_device(): lax.ppermute(e, 'gx', [(i, i ^ s) for i in range(nx)])  3.39 us
    ppermute x1, waiting for transfers between devices, on_device(): lax.ppermute(second, 'gy', [(i, (i - 1 ^ 1) + 1 if 0 < i < ny - 1 else ny...  1.83 us
  transfers between devices with their start and end apart: 5, of which 2 were waited for; matrix products, arithmetic and copies ran while one was open for 0% of the time, Pallas kernels for 0%

profile of v1, /device:TPU:0, one launch (start us, length us, event | category | flops | bytes accessed | tf_op | source)
XLA Modules:
  0.0 34.3 jit_solution(5891067301159791058)
XLA Ops:
  0.6 0.0 copy-start
  0.6 0.9 %copy-done = f32[128,512]{1,0:T(8,128)S(1)} copy-done((f32[128,512]{1,0:T(8,128)S(1)}, f32[128,512]{1,0:T(8,128)}, u32[]{:S(2)}) %copy-start) | copy-done | bytes 262168
  1.6 0.0 copy-start.1
  1.6 0.9 %copy-done.1 = f32[128,512]{1,0:T(8,128)S(1)} copy-done((f32[128,512]{1,0:T(8,128)S(1)}, f32[128,512]{1,0:T(8,128)}, u32[]{:S(2)}) %copy-start.1) | copy-done | bytes 262168
  2.5 0.0 copy-start.2
  2.5 0.8 %copy-done.2 = f32[2,8,8,128]{3,2,1,0:T(8,128)S(1)} copy-done((f32[2,8,8,128]{3,2,1,0:T(8,128)S(1)}, f32[2,8,8,128]{3,2,1,0:T(8,128)}, u32[]{:S(2)}) %copy-start.2) | copy-done | bytes 65560
  3.4 0.0 copy-start.3
  3.4 0.8 %copy-done.3 = f32[2,8,8,128]{3,2,1,0:T(8,128)S(1)} copy-done((f32[2,8,8,128]{3,2,1,0:T(8,128)S(1)}, f32[2,8,8,128]{3,2,1,0:T(8,128)}, u32[]{:S(2)}) %copy-start.3) | copy-done | bytes 65560
  4.2 0.0 copy-start.4
  4.2 0.8 %copy-done.4 = f32[2,8,8,128]{3,2,1,0:T(8,128)S(1)} copy-done((f32[2,8,8,128]{3,2,1,0:T(8,128)S(1)}, f32[2,8,8,128]{3,2,1,0:T(8,128)}, u32[]{:S(2)}) %copy-start.4) | copy-done | bytes 65560
  5.1 0.0 copy-start.5
  5.1 0.8 %copy-done.5 = s32[8,8,9]{2,1,0:T(8,128)S(1)} copy-done((s32[8,8,9]{2,1,0:T(8,128)S(1)}, s32[8,8,9]{2,1,0:T(8,128)}, u32[]{:S(2)}) %copy-start.5) | copy-done | bytes 2328
  5.8 0.0 copy-start.6
  5.8 0.7 %copy-done.6 = s32[8,128]{1,0:T(8,128)S(1)} copy-done((s32[8,128]{1,0:T(8,128)S(1)}, s32[8,128]{1,0:T(8,128)}, u32[]{:S(2)}) %copy-start.6) | copy-done | bytes 4120
  6.5 0.0 copy-start.7
  6.5 0.7 %copy-done.7 = f32[8,128]{1,0:T(8,128)S(1)} copy-done((f32[8,128]{1,0:T(8,128)S(1)}, f32[8,128]{1,0:T(8,128)}, u32[]{:S(2)}) %copy-start.7) | copy-done | bytes 4120
  7.2 0.4 %shard_map.111 = (f32[88,128]{1,0:T(8,128)S(1)}, f32[88,128]{1,0:T(8,128)S(1)}) custom-call(f32[2,8,8,128]{3,2,1,0:T(8,128)S(1)} %copy-done.2, f32[2,8,8,128]{3,2,1,0:T(8,128)S(1)} %copy-done.3, f32[2,8,8,128]{3,2,1,0:T(8,128)S(1)} %copy-done.4, s32[8,8,9]{2,1,0:T(8,128)S(1)} %copy-done.5, s32[8,128]{1,0:T(8,128)S(1)} %copy-done.6, f32[8,128]{1,0:T(8,128)S(1)} %copy-done.7, ...), custom_call_target="tpu_custom_call" | custom-call | tf_op jit(solution)/shard_map/pallas_call | solution.py:704
  7.6 0.5 %collective-permute-start = (f32[88,128]{1,0:T(8,128)S(1)}, f32[88,128]{1,0:T(8,128)S(1)}, u32[]{:S(2)}, u32[]{:S(2)}) collective-permute-start(f32[88,128]{1,0:T(8,128)S(1)} %get-tuple-element.12), channel_id=1, source_target_pairs={{0,1},{1,0},{2,3},{3,2},{4,5},{5,4},{6,7},{7,6},{8,9},{9,8},{10,11... | collective-permute-start | bytes 135176 | tf_op jit(solution)/shard_map/ppermute | solution.py:715
  8.1 4.7 %collective-permute-start.1 = (f32[88,128]{1,0:T(8,128)S(1)}, f32[88,128]{1,0:T(8,128)S(1)}, u32[]{:S(2)}, u32[]{:S(2)}) collective-permute-start(f32[88,128]{1,0:T(8,128)S(1)} %get-tuple-element.13), channel_id=1, source_target_pairs={{0,7},{1,2},{2,1},{3,4},{4,3},{5,6},{6,5},{7,0},{8,15},{9,10},{10,... | collective-permute-start | bytes 135176 | tf_op jit(solution)/shard_map/ppermute | solution.py:716
  12.8 0.0 collective-permute-done.first
  12.8 1.8 %collective-permute-done.1.second = f32[88,128]{1,0:T(8,128)S(1)} collective-permute-done((f32[88,128]{1,0:T(8,128)S(1)}, f32[88,128]{1,0:T(8,128)S(1)}, u32[]{:S(2)}, u32[]{:S(2)}) %collective-permute-start.1) | collective-permute-done | bytes 45088 | tf_op jit(solution)/shard_map/ppermute | solution.py:716
  14.7 1.6 %shard_map.112 = (f32[144,128]{1,0:T(8,128)S(1)}, f32[24,128]{1,0:T(8,128)S(1)}, f32[144,128]{1,0:T(8,128)S(1)}, f32[48,128]{1,0:T(8,128)S(1)}, f32[128,128]{1,0:T(8,128)S(1)}, /*index=5*/f32[128,128]{1,0:T(8,128)S(1)}) custom-call(f32[2,8,8,128]{3,2,1,0:T(8,128)S(1)} %copy-done.2, f32[2,8,8,128]{3,2,1,0:T(8,128)S(1)} %copy-done.3, ...), custom_call_target="tpu_custom_call" | custom-call | tf_op jit(solution)/shard_map/pallas_call | solution.py:704
  16.3 1.6 %collective-permute-start.2 = (f32[144,128]{1,0:T(8,128)S(1)}, f32[144,128]{1,0:T(8,128)S(1)}, u32[]{:S(2)}, u32[]{:S(2)}) collective-permute-start(f32[144,128]{1,0:T(8,128)S(1)} %get-tuple-element.17), channel_id=1, source_target_pairs={{0,8},{8,0},{16,24},{24,16},{1,9},{9,1},{17,25},{25,17},{2,10},{10... | collective-permute-start | bytes 221192 | tf_op jit(solution)/shard_map/ppermute | solution.py:732
  17.8 1.5 %collective-permute-start.4 = (f32[144,128]{1,0:T(8,128)S(1)}, f32[144,128]{1,0:T(8,128)S(1)}, u32[]{:S(2)}, u32[]{:S(2)}) collective-permute-start(f32[144,128]{1,0:T(8,128)S(1)} %get-tuple-element.19), channel_id=1, source_target_pairs={{0,24},{8,16},{16,8},{24,0},{1,25},{9,17},{17,9},{25,1},{2,26},{10... | collective-permute-start | bytes 221192 | tf_op jit(solution)/shard_map/ppermute | solution.py:732
  19.3 0.5 %collective-permute-start.3 = (f32[24,128]{1,0:T(8,128)S(1)}, f32[24,128]{1,0:T(8,128)S(1)}, u32[]{:S(2)}, u32[]{:S(2)}) collective-permute-start(f32[24,128]{1,0:T(8,128)S(1)} %get-tuple-element.18), channel_id=1, source_target_pairs={{0,16},{8,24},{16,0},{24,8},{1,17},{9,25},{17,1},{25,9},{2,18},{10... | collective-permute-start | bytes 36872 | tf_op jit(solution)/shard_map/ppermute | solution.py:732
  19.8 3.4 %collective-permute-done.3.refs_1_ = f32[24,128]{1,0:T(8,128)S(1)} collective-permute-done((f32[24,128]{1,0:T(8,128)S(1)}, f32[24,128]{1,0:T(8,128)S(1)}, u32[]{:S(2)}, u32[]{:S(2)}) %collective-permute-start.3) | collective-permute-done | bytes 12320 | tf_op jit(solution)/shard_map/ppermute | solution.py:732
  23.2 0.0 collective-permute-done.2.refs_0_
  23.2 0.0 collective-permute-done.4.refs_2_
  23.2 11.1 %shard_map.113 = (f32[2,8,8,128]{3,2,1,0:T(8,128)}, f32[2,8,8,128]{3,2,1,0:T(8,128)}, f32[128,512]{1,0:T(8,128)}, f32[128,512]{1,0:T(8,128)}) custom-call(f32[2,8,8,128]{3,2,1,0:T(8,128)S(1)} %copy-done.2, f32[2,8,8,128]{3,2,1,0:T(8,128)S(1)} %copy-done.3, f32[2,8,8,128]{3,2,1,0:T(8,128)S(1)} %copy-done.4, s32[8,8,9]{2,1,0:T(8,128)S(1)} %copy-done.5, ...), custom_call_target="tpu_custom_call" | custom-call | tf_op jit(solution)/shard_map/pallas_call | solution.py:704
Async XLA Ops:
  0.6 1.0 %copy-start = (f32[128,512]{1,0:T(8,128)S(1)}, f32[128,512]{1,0:T(8,128)}, u32[]{:S(2)}) copy-start(f32[128,512]{1,0:T(8,128)} %shell.5) | copy-start | bytes 786436
  1.6 0.9 %copy-start.1 = (f32[128,512]{1,0:T(8,128)S(1)}, f32[128,512]{1,0:T(8,128)}, u32[]{:S(2)}) copy-start(f32[128,512]{1,0:T(8,128)} %speed.5) | copy-start | bytes 786436
  2.5 0.8 %copy-start.2 = (f32[2,8,8,128]{3,2,1,0:T(8,128)S(1)}, f32[2,8,8,128]{3,2,1,0:T(8,128)}, u32[]{:S(2)}) copy-start(f32[2,8,8,128]{3,2,1,0:T(8,128)} %disp.5) | copy-start | bytes 196612
  3.4 0.8 %copy-start.3 = (f32[2,8,8,128]{3,2,1,0:T(8,128)S(1)}, f32[2,8,8,128]{3,2,1,0:T(8,128)}, u32[]{:S(2)}) copy-start(f32[2,8,8,128]{3,2,1,0:T(8,128)} %vel.5) | copy-start | bytes 196612
  4.2 0.8 %copy-start.4 = (f32[2,8,8,128]{3,2,1,0:T(8,128)S(1)}, f32[2,8,8,128]{3,2,1,0:T(8,128)}, u32[]{:S(2)}) copy-start(f32[2,8,8,128]{3,2,1,0:T(8,128)} %jit.5) | copy-start | bytes 196612
  5.1 0.8 %copy-start.5 = (s32[8,8,9]{2,1,0:T(8,128)S(1)}, s32[8,8,9]{2,1,0:T(8,128)}, u32[]{:S(2)}) copy-start(s32[8,8,9]{2,1,0:T(8,128)} %words.5) | copy-start | bytes 6916
  5.8 0.7 %copy-start.6 = (s32[8,128]{1,0:T(8,128)S(1)}, s32[8,128]{1,0:T(8,128)}, u32[]{:S(2)}) copy-start(s32[8,128]{1,0:T(8,128)} %node.5) | copy-start | bytes 12292
  6.5 0.7 %copy-start.7 = (f32[8,128]{1,0:T(8,128)S(1)}, f32[8,128]{1,0:T(8,128)}, u32[]{:S(2)}) copy-start(f32[8,128]{1,0:T(8,128)} %inter.5) | copy-start | bytes 12292
  7.6 5.2 %collective-permute-start = (f32[88,128]{1,0:T(8,128)S(1)}, f32[88,128]{1,0:T(8,128)S(1)}, u32[]{:S(2)}, u32[]{:S(2)}) collective-permute-start(f32[88,128]{1,0:T(8,128)S(1)} %get-tuple-element.12), channel_id=1, source_target_pairs={{0,1},{1,0},{2,3},{3,2},{4,5},{5,4},{6,7},{7,6},{8,9},{9,8},{10,11... | collective-permute-start | bytes 135176 | tf_op jit(solution)/shard_map/ppermute | solution.py:715
  8.1 6.5 %collective-permute-start.1 = (f32[88,128]{1,0:T(8,128)S(1)}, f32[88,128]{1,0:T(8,128)S(1)}, u32[]{:S(2)}, u32[]{:S(2)}) collective-permute-start(f32[88,128]{1,0:T(8,128)S(1)} %get-tuple-element.13), channel_id=1, source_target_pairs={{0,7},{1,2},{2,1},{3,4},{4,3},{5,6},{6,5},{7,0},{8,15},{9,10},{10,... | collective-permute-start | bytes 135176 | tf_op jit(solution)/shard_map/ppermute | solution.py:716
  16.3 6.9 %collective-permute-start.2 = (f32[144,128]{1,0:T(8,128)S(1)}, f32[144,128]{1,0:T(8,128)S(1)}, u32[]{:S(2)}, u32[]{:S(2)}) collective-permute-start(f32[144,128]{1,0:T(8,128)S(1)} %get-tuple-element.17), channel_id=1, source_target_pairs={{0,8},{8,0},{16,24},{24,16},{1,9},{9,1},{17,25},{25,17},{2,10},{10... | collective-permute-start | bytes 221192 | tf_op jit(solution)/shard_map/ppermute | solution.py:732
  17.8 5.4 %collective-permute-start.4 = (f32[144,128]{1,0:T(8,128)S(1)}, f32[144,128]{1,0:T(8,128)S(1)}, u32[]{:S(2)}, u32[]{:S(2)}) collective-permute-start(f32[144,128]{1,0:T(8,128)S(1)} %get-tuple-element.19), channel_id=1, source_target_pairs={{0,24},{8,16},{16,8},{24,0},{1,25},{9,17},{17,9},{25,1},{2,26},{10... | collective-permute-start | bytes 221192 | tf_op jit(solution)/shard_map/ppermute | solution.py:732
  19.3 3.9 %collective-permute-start.3 = (f32[24,128]{1,0:T(8,128)S(1)}, f32[24,128]{1,0:T(8,128)S(1)}, u32[]{:S(2)}, u32[]{:S(2)}) collective-permute-start(f32[24,128]{1,0:T(8,128)S(1)} %get-tuple-element.18), channel_id=1, source_target_pairs={{0,16},{8,24},{16,0},{24,8},{1,17},{9,25},{17,1},{25,9},{2,18},{10... | collective-permute-start | bytes 36872 | tf_op jit(solution)/shard_map/ppermute | solution.py:732

commit v2 on v1

--- a/solution.py
+++ b/solution.py
@@ -218,8 +218,19 @@
 Y_ROWS = 88
 
 
-def pack_sides(place_args, disp, vel, jit, words, node, inter, shell, speed, first, second, wide_ref):
+def fetch(pairs, sems):
+    copies = [pltpu.make_async_copy(source, target, sems.at[n]) for n, (source, target) in enumerate(pairs)]
+    for copy in copies:
+        copy.start()
+    for copy in copies:
+        copy.wait()
+
+
+def pack_sides(place_args, *refs):
+    sources, (first, second), held, (wide_ref, sems) = refs[:8], refs[8:10], refs[10:18], refs[18:]
     place = Place(*place_args)
+    fetch(list(zip(sources, held)), sems)
+    disp, vel, jit, words, node, inter, shell, speed = held
     tiles = disp.shape[2]
     even = place.gy % 2 == 0
     blocks = place.shell_cols // PTS
@@ -700,17 +711,25 @@
     shifts = tuple(range(1, nx))
     base = (disp, vel, jit, words, node, inter, shell, speed)
 
-    def call(body, out, scratch, *args):
+    def call(body, out, scratch, *args, far=0):
+        args = [pltpu.with_memory_space_constraint(x, pltpu.MemorySpace.HBM) for x in args[:far]] + list(args[far:])
+        specs = [pl.BlockSpec(memory_space=pltpu.MemorySpace.HBM)] * far
+        specs += [pl.BlockSpec(memory_space=pltpu.VMEM)] * (len(args) - far)
         return pl.pallas_call(
             body,
             out_shape=out,
+            in_specs=specs,
             scratch_shapes=scratch,
             compiler_params=pltpu.CompilerParams(vmem_limit_bytes=40 * 1024 * 1024),
         )(*args)
 
     side = jax.ShapeDtypeStruct((Y_ROWS, PTS), F32)
-    first, second = call(
-        functools.partial(pack_sides, place_args), (side, side), [pltpu.VMEM((TILE_X, 8, cols), F32)], *base
+    first, second, *base = call(
+        functools.partial(pack_sides, place_args),
+        [side, side] + [jax.ShapeDtypeStruct(x.shape, x.dtype) for x in base],
+        [pltpu.VMEM((TILE_X, 8, cols), F32), pltpu.SemaphoreType.DMA((len(base),))],
+        *base,
+        far=len(base),
     )
     first = lax.ppermute(first, "gy", [(i, i ^ 1) for i in range(ny)])
     second = lax.ppermute(second, "gy", [(i, ((i - 1) ^ 1) + 1 if 0 < i < ny - 1 else ny - 1 - i) for i in range(ny)])

time: 34.8 us -> 29.2 us (0.84); the launches traced: 34.3 us -> 29.1 us
  local copies, waits for them, and re-layouts: 6.54 us -> 0 us
  Pallas kernels: 13.1 us -> 14.4 us
    unnamed x16 -> x0, local copies, waits for them, and re-layouts: 6.54 us -> none
    pallas_call x3, Pallas kernels: 13.1 us -> 14.4 us  [call(): pl.pallas_call(body, out_shape=out, in_specs=specs, scratch_shapes=scratc...]
where the time goes in v2:
time: 29.2 us; the launch traced here: 29.1 us
  Pallas kernels  14.4 us (49%)
  starting transfers between devices  8.78 us (30%)
  waiting for transfers between devices  5.23 us (18%)
  between operations  0.65 us (2%)
    pallas_call x3, Pallas kernels, call(): pl.pallas_call(body, out_shape=out, in_specs=specs, scratch_shapes=scratc...  14.4 us
    ppermute x1, starting transfers between devices, on_device(): lax.ppermute(second, 'gy', [(i, (i - 1 ^ 1) + 1 if 0 < i < ny - 1 else ny...  4.71 us
    ppermute x3, starting transfers between devices, on_device(): lax.ppermute(e, 'gx', [(i, i ^ s) for i in range(nx)])  3.55 us
    ppermute x3, waiting for transfers between devices, on_device(): lax.ppermute(e, 'gx', [(i, i ^ s) for i in range(nx)])  3.39 us
    ppermute x1, waiting for transfers between devices, on_device(): lax.ppermute(second, 'gy', [(i, (i - 1 ^ 1) + 1 if 0 < i < ny - 1 else ny...  1.83 us
  transfers between devices with their start and end apart: 5, of which 2 were waited for; matrix products, arithmetic and copies ran while one was open for 0% of the time, Pallas kernels for 0%

profile of v2, /device:TPU:0, one launch (start us, length us, event | category | flops | bytes accessed | tf_op | source)
XLA Modules:
  0.0 29.1 jit_solution(2539025900234205737)
XLA Ops:
  0.6 1.7 %shard_map.111 = (f32[88,128]{1,0:T(8,128)S(1)}, f32[88,128]{1,0:T(8,128)S(1)}, f32[2,8,8,128]{3,2,1,0:T(8,128)S(1)}, f32[2,8,8,128]{3,2,1,0:T(8,128)S(1)}, f32[...) custom-call(f32[2,8,8,128]{3,2,1,0:T(8,128)} %refs_0_.1, ...), custom_call_target="tpu_custom_call" | custom-call | tf_op jit(solution)/shard_map/pallas_call | solution.py:718
  2.4 0.5 %collective-permute-start = (f32[88,128]{1,0:T(8,128)S(1)}, f32[88,128]{1,0:T(8,128)S(1)}, u32[]{:S(2)}, u32[]{:S(2)}) collective-permute-start(f32[88,128]{1,0:T(8,128)S(1)} %get-tuple-element.28), channel_id=1, source_target_pairs={{0,1},{1,0},{2,3},{3,2},{4,5},{5,4},{6,7},{7,6},{8,9},{9,8},{10,11... | collective-permute-start | bytes 135176 | tf_op jit(solution)/shard_map/ppermute | solution.py:734
  2.9 4.7 %collective-permute-start.1 = (f32[88,128]{1,0:T(8,128)S(1)}, f32[88,128]{1,0:T(8,128)S(1)}, u32[]{:S(2)}, u32[]{:S(2)}) collective-permute-start(f32[88,128]{1,0:T(8,128)S(1)} %get-tuple-element.29), channel_id=1, source_target_pairs={{0,7},{1,2},{2,1},{3,4},{4,3},{5,6},{6,5},{7,0},{8,15},{9,10},{10,... | collective-permute-start | bytes 135176 | tf_op jit(solution)/shard_map/ppermute | solution.py:735
  7.6 0.0 collective-permute-done.first
  7.6 1.8 %collective-permute-done.1.second = f32[88,128]{1,0:T(8,128)S(1)} collective-permute-done((f32[88,128]{1,0:T(8,128)S(1)}, f32[88,128]{1,0:T(8,128)S(1)}, u32[]{:S(2)}, u32[]{:S(2)}) %collective-permute-start.1) | collective-permute-done | bytes 45088 | tf_op jit(solution)/shard_map/ppermute | solution.py:735
  9.4 1.6 %shard_map.112 = (f32[144,128]{1,0:T(8,128)S(1)}, f32[24,128]{1,0:T(8,128)S(1)}, f32[144,128]{1,0:T(8,128)S(1)}, f32[48,128]{1,0:T(8,128)S(1)}, f32[128,128]{1,0:T(8,128)S(1)}, /*index=5*/f32[128,128]{1,0:T(8,128)S(1)}) custom-call(f32[2,8,8,128]{3,2,1,0:T(8,128)S(1)} %get-tuple-element.20.disp, f32[2,8,8,128]{3,2,1,0:T(8,128)S(1)} %get-tuple-element.21.vel, ...), custom_call_target="tpu_custom_call" | custom-call | tf_op jit(solution)/shard_map/pallas_call | solution.py:718
  11.0 1.6 %collective-permute-start.2 = (f32[144,128]{1,0:T(8,128)S(1)}, f32[144,128]{1,0:T(8,128)S(1)}, u32[]{:S(2)}, u32[]{:S(2)}) collective-permute-start(f32[144,128]{1,0:T(8,128)S(1)} %get-tuple-element.33), channel_id=1, source_target_pairs={{0,8},{8,0},{16,24},{24,16},{1,9},{9,1},{17,25},{25,17},{2,10},{10... | collective-permute-start | bytes 221192 | tf_op jit(solution)/shard_map/ppermute | solution.py:751
  12.6 1.5 %collective-permute-start.4 = (f32[144,128]{1,0:T(8,128)S(1)}, f32[144,128]{1,0:T(8,128)S(1)}, u32[]{:S(2)}, u32[]{:S(2)}) collective-permute-start(f32[144,128]{1,0:T(8,128)S(1)} %get-tuple-element.35), channel_id=1, source_target_pairs={{0,24},{8,16},{16,8},{24,0},{1,25},{9,17},{17,9},{25,1},{2,26},{10... | collective-permute-start | bytes 221192 | tf_op jit(solution)/shard_map/ppermute | solution.py:751
  14.1 0.5 %collective-permute-start.3 = (f32[24,128]{1,0:T(8,128)S(1)}, f32[24,128]{1,0:T(8,128)S(1)}, u32[]{:S(2)}, u32[]{:S(2)}) collective-permute-start(f32[24,128]{1,0:T(8,128)S(1)} %get-tuple-element.34), channel_id=1, source_target_pairs={{0,16},{8,24},{16,0},{24,8},{1,17},{9,25},{17,1},{25,9},{2,18},{10... | collective-permute-start | bytes 36872 | tf_op jit(solution)/shard_map/ppermute | solution.py:751
  14.6 3.4 %collective-permute-done.3.refs_1_ = f32[24,128]{1,0:T(8,128)S(1)} collective-permute-done((f32[24,128]{1,0:T(8,128)S(1)}, f32[24,128]{1,0:T(8,128)S(1)}, u32[]{:S(2)}, u32[]{:S(2)}) %collective-permute-start.3) | collective-permute-done | bytes 12320 | tf_op jit(solution)/shard_map/ppermute | solution.py:751
  18.0 0.0 collective-permute-done.2.refs_0_
  18.0 0.0 collective-permute-done.4.refs_2_
  18.0 11.1 %shard_map.113 = (f32[2,8,8,128]{3,2,1,0:T(8,128)}, f32[2,8,8,128]{3,2,1,0:T(8,128)}, f32[128,512]{1,0:T(8,128)}, f32[128,512]{1,0:T(8,128)}) custom-call(f32[2,8,8,128]{3,2,1,0:T(8,128)S(1)} %get-tuple-element.20.disp, f32[2,8,8,128]{3,2,1,0:T(8,128)S(1)} %get-tuple-element.21.vel, f32[2,8,8,128]{3,2,1,0:T(8,128)S(1)} %get-tuple-element.22.jit, ...), custom_call_target="tpu_custom_call" | custom-call | tf_op jit(solution)/shard_map/pallas_call | solution.py:718
Async XLA Ops:
  2.4 5.2 %collective-permute-start = (f32[88,128]{1,0:T(8,128)S(1)}, f32[88,128]{1,0:T(8,128)S(1)}, u32[]{:S(2)}, u32[]{:S(2)}) collective-permute-start(f32[88,128]{1,0:T(8,128)S(1)} %get-tuple-element.28), channel_id=1, source_target_pairs={{0,1},{1,0},{2,3},{3,2},{4,5},{5,4},{6,7},{7,6},{8,9},{9,8},{10,11... | collective-permute-start | bytes 135176 | tf_op jit(solution)/shard_map/ppermute | solution.py:734
  2.9 6.5 %collective-permute-start.1 = (f32[88,128]{1,0:T(8,128)S(1)}, f32[88,128]{1,0:T(8,128)S(1)}, u32[]{:S(2)}, u32[]{:S(2)}) collective-permute-start(f32[88,128]{1,0:T(8,128)S(1)} %get-tuple-element.29), channel_id=1, source_target_pairs={{0,7},{1,2},{2,1},{3,4},{4,3},{5,6},{6,5},{7,0},{8,15},{9,10},{10,... | collective-permute-start | bytes 135176 | tf_op jit(solution)/shard_map/ppermute | solution.py:735
  11.0 6.9 %collective-permute-start.2 = (f32[144,128]{1,0:T(8,128)S(1)}, f32[144,128]{1,0:T(8,128)S(1)}, u32[]{:S(2)}, u32[]{:S(2)}) collective-permute-start(f32[144,128]{1,0:T(8,128)S(1)} %get-tuple-element.33), channel_id=1, source_target_pairs={{0,8},{8,0},{16,24},{24,16},{1,9},{9,1},{17,25},{25,17},{2,10},{10... | collective-permute-start | bytes 221192 | tf_op jit(solution)/shard_map/ppermute | solution.py:751
  12.6 5.4 %collective-permute-start.4 = (f32[144,128]{1,0:T(8,128)S(1)}, f32[144,128]{1,0:T(8,128)S(1)}, u32[]{:S(2)}, u32[]{:S(2)}) collective-permute-start(f32[144,128]{1,0:T(8,128)S(1)} %get-tuple-element.35), channel_id=1, source_target_pairs={{0,24},{8,16},{16,8},{24,0},{1,25},{9,17},{17,9},{25,1},{2,26},{10... | collective-permute-start | bytes 221192 | tf_op jit(solution)/shard_map/ppermute | solution.py:751
  14.1 3.9 %collective-permute-start.3 = (f32[24,128]{1,0:T(8,128)S(1)}, f32[24,128]{1,0:T(8,128)S(1)}, u32[]{:S(2)}, u32[]{:S(2)}) collective-permute-start(f32[24,128]{1,0:T(8,128)S(1)} %get-tuple-element.34), channel_id=1, source_target_pairs={{0,16},{8,24},{16,0},{24,8},{1,17},{9,25},{17,1},{25,9},{2,18},{10... | collective-permute-start | bytes 36872 | tf_op jit(solution)/shard_map/ppermute | solution.py:751

commit v3 on v2

--- a/solution.py
+++ b/solution.py
@@ -136,24 +136,119 @@
     return fx, fy
 
 
-def second_forces(get_dx, get_dy, kept):
-    masks, _ = lane_masks()
-    dx0, dy0 = get_dx(0, 0), get_dy(0, 0)
+def pick_lanes(block, index):
+    return jnp.take_along_axis(block, index, axis=1, mode="promise_in_bounds")
+
+
+def flips(blocks):
+    lane, sub = lanes(), subs()
+    for level in (2, 1, 0):
+        step = 1 << level
+        stay = ((lane >> (level + 4)) ^ (sub >> level)) & 1 == 0
+        if step == 4:
+            others = [turn(pltpu.roll(block, 4, 0), 64) for block in blocks]
+        else:
+            low = (sub >> level) & 1 == 0
+            index = lane ^ (TILE_Y * step)
+            others = [jnp.where(low, pltpu.roll(block, 8 - step, 0), pltpu.roll(block, step, 0)) for block in blocks]
+            others = [pick_lanes(block, index) for block in others]
+        blocks = [jnp.where(stay, block, other) for block, other in zip(blocks, others)]
+    return blocks
+
+
+def flip(block):
+    return flips([block])[0]
+
+
+def side_columns(row):
+    return pick_lanes(jnp.broadcast_to(row, (8, PTS)), TILE_Y * subs() + (lanes() & (TILE_Y - 1)))
+
+
+def word_row(packed, s):
+    word = jnp.where(subs() == lanes() // TILE_Y, jnp.broadcast_to(packed[:, s : s + 1], (8, PTS)), 0)
+    for step in (4, 2, 1):
+        word = word | pltpu.roll(word, step, 0)
+    return word
+
+
+def sideways(cells, beside, oy):
+    if not oy:
+        return cells
+    lane = lanes()
+    mask = lane < oy if oy > 0 else lane >= PTS + oy
+    return turn(jnp.where(mask, beside, cells), -oy)
+
+
+FROM = 5
+
+
+def group_masks():
+    lane, sub = lanes(), subs()
+    row = (sub + FROM) & (TILE_X - 1)
+    col = lane & (TILE_Y - 1)
+    masks, bits = {}, {}
+    for o in (1, 2, 3):
+        masks["col", o] = col >= TILE_Y - o
+        masks["col", -o] = col < o
+        masks["row", o] = row >= TILE_X - o
+        masks["row", -o] = row < o
+    for ox in range(-3, 4):
+        bits[ox] = jnp.left_shift(jnp.int32(1), 4 * row + ((row + ox) & 7) // 2)
+    return masks, bits
+
+
+def group_first(cell, word, keep):
+    masks, bits = group_masks()
+    zero = [cell(f, 0, 0) for f in range(4)]
     fx = jnp.zeros((8, PTS), F32)
     fy = jnp.zeros((8, PTS), F32)
+    plain = [word(slot(dx, 0)) for dx in (-1, 0, 1)]
     for oy in SIDEWAYS:
-        dxs, dys = moved(get_dx, oy, masks), moved(get_dy, oy, masks)
+        words = plain
+        if oy:
+            words = [jnp.where(masks["col", oy], word(slot(dx, sign(oy))), plain[dx + 1]) for dx in (-1, 0, 1)]
+        base_y, base_v = zero[1] - float(oy), zero[3] - float(oy)
         for number, (ox, other) in enumerate(OFFSETS):
             if other != oy:
                 continue
-            now_x = across(dxs, ox, masks) - (dx0 - float(ox))
-            now_y = across(dys, ox, masks) - (dy0 - float(oy))
+            picked = words[1]
+            if ox:
+                picked = jnp.where(masks["row", ox], words[sign(ox) + 1], picked)
+            intact = (picked & bits[ox]) != 0
+            rest_x = cell(0, oy, ox) - (zero[0] - float(ox))
+            rest_y = cell(1, oy, ox) - base_y
+            now_x = cell(2, oy, ox) - (zero[2] - float(ox))
+            now_y = cell(3, oy, ox) - base_v
+            rest_sq = rest_x * rest_x + rest_y * rest_y + DELTA_SQ
             now_sq = now_x * now_x + now_y * now_y + DELTA_SQ
-            weight, level = kept(number)
+            rest_inv = lax.rsqrt(rest_sq)
+            reach = jnp.maximum(1.0 - rest_sq * rest_inv * (1.0 / HORIZON), 0.0)
+            weight = jnp.where(intact, reach * reach, 0.0)
+            level = weight * rest_inv
+            keep(number, weight, level)
             factor = level - weight * lax.rsqrt(now_sq)
             fx = fx + factor * now_x
             fy = fy + factor * now_y
     return fx, fy
+
+
+def group_second(cell, kept):
+    zero = [cell(f, 0, 0) for f in range(2)]
+    fx = jnp.zeros((8, PTS), F32)
+    fy = jnp.zeros((8, PTS), F32)
+    for number, (ox, oy) in enumerate(OFFSETS):
+        now_x = cell(0, oy, ox) - (zero[0] - float(ox))
+        now_y = cell(1, oy, ox) - (zero[1] - float(oy))
+        now_sq = now_x * now_x + now_y * now_y + DELTA_SQ
+        weight, level = kept(number)
+        factor = level - weight * lax.rsqrt(now_sq)
+        fx = fx + factor * now_x
+        fy = fy + factor * now_y
+    return fx, fy
+
+
+def joined(low_part, high_part):
+    return jnp.left_shift(high_part.astype(I32), 16) | low_part.astype(I32)
 
 
 def widen(row_of, count):
@@ -162,7 +257,7 @@
     out = []
     for j in range(count):
         left, right = (
-            jnp.take_along_axis(jnp.broadcast_to(row_of(b), (8, PTS)), index, axis=1) for b in (2 * j, 2 * j + 1)
+            pick_lanes(jnp.broadcast_to(row_of(b), (8, PTS)), index) for b in (2 * j, 2 * j + 1)
         )
         out.append(jnp.where(lane < 64, left, right))
     return out
@@ -175,7 +270,7 @@
         held = block_of(b // 2)
         held = held + turn(held, -1)
         held = held + turn(held, -2)
-        picked = jnp.take_along_axis(held, 64 * (b % 2) + SPLIT * (lane % TILE_Y), axis=1)
+        picked = pick_lanes(held, 64 * (b % 2) + SPLIT * (lane % TILE_Y))
         out.append(jnp.sum(jnp.where(sub == lane // TILE_Y, picked, 0.0), axis=0, keepdims=True))
     return out
 
@@ -438,13 +533,113 @@
         out[at : at + CONTACT_ROWS, :] = mine
 
 
-def both_steps(
-    place_args, shifts, disp, vel, jit, words, node, inter, shell, speed, first, second, own, strip_d, strip_v, *refs
-):
+def inner_rows(place_args, disp, vel, jit, words, first, second, *refs):
     place = Place(*place_args)
-    ends = refs[: len(shifts)]
-    out_disp, out_vel, out_shell, out_speed = refs[len(shifts) : len(shifts) + 4]
-    grid, near, vels, kinds, weights, levels, tall, tall_v, bent, pushed, gaps, trial, halo = refs[len(shifts) + 4 :]
+    win, weights, levels, flat, lead, beside, tiles_f, ends_w, strips, kinds, groups_w = refs
+    rows_a, tiles = disp.shape[1], disp.shape[2]
+    right, left = place.sides(first[...], second[...])
+    lane, sub = lanes(), subs()
+    west, east = place.gy == 0, place.gy == place.ny - 1
+    north, south = place.gx == 0, place.gx == place.nx - 1
+    leftward = (lane & (TILE_Y - 1)) >= TILE_Y // 2
+    side = [jnp.where(leftward, left[8 * f : 8 * f + 8], right[8 * f : 8 * f + 8]) for f in range(6)]
+
+    strips[...] = jnp.zeros_like(strips)
+    for f in range(4):
+        rest = jit[f % 2]
+        whole = rest if f < 2 else rest + disp[f % 2]
+        cols = side[4 + f % 2] if f < 2 else side[4 + f % 2] + side[f % 2]
+        strips[f, 0, 8:16, :] = cols
+        strips[f, 1, 8:16, :] = whole[:, 0, :]
+        strips[f, 2, 8:16, :] = whole[:, tiles - 1, :]
+        turned = flips([whole[a] for a in range(rows_a)])
+        nears = [side_columns(cols[a : a + 1]) for a in range(rows_a)]
+        for a, cells, near in zip(range(rows_a), turned, nears):
+            for n, oy in enumerate(SIDEWAYS):
+                shifted = sideways(cells, near, oy)
+                if a < rows_a - 1:
+                    win[f, n, a, 0:8, :] = shifted
+                if a > 0:
+                    win[f, n, a - 1, 8:16, :] = shifted
+    for f in range(2):
+        for a, cells in enumerate(flips([jit[f, a] + disp[f, a] + STEP_DT * vel[f, a] for a in range(rows_a)])):
+            lead[f, a] = cells
+
+    before = [None] * 9
+    for a in range(rows_a):
+        packed = words[a]
+        for dx in (-1, 0, 1):
+            for dy in (-1, 0, 1):
+                s = slot(dx, dy)
+                word = word_row(packed, s)
+                if dy < 0:
+                    word = jnp.where((lane < TILE_Y) & west, 0, word)
+                if dy > 0:
+                    word = jnp.where((lane >= PTS - TILE_Y) & east, 0, word)
+                if dx < 0 and a == 0:
+                    word = jnp.where(north, 0, word)
+                if dx > 0 and a == rows_a - 1:
+                    word = jnp.where(south, 0, word)
+                if a:
+                    groups_w[s, a - 1] = jnp.where(sub < TILE_X - FROM, before[s], word)
+                if a in (0, rows_a - 1):
+                    ends_w[s, min(a, 1)] = word
+                before[s] = word
+    left_words = joined(left[48:56], left[56:64])
+    right_words = joined(right[48:56], right[56:64])
+    for s in range(9):
+        kinds[s] = jnp.where(
+            leftward,
+            jnp.broadcast_to(left_words[:, s : s + 1], (8, PTS)),
+            jnp.broadcast_to(right_words[:, s : s + 1], (8, PTS)),
+        )
+
+    flat[...] = jnp.zeros_like(flat)
+
+    @pl.loop(0, rows_a - 1)
+    def _(k):
+        def cell(f, oy, ox):
+            return win[f, SIDEWAYS.index(oy), k, FROM + ox : FROM + ox + 8, :]
+
+        def keep(number, weight, level):
+            weights[number, k] = weight
+            levels[number, k] = level
+
+        fx, fy = group_first(cell, lambda s: groups_w[s, k], keep)
+        at = pl.multiple_of(8 * k + 16, 8)
+        flat[0, pl.ds(at, 8), :] = fx
+        flat[1, pl.ds(at, 8), :] = fy
+
+    def getter(f):
+        held = {}
+
+        def get(dx, dy):
+            if (dx, dy) not in held:
+                held[dx, dy] = turn(strips[f, dy % 3, 8 + dx : 16 + dx, :], TILE_Y * dy)
+            return held[dx, dy]
+
+        return get
+
+    forces = first_forces(getter(0), getter(1), getter(2), getter(3), lambda dx, dy: kinds[slot(dx, dy)])
+    for f in range(2):
+        moved_side = side[4 + f] + side[f] + STEP_DT * (side[2 + f] + STEP_DT * forces[f])
+        for a in range(rows_a):
+            beside[f, a] = side_columns(moved_side[a : a + 1])
+        for a, cells in enumerate(flips([flat[f, 8 * a + 11 : 8 * a + 19, :] for a in range(1, rows_a - 1)])):
+            tiles_f[f, a + 1] = cells
+        tiles_f[f, 0] = jnp.zeros((8, PTS), F32)
+        tiles_f[f, rows_a - 1] = jnp.zeros((8, PTS), F32)
+
+
+def both_steps(place_args, shifts, *refs):
+    place = Place(*place_args)
+    disp, vel, jit, words, node, inter, shell, speed, first, second, own, strip_d, strip_v = refs[:13]
+    win, weights, levels, flat_in, lead, beside, tiles_f, ends_w = refs[13:21]
+    ends = refs[21 : 21 + len(shifts)]
+    out_disp, out_vel, out_shell, out_speed = refs[21 + len(shifts) : 25 + len(shifts)]
+    tall, tall_v, bent, pushed, gaps, halo, ewin, ewords, eweights, elevels, flat, flat2, corners, kinds, swin = refs[
+        25 + len(shifts) :
+    ]
     rows_a, tiles = disp.shape[1], disp.shape[2]
     rows, cols = place.shell_rows, place.shell_cols
     right, left = place.sides(first[...], second[...])
@@ -529,179 +724,198 @@
         out_speed[row : row + 8, :] = fast
         out_shell[row : row + 8, :] = here + STEP_DT * fast
 
-    grid[...] = jnp.zeros_like(grid)
-    top, low = STRIDE, (rows_a + 2) * STRIDE
-    for f in range(4):
-        source, at = ((jit, 32 + 8 * f), (disp, 8 * (f - 2)))[f >= 2]
-        extra = 32 + 8 * (f - 2)
-
-        def with_rest(values, rest):
-            return values + rest if f >= 2 else values
-
-        for a in range(rows_a):
-            base = (a + 2) * STRIDE + 8
-            grid[f, base : base + tiles, :] = with_rest(source[f % 2, a], jit[f % 2, a])
-        for side, offset in ((right, 16), (left, 7)):
-            grid[f, pl.ds(2 * STRIDE + offset, rows_a, stride=STRIDE), :] = with_rest(
-                side[at : at + 8], side[extra : extra + 8]
-            )
-        for end, base in ((0, top), (1, low)):
-            grid[f, base + 8 : base + 16, :] = with_rest(halo[end, at : at + 8, :], halo[end, extra : extra + 8, :])
-            for part, offset in ((64, 16), (72, 7)):
-                grid[f, base + offset : base + offset + 1, :] = with_rest(
-                    halo[end, part + at // 8 : part + at // 8 + 1, :],
-                    halo[end, part + extra // 8 : part + extra // 8 + 1, :],
-                )
-
-    blocks = rows_a + 5
-    corner = 8 * (rows_a + 4)
-
-    def spread_grid(f, row_blocks, edges):
+    lane, sub = lanes(), subs()
+    west, east = place.gy == 0, place.gy == place.ny - 1
+    north, south = place.gx == 0, place.gx == place.nx - 1
+    leftward = (lane & (TILE_Y - 1)) >= TILE_Y // 2
+    topmost = lane >= PTS // 2
+    last = rows_a - 1
+
+    def side_row(end, part):
+        return jnp.where(leftward[0:1], halo[end, 72 + part : 73 + part, :], halo[end, 64 + part : 65 + part, :])
+
+    sides = {(end, part): side_row(end, part) for end in (0, 1) for part in range(6)}
+    far_lead = {}
+    for end in (0, 1):
+        for f in range(2):
+            rest = halo[end, 32 + 8 * f : 40 + 8 * f, :]
+            whole = rest + halo[end, 8 * f : 8 * f + 8, :]
+            far_lead[f, end] = flip(whole + STEP_DT * halo[end, 16 + 8 * f : 24 + 8 * f, :])
+            for field, cells, row in (
+                (f, rest, sides[end, 4 + f]),
+                (2 + f, whole, sides[end, 4 + f] + sides[end, f]),
+            ):
+                cells = flip(cells)
+                near = side_columns(row)
+                for n, oy in enumerate(SIDEWAYS):
+                    shifted = sideways(cells, near, oy)
+                    if end == 0:
+                        ewin[field, n, 0, 0:8, :] = shifted
+                        ewin[field, n, 0, 8:16, :] = win[field, n, 0, 0:8, :]
+                    else:
+                        ewin[field, n, 1, 0:8, :] = win[field, n, rows_a - 2, 8:16, :]
+                        ewin[field, n, 1, 8:16, :] = shifted
+        packed = joined(halo[end, 48:56, :], halo[end, 56:64, :])
         for dx in (-1, 0, 1):
             for dy in (-1, 0, 1):
                 s = slot(dx, dy)
-                for t in row_blocks:
-                    a = t if t < rows_a else (-1, rows_a)[t - rows_a]
-                    base = (a + 2 + dx) * STRIDE + 8 + dy
-                    near[f, s, 8 * t : 8 * t + 8, :] = turn(grid[f, base : base + 8, :], TILE_Y * dy)
-                if edges:
-                    for t, offset in ((rows_a + 2, 7), (rows_a + 3, 16)):
-                        near[f, s, 8 * t : 8 * t + 8, :] = turn(
-                            grid[f, pl.ds((2 + dx) * STRIDE + offset + dy, 8, stride=STRIDE), :], TILE_Y * dy
-                        )
-                    near[f, s, corner : corner + 8, :] = jnp.zeros((8, PTS), F32)
-                    for n, offset in enumerate((7, 16)):
-                        for m, base in enumerate((top, low)):
-                            start = base + dx * STRIDE + offset + dy
-                            at = corner + 2 * n + m
-                            near[f, s, at : at + 1, :] = turn(grid[f, start : start + 1, :], TILE_Y * dy)
-
+                word = word_row(packed, s)
+                if dy < 0:
+                    word = jnp.where((lane < TILE_Y) & west, 0, word)
+                if dy > 0:
+                    word = jnp.where((lane >= PTS - TILE_Y) & east, 0, word)
+                pair = (word, ends_w[s, 0]) if end == 0 else (ends_w[s, 1], word)
+                ewords[s, end] = jnp.where(sub < TILE_X - FROM, *pair)
+
+    flat[...] = flat_in[...]
+
+    @pl.loop(0, 2)
+    def _(e):
+        def cell(f, oy, ox):
+            return ewin[f, SIDEWAYS.index(oy), e, FROM + ox : FROM + ox + 8, :]
+
+        def keep(number, weight, level):
+            eweights[number, e] = weight
+            elevels[number, e] = level
+
+        fx, fy = group_first(cell, lambda s: ewords[s, e], keep)
+        at = pl.multiple_of(8 + 8 * rows_a * e, 8)
+        flat[0, pl.ds(at, 8), :] = fx
+        flat[1, pl.ds(at, 8), :] = fy
+
+    corners[...] = jnp.zeros_like(corners)
     for f in range(4):
-        spread_grid(f, range(rows_a + 2), True)
-
-    for f in range(2):
-        at = 16 + 8 * f
-        for a in range(rows_a):
-            vels[f, 8 * a : 8 * a + 8, :] = vel[f, a]
-        for end in (0, 1):
-            t = rows_a + end
-            vels[f, 8 * t : 8 * t + 8, :] = halo[end, at : at + 8, :]
-        vels[f, corner - 16 : corner - 8, :] = left[at : at + 8]
-        vels[f, corner - 8 : corner, :] = right[at : at + 8]
-        vels[f, corner : corner + 8, :] = jnp.zeros((8, PTS), F32)
-        for n, part in enumerate((72, 64)):
-            for end in (0, 1):
-                vels[f, corner + 2 * n + end : corner + 2 * n + end + 1, :] = halo[
-                    end, part + 2 + f : part + 3 + f, :
-                ]
-
-    def joined(low_part, high_part):
-        return jnp.left_shift(high_part.astype(I32), 16) | low_part.astype(I32)
-
-    sub = subs()
-    west, east = place.gy == 0, place.gy == place.ny - 1
-    north, south = place.gx == 0, place.gx == place.nx - 1
-    for t in range(blocks):
-        if t < rows_a:
-            packed = words[t]
-        elif t < rows_a + 2:
-            packed = joined(halo[t - rows_a, 48:56, :], halo[t - rows_a, 56:64, :])
-        elif t < rows_a + 4:
-            side = (left, right)[t - rows_a - 2]
-            packed = joined(side[48:56], side[56:64])
-        else:
-            zero = jnp.zeros((4, PTS), F32)
-            lows = [halo[end, part + 6 : part + 7, :] for part in (72, 64) for end in (0, 1)]
-            highs = [halo[end, part + 7 : part + 8, :] for part in (72, 64) for end in (0, 1)]
-            packed = joined(jnp.concatenate(lows + [zero], axis=0), jnp.concatenate(highs + [zero], axis=0))
-        for dx in (-1, 0, 1):
-            for dy in (-1, 0, 1):
+
+        def strip(a, dy, f=f):
+            if dy == 0:
+                if 0 <= a < rows_a:
+                    at = 32 + 8 * (f % 2) + a
+                    row = jnp.where(leftward[0:1], left[at : at + 1], right[at : at + 1])
+                    if f >= 2:
+                        at = 8 * (f % 2) + a
+                        row = row + jnp.where(leftward[0:1], left[at : at + 1], right[at : at + 1])
+                    return row
+                end = 0 if a < 0 else 1
+                return sides[end, 4 + f % 2] + (sides[end, f % 2] if f >= 2 else 0.0)
+            b = 0 if dy > 0 else tiles - 1
+            if 0 <= a < rows_a:
+                row = jit[f % 2, a, b : b + 1, :]
+                return row + disp[f % 2, a, b : b + 1, :] if f >= 2 else row
+            end = 0 if a < 0 else 1
+            at = 32 + 8 * (f % 2) + b
+            row = halo[end, at : at + 1, :]
+            at = 8 * (f % 2) + b
+            return row + halo[end, at : at + 1, :] if f >= 2 else row
+
+        for dy in (-1, 0, 1):
+            for dx in (-1, 0, 1):
                 s = slot(dx, dy)
-                word = jnp.broadcast_to(packed[:, s : s + 1], (8, PTS))
-                if t < rows_a + 2:
-                    if dy < 0:
-                        word = jnp.where((sub == 0) & west, 0, word)
-                    if dy > 0:
-                        word = jnp.where((sub == tiles - 1) & east, 0, word)
-                    if dx < 0 and t == 0:
-                        word = jnp.where(north, 0, word)
-                    if dx > 0 and t == rows_a - 1:
-                        word = jnp.where(south, 0, word)
-                elif t < rows_a + 4:
-                    if dx < 0:
-                        word = jnp.where((sub == 0) & north, 0, word)
-                    if dx > 0:
-                        word = jnp.where((sub == rows_a - 1) & south, 0, word)
-                kinds[s, 8 * t : 8 * t + 8, :] = word
-
-    def getter(ref, f, at):
+                corners[f, s, 0:1, :] = strip(dx, dy)
+                corners[f, s, 1:2, :] = strip(last + dx, dy)
+                if dx == 0:
+                    corners[f, s, 2:3, :] = jnp.where(topmost[0:1], strip(-1, dy), strip(rows_a, dy))
+                else:
+                    corners[f, s, 2:3, :] = strip(0 if dx > 0 else last, dy)
+    quarters = {}
+    filler = jnp.zeros((5, PTS), F32)
+    for end in (0, 1):
+        for values, part in ((left, 72), (right, 64)):
+            low = [values[48:49], values[48 + last : 49 + last], halo[end, part + 6 : part + 7, :], filler]
+            high = [values[56:57], values[56 + last : 57 + last], halo[end, part + 7 : part + 8, :], filler]
+            quarters[end, part] = joined(jnp.concatenate(low, axis=0), jnp.concatenate(high, axis=0))
+    for dx in (-1, 0, 1):
+        for dy in (-1, 0, 1):
+            s = slot(dx, dy)
+            upper, lower = (
+                jnp.where(
+                    leftward,
+                    jnp.broadcast_to(quarters[end, 72][:, s : s + 1], (8, PTS)),
+                    jnp.broadcast_to(quarters[end, 64][:, s : s + 1], (8, PTS)),
+                )
+                for end in (0, 1)
+            )
+            word = jnp.where(topmost, upper, lower)
+            if dx < 0:
+                word = jnp.where((sub == 0) & north, 0, word)
+            if dx > 0:
+                word = jnp.where((sub == 1) & south, 0, word)
+            kinds[s] = word
+
+    def getter(f):
         held = {}
 
         def get(dx, dy):
             if (dx, dy) not in held:
-                cut = (slot(dx, dy), pl.ds(at, 8), slice(None))
-                held[dx, dy] = ref[cut] if f is None else ref[(f,) + cut]
+                held[dx, dy] = turn(corners[f, slot(dx, dy)], TILE_Y * dy)
             return held[dx, dy]
 
         return get
 
-    @pl.loop(0, blocks)
-    def _(t):
-        at = pl.multiple_of(8 * t, 8)
-
-        def keep(number, weight, level):
-            weights[number, pl.ds(at, 8), :] = weight
-            levels[number, pl.ds(at, 8), :] = level
-
-        fx, fy = first_forces(
-            getter(near, 0, at),
-            getter(near, 1, at),
-            getter(near, 2, at),
-            getter(near, 3, at),
-            getter(kinds, None, at),
-            keep,
-        )
-        trial[0, pl.ds(at, 8), :] = fx
-        trial[1, pl.ds(at, 8), :] = fy
+    side_f = first_forces(getter(0), getter(1), getter(2), getter(3), lambda dx, dy: kinds[slot(dx, dy)])
 
     here = jnp.where(place.front, 1.0, 0.0)
     push = PENALTY * here * jnp.maximum(contact[8:18] - owners[8:18], 0.0)
-    last = rows_a - 1
-    trial[0, 8 * last : 8 * last + 8, :] -= push[0:8]
-    at = 8 * (rows_a + 2) + last
-    trial[0, at : at + 1, :] -= push[9:10]
-    trial[0, at + 8 : at + 9, :] -= push[8:9]
+    side_push = jnp.where(leftward[0:1], push[9:10], push[8:9])
+    push = push[0:8]
+
     for f in range(2):
-        vels[f] = vels[f] + STEP_DT * trial[f]
-        trial[f] = near[2 + f, slot(0, 0)] + STEP_DT * vels[f]
-        for t in range(rows_a + 2):
-            a = t if t < rows_a else (-1, rows_a)[t - rows_a]
-            grid[2 + f, (a + 2) * STRIDE + 8 : (a + 2) * STRIDE + 16, :] = trial[f, 8 * t : 8 * t + 8, :]
-        for t, offset in ((rows_a + 2, 7), (rows_a + 3, 16)):
-            grid[2 + f, pl.ds(2 * STRIDE + offset, 8, stride=STRIDE), :] = trial[f, 8 * t : 8 * t + 8, :]
-        for n, offset in enumerate((7, 16)):
-            for m, base in enumerate((top, low)):
-                at = corner + 2 * n + m
-                grid[2 + f, base + offset : base + offset + 1, :] = trial[f, at : at + 1, :]
-        spread_grid(2 + f, range(rows_a), False)
-
-    @pl.loop(0, rows_a)
-    def _(t):
-        at = pl.multiple_of(8 * t, 8)
-
-        def kept(number):
-            return weights[number, pl.ds(at, 8), :], levels[number, pl.ds(at, 8), :]
-
-        fx, fy = second_forces(getter(near, 2, at), getter(near, 3, at), kept)
-        out_vel[0, t] = vels[0, pl.ds(at, 8), :] + STEP_DT * fx
-        out_vel[1, t] = vels[1, pl.ds(at, 8), :] + STEP_DT * fy
-
-    gap = trial[0, 8 * last : 8 * last + 8, :] - jit[0, last] + inter[...]
-    reached = owners[0:8] + (STEP_DT * STEP_DT) * push[0:8]
-    out_vel[0, last] = out_vel[0, last] - (STEP_DT * PENALTY) * here * jnp.maximum(gap - reached, 0.0)
+        ends_beside = {}
+        speeds = [jnp.where(leftward[0:1], left[16 + 8 * f + a : 17 + 8 * f + a], right[16 + 8 * f + a : 17 + 8 * f + a]) for a in (0, last)]
+        speeds.append(jnp.where(topmost[0:1], sides[0, 2 + f], sides[1, 2 + f]))
+        for n in range(3):
+            force = side_f[f][n : n + 1]
+            if n == 1 and f == 0:
+                force = force - side_push
+            row = corners[2 + f, slot(0, 0), n : n + 1, :] + STEP_DT * (speeds[n] + STEP_DT * force)
+            ends_beside[n] = side_columns(row)
+        for a in range(-1, rows_a + 1):
+            if a in (-1, rows_a):
+                cells, near = far_lead[f, 0 if a < 0 else 1], ends_beside[2]
+            else:
+                cells = lead[f, a]
+                near = ends_beside[0] if a == 0 else ends_beside[1] if a == last else beside[f, a]
+            cells = cells + (STEP_DT * STEP_DT) * flat[f, 8 * a + 11 : 8 * a + 19, :]
+            if a == last and f == 0:
+                cells = cells - (STEP_DT * STEP_DT) * flip(push)
+            for n, oy in enumerate(SIDEWAYS):
+                shifted = sideways(cells, near, oy)
+                if a < rows_a:
+                    swin[f, n, a + 1, 0:8, :] = shifted
+                if a >= 0:
+                    swin[f, n, a, 8:16, :] = shifted
+
+    def second_group(k, kept):
+        def cell(f, oy, ox):
+            return swin[f, SIDEWAYS.index(oy), k, FROM + ox : FROM + ox + 8, :]
+
+        fx, fy = group_second(cell, kept)
+        at = pl.multiple_of(8 * k + 8, 8)
+        flat2[0, pl.ds(at, 8), :] = fx
+        flat2[1, pl.ds(at, 8), :] = fy
+
+    @pl.loop(0, 2)
+    def _(e):
+        second_group(e * rows_a, lambda number: (eweights[number, e], elevels[number, e]))
+
+    @pl.loop(0, rows_a - 1)
+    def _(k):
+        second_group(k + 1, lambda number: (weights[number, k], levels[number, k]))
+
     for f in range(2):
+        thens = flips([flat2[f, 8 * a + 11 : 8 * a + 19, :] for a in range(rows_a)])
+        end_was = flips([flat[f, 8 * a + 11 : 8 * a + 19, :] for a in (0, last)])
         for a in range(rows_a):
-            out_disp[f, a] = (trial[f, 8 * a : 8 * a + 8, :] - jit[f, a]) + STEP_DT * out_vel[f, a]
+            was = end_was[min(a, 1)] if a in (0, last) else tiles_f[f, a]
+            then = thens[a]
+            if f == 0 and a == last:
+                was = was - push
+                gap = disp[0, last] + STEP_DT * (vel[0, last] + STEP_DT * was) + inter[...]
+                reached = owners[0:8] + (STEP_DT * STEP_DT) * push
+                then = then - PENALTY * here * jnp.maximum(gap - reached, 0.0)
+            fast = vel[f, a] + STEP_DT * was
+            faster = fast + STEP_DT * then
+            out_vel[f, a] = faster
+            out_disp[f, a] = disp[f, a] + STEP_DT * (fast + faster)
 
 
 def on_device(nx, ny, disp, vel, jit, words, node, inter, shell, speed):
@@ -720,7 +934,7 @@
             out_shape=out,
             in_specs=specs,
             scratch_shapes=scratch,
-            compiler_params=pltpu.CompilerParams(vmem_limit_bytes=40 * 1024 * 1024),
+            compiler_params=pltpu.CompilerParams(vmem_limit_bytes=20 * 1024 * 1024),
         )(*args)
 
     side = jax.ShapeDtypeStruct((Y_ROWS, PTS), F32)
@@ -732,7 +946,7 @@
         far=len(base),
     )
     first = lax.ppermute(first, "gy", [(i, i ^ 1) for i in range(ny)])
-    second = lax.ppermute(second, "gy", [(i, ((i - 1) ^ 1) + 1 if 0 < i < ny - 1 else ny - 1 - i) for i in range(ny)])
+    second = lax.ppermute(second, "gy", [(i, ((i - 1) ^ 1) + 1) for i in range(1, ny - 1)])
 
     tall = pltpu.VMEM((rows + 2 * PAD, WIDE), F32)
     outs = [
@@ -750,25 +964,61 @@
     )
     ends = [lax.ppermute(e, "gx", [(i, i ^ s) for i in range(nx)]) for s, e in zip(shifts, ends)]
 
-    held = 8 * (rows_a + 5)
+    span, count = rows_a - 1, len(OFFSETS)
+
+    def shaped(*shape, dtype=F32):
+        return jax.ShapeDtypeStruct(shape + (PTS,), dtype)
+
+    inner = call(
+        functools.partial(inner_rows, place_args),
+        [
+            shaped(4, len(SIDEWAYS), span, 16),
+            shaped(count, span, 8),
+            shaped(count, span, 8),
+            shaped(2, 8 * (rows_a + 3)),
+            shaped(2, rows_a, 8),
+            shaped(2, rows_a, 8),
+            shaped(2, rows_a, 8),
+            shaped(9, 2, 8, dtype=I32),
+        ],
+        [pltpu.VMEM((4, 3, 24, PTS), F32), pltpu.VMEM((9, 8, PTS), I32), pltpu.VMEM((9, span, 8, PTS), I32)],
+        *base[:4],
+        first,
+        second,
+    )
+
     scratch = [
-        pltpu.VMEM((4, (rows_a + 4) * STRIDE, PTS), F32),
-        pltpu.VMEM((4, 9, held, PTS), F32),
-        pltpu.VMEM((2, held, PTS), F32),
-        pltpu.VMEM((9, held, PTS), I32),
-        pltpu.VMEM((len(OFFSETS), held, PTS), F32),
-        pltpu.VMEM((len(OFFSETS), held, PTS), F32),
         tall,
         tall,
         tall,
         tall,
         pltpu.VMEM((3, TILE_X, 8, WIDE), F32),
-        pltpu.VMEM((2, held, PTS), F32),
         pltpu.VMEM((2, HALO_ROWS, PTS), F32),
+        pltpu.VMEM((4, len(SIDEWAYS), 2, 16, PTS), F32),
+        pltpu.VMEM((9, 2, 8, PTS), I32),
+        pltpu.VMEM((count, 2, 8, PTS), F32),
+        pltpu.VMEM((count, 2, 8, PTS), F32),
+        pltpu.VMEM((2, 8 * (rows_a + 3), PTS), F32),
+        pltpu.VMEM((2, 8 * (rows_a + 3), PTS), F32),
+        pltpu.VMEM((4, 9, 8, PTS), F32),
+        pltpu.VMEM((9, 8, PTS), I32),
+        pltpu.VMEM((2, len(SIDEWAYS), rows_a + 1, 16, PTS), F32),
     ]
     out = [jax.ShapeDtypeStruct(x.shape, F32) for x in (disp, vel, shell, speed)]
     return tuple(
-        call(functools.partial(both_steps, place_args, shifts), out, scratch, *base, first, second, own, strip_d, strip_v, *ends)
+        call(
+            functools.partial(both_steps, place_args, shifts),
+            out,
+            scratch,
+            *base,
+            first,
+            second,
+            own,
+            strip_d,
+            strip_v,
+            *inner,
+            *ends,
+        )
     )
 
 

time: 29.2 us -> 23.1 us (0.79)
  the two profiles are of different devices: /device:TPU:0 before, /device:TPU:1 now
where the time goes in v3:
time: 23.1 us; the launch traced here: 22.9 us
  Pallas kernels  12.8 us (55%)
  starting transfers between devices  7.74 us (34%)
  waiting for transfers between devices  1.72 us (7%)
  between operations  0.69 us (3%)
    pallas_call x4, Pallas kernels, call(): pl.pallas_call(body, out_shape=out, in_specs=specs, scratch_shapes=scratc...  12.8 us
    ppermute x1, starting transfers between devices, on_device(): lax.ppermute(second, 'gy', [(i, (i - 1 ^ 1) + 1) for i in range(1, ny - 1)])  4.55 us
    ppermute x3, starting transfers between devices, on_device(): lax.ppermute(e, 'gx', [(i, i ^ s) for i in range(nx)])  3.06 us
    ppermute x1, waiting for transfers between devices, on_device(): lax.ppermute(second, 'gy', [(i, (i - 1 ^ 1) + 1) for i in range(1, ny - 1)])  1.7 us
  transfers between devices with their start and end apart: 5, of which 1 were waited for; matrix products, arithmetic and copies ran while one was open for 0% of the time, Pallas kernels for 16%

profile of v3, /device:TPU:1, one launch (start us, length us, event | category | flops | bytes accessed | tf_op | source)
XLA Modules:
  0.0 22.9 jit_solution(3511210584491994970)
XLA Ops:
  0.6 1.7 %shard_map.111 = (f32[88,128]{1,0:T(8,128)S(1)}, f32[88,128]{1,0:T(8,128)S(1)}, f32[2,8,8,128]{3,2,1,0:T(8,128)S(1)}, f32[2,8,8,128]{3,2,1,0:T(8,128)S(1)}, f32[...) custom-call(f32[2,8,8,128]{3,2,1,0:T(8,128)} %refs_0_.1, ...), custom_call_target="tpu_custom_call" | custom-call | tf_op jit(solution)/shard_map/pallas_call | solution.py:932
  2.4 0.1 collective-permute-start
  2.5 4.6 %collective-permute-start.1 = (f32[88,128]{1,0:T(8,128)S(1)}, f32[88,128]{1,0:T(8,128)S(1)}, u32[]{:S(2)}, u32[]{:S(2)}) collective-permute-start(f32[88,128]{1,0:T(8,128)S(1)} %get-tuple-element.37), channel_id=1, source_target_pairs={{1,2},{2,1},{3,4},{4,3},{5,6},{6,5},{9,10},{10,9},{11,12},{12,11},... | collective-permute-start | bytes 135176 | tf_op jit(solution)/shard_map/ppermute | solution.py:949
  7.0 0.0 collective-permute-done.first.refs_8_
  7.1 1.7 %collective-permute-done.1.second.refs_9_ = f32[88,128]{1,0:T(8,128)S(1)} collective-permute-done((f32[88,128]{1,0:T(8,128)S(1)}, f32[88,128]{1,0:T(8,128)S(1)}, u32[]{:S(2)}, u32[]{:S(2)}) %collective-permute-start.1) | collective-permute-done | bytes 45088 | tf_op jit(solution)/shard_map/ppermute | solution.py:949
  8.8 1.6 %shard_map.112 = (f32[144,128]{1,0:T(8,128)S(1)}, f32[24,128]{1,0:T(8,128)S(1)}, f32[144,128]{1,0:T(8,128)S(1)}, f32[48,128]{1,0:T(8,128)S(1)}, f32[128,128]{1,0:T(8,128)S(1)}, /*index=5*/f32[128,128]{1,0:T(8,128)S(1)}) custom-call(f32[2,8,8,128]{3,2,1,0:T(8,128)S(1)} %get-tuple-element.28.disp.refs_0_, f32[2,8,8,128]{3,2,1,0:T(8,128)S(1)} %get-tuple-element.29.vel.refs_1_, ...), custom_call_target="tpu_custom_call" | custom-call | tf_op jit(solution)/shard_map/pallas_call | solution.py:932
  10.4 1.8 %collective-permute-start.2 = (f32[144,128]{1,0:T(8,128)S(1)}, f32[144,128]{1,0:T(8,128)S(1)}, u32[]{:S(2)}, u32[]{:S(2)}) collective-permute-start(f32[144,128]{1,0:T(8,128)S(1)} %get-tuple-element.49), channel_id=1, source_target_pairs={{0,8},{8,0},{16,24},{24,16},{1,9},{9,1},{17,25},{25,17},{2,10},{10... | collective-permute-start | bytes 221192 | tf_op jit(solution)/shard_map/ppermute | solution.py:965
  12.2 1.2 %collective-permute-start.4 = (f32[144,128]{1,0:T(8,128)S(1)}, f32[144,128]{1,0:T(8,128)S(1)}, u32[]{:S(2)}, u32[]{:S(2)}) collective-permute-start(f32[144,128]{1,0:T(8,128)S(1)} %get-tuple-element.51), channel_id=1, source_target_pairs={{0,24},{8,16},{16,8},{24,0},{1,25},{9,17},{17,9},{25,1},{2,26},{10... | collective-permute-start | bytes 221192 | tf_op jit(solution)/shard_map/ppermute | solution.py:965
  13.4 0.1 collective-permute-start.3
  13.4 3.6 %shard_map.113 = (f32[4,7,7,16,128]{4,3,2,1,0:T(8,128)S(1)}, f32[44,7,8,128]{3,2,1,0:T(8,128)S(1)}, f32[44,7,8,128]{3,2,1,0:T(8,128)S(1)}, f32[2,88,128]{2,1,0:T...) custom-call(f32[2,8,8,128]{3,2,1,0:T(8,128)S(1)} %get-tuple-element., ...), custom_call_target="tpu_custom_call" | custom-call | tf_op jit(solution)/shard_map/pallas_call | solution.py:932
  17.0 0.0 collective-permute-done.3.refs_22_
  17.0 0.0 collective-permute-done.2.refs_21_
  17.0 0.0 collective-permute-done.4.refs_23_
  17.0 5.9 %shard_map.114 = (f32[2,8,8,128]{3,2,1,0:T(8,128)}, f32[2,8,8,128]{3,2,1,0:T(8,128)}, f32[128,512]{1,0:T(8,128)}, f32[128,512]{1,0:T(8,128)}) custom-call(f32[2,8,8,128]{3,2,1,0:T(8,128)S(1)} %get-tuple-element.28.disp.refs_0_, f32[2,8,8,128]{3,2,1,0:T(8,128)S(1)} %get-tuple-element.29.vel.refs_1_, f32[2,8,8,128]{3,2,1,0:T(8,128)S(1)} %get-tuple-element.30.jit.refs_2_, ...), custom_call_target="tpu_custom_call" | custom-call | tf_op jit(solution)/shard_map/pallas_call | solution.py:932
Async XLA Ops:
  2.4 4.7 %collective-permute-start = (f32[88,128]{1,0:T(8,128)S(1)}, f32[88,128]{1,0:T(8,128)S(1)}, u32[]{:S(2)}, u32[]{:S(2)}) collective-permute-start(f32[88,128]{1,0:T(8,128)S(1)} %get-tuple-element.36), channel_id=1, source_target_pairs={{0,1},{1,0},{2,3},{3,2},{4,5},{5,4},{6,7},{7,6},{8,9},{9,8},{10,11... | collective-permute-start | bytes 135176 | tf_op jit(solution)/shard_map/ppermute | solution.py:948
  2.5 6.3 %collective-permute-start.1 = (f32[88,128]{1,0:T(8,128)S(1)}, f32[88,128]{1,0:T(8,128)S(1)}, u32[]{:S(2)}, u32[]{:S(2)}) collective-permute-start(f32[88,128]{1,0:T(8,128)S(1)} %get-tuple-element.37), channel_id=1, source_target_pairs={{1,2},{2,1},{3,4},{4,3},{5,6},{6,5},{9,10},{10,9},{11,12},{12,11},... | collective-permute-start | bytes 135176 | tf_op jit(solution)/shard_map/ppermute | solution.py:949
  10.4 6.7 %collective-permute-start.2 = (f32[144,128]{1,0:T(8,128)S(1)}, f32[144,128]{1,0:T(8,128)S(1)}, u32[]{:S(2)}, u32[]{:S(2)}) collective-permute-start(f32[144,128]{1,0:T(8,128)S(1)} %get-tuple-element.49), channel_id=1, source_target_pairs={{0,8},{8,0},{16,24},{24,16},{1,9},{9,1},{17,25},{25,17},{2,10},{10... | collective-permute-start | bytes 221192 | tf_op jit(solution)/shard_map/ppermute | solution.py:965
  12.2 4.9 %collective-permute-start.4 = (f32[144,128]{1,0:T(8,128)S(1)}, f32[144,128]{1,0:T(8,128)S(1)}, u32[]{:S(2)}, u32[]{:S(2)}) collective-permute-start(f32[144,128]{1,0:T(8,128)S(1)} %get-tuple-element.51), channel_id=1, source_target_pairs={{0,24},{8,16},{16,8},{24,0},{1,25},{9,17},{17,9},{25,1},{2,26},{10... | collective-permute-start | bytes 221192 | tf_op jit(solution)/shard_map/ppermute | solution.py:965
  13.4 3.6 %collective-permute-start.3 = (f32[24,128]{1,0:T(8,128)S(1)}, f32[24,128]{1,0:T(8,128)S(1)}, u32[]{:S(2)}, u32[]{:S(2)}) collective-permute-start(f32[24,128]{1,0:T(8,128)S(1)} %get-tuple-element.50), channel_id=1, source_target_pairs={{0,16},{8,24},{16,0},{24,8},{1,17},{9,25},{17,1},{25,9},{2,18},{10... | collective-permute-start | bytes 36872 | tf_op jit(solution)/shard_map/ppermute | solution.py:965

commit v4 on v3

v4 whole, which is shorter than its diff:
```python
import functools

import jax
import jax.numpy as jnp
from jax import lax
from jax.experimental import pallas as pl
from jax.experimental.pallas import tpu as pltpu
from jax.sharding import PartitionSpec as P

TILE_X = 8
TILE_Y = 16
PTS = 128
SPLIT = 4

HORIZON = 3.5
DELTA_SQ = 0.25
PENALTY = 4.0
BEND = 0.5
STEP_DT = 0.2

F32 = jnp.float32
I32 = jnp.int32

STRIDE = 24
WIDE = 640
PAD = 16


def bond_offsets():
    limit = HORIZON * HORIZON - DELTA_SQ
    found = []
    for oy in range(-4, 5):
        for ox in range(-4, 5):
            near = max(abs(ox) - 0.4, 0.0) ** 2 + max(abs(oy) - 0.4, 0.0) ** 2
            if near < limit and (ox or oy):
                found.append((ox, oy))
    return found


OFFSETS = bond_offsets()
SIDEWAYS = sorted({oy for _, oy in OFFSETS})


def sign(value):
    return (value > 0) - (value < 0)


def lanes():
    return lax.broadcasted_iota(I32, (8, PTS), 1)


def subs():
    return lax.broadcasted_iota(I32, (8, PTS), 0)


def turn(values, shift):
    size = values.shape[1]
    return pltpu.roll(values, shift % size, 1) if shift % size else values


def slot(dx, dy):
    return 3 * (dx + 1) + dy + 1


def lane_masks():
    lane = lanes()
    row, col = lane // TILE_Y, lane % TILE_Y
    masks = {}
    for o in (1, 2, 3):
        masks["col_at", o] = col < o
        masks["col_at", -o] = col >= TILE_Y - o
        masks["col_from", o] = col >= TILE_Y - o
        masks["col_from", -o] = col < o
        masks["row_at", o] = row < o
        masks["row_at", -o] = row >= TILE_X - o
        masks["row_from", o] = row >= TILE_X - o
        masks["row_from", -o] = row < o
    bits = {}
    for ox in range(-3, 4):
        bits[ox] = jnp.left_shift(jnp.int32(1), 4 * row + ((row + ox) & 7) // 2)
    return masks, bits


def moved(get, oy, masks):
    out = {}
    for dx in (-1, 0, 1):
        held = get(dx, 0)
        if oy:
            held = turn(jnp.where(masks["col_at", oy], get(dx, sign(oy)), held), -oy)
        out[dx] = held
    return out


def across(cells, ox, masks):
    if not ox:
        return cells[0]
    return turn(jnp.where(masks["row_at", ox], cells[sign(ox)], cells[0]), -TILE_Y * ox)


def first_forces(get_jx, get_jy, get_dx, get_dy, get_words, keep=None, both=True):
    masks, bits = lane_masks()
    jx0, jy0, dx0, dy0 = get_jx(0, 0), get_jy(0, 0), get_dx(0, 0), get_dy(0, 0)
    fx = jnp.zeros((8, PTS), F32)
    fy = jnp.zeros((8, PTS), F32)
    for oy in SIDEWAYS:
        jxs, jys = moved(get_jx, oy, masks), moved(get_jy, oy, masks)
        dxs, dys = moved(get_dx, oy, masks), moved(get_dy, oy, masks)
        words = {}
        for dx in (-1, 0, 1):
            words[dx] = get_words(dx, 0)
            if oy:
                words[dx] = jnp.where(masks["col_from", oy], get_words(dx, sign(oy)), words[dx])
        for number, (ox, other) in enumerate(OFFSETS):
            if other != oy:
                continue
            word = words[0]
            if ox:
                word = jnp.where(masks["row_from", ox], words[sign(ox)], word)
            intact = (word & bits[ox]) != 0
            rest_x = across(jxs, ox, masks) - (jx0 - float(ox))
            rest_y = across(jys, ox, masks) - (jy0 - float(oy))
            now_x = across(dxs, ox, masks) - (dx0 - float(ox))
            now_y = across(dys, ox, masks) - (dy0 - float(oy))
            rest_sq = rest_x * rest_x + rest_y * rest_y + DELTA_SQ
            now_sq = now_x * now_x + now_y * now_y + DELTA_SQ
            rest_inv = lax.rsqrt(rest_sq)
            reach = jnp.maximum(1.0 - rest_sq * rest_inv * (1.0 / HORIZON), 0.0)
            weight = jnp.where(intact, reach * reach, 0.0)
            level = weight * rest_inv
            if keep is not None:
                keep(number, weight, level)
            factor = level - weight * lax.rsqrt(now_sq)
            fx = fx + factor * now_x
            if both:
                fy = fy + factor * now_y
    return fx, fy


def pick_lanes(block, index):
    return jnp.take_along_axis(block, index, axis=1, mode="promise_in_bounds")


def flips(blocks):
    lane, sub = lanes(), subs()
    for level in (2, 1, 0):
        step = 1 << level
        stay = ((lane >> (level + 4)) ^ (sub >> level)) & 1 == 0
        if step == 4:
            others = [turn(pltpu.roll(block, 4, 0), 64) for block in blocks]
        else:
            low = (sub >> level) & 1 == 0
            index = lane ^ (TILE_Y * step)
            others = [jnp.where(low, pltpu.roll(block, 8 - step, 0), pltpu.roll(block, step, 0)) for block in blocks]
            others = [pick_lanes(block, index) for block in others]
        blocks = [jnp.where(stay, block, other) for block, other in zip(blocks, others)]
    return blocks


def flip(block):
    return flips([block])[0]


def side_columns(row):
    return pick_lanes(jnp.broadcast_to(row, (8, PTS)), TILE_Y * subs() + (lanes() & (TILE_Y - 1)))


def word_row(packed, s):
    word = jnp.where(subs() == lanes() // TILE_Y, jnp.broadcast_to(packed[:, s : s + 1], (8, PTS)), 0)
    for step in (4, 2, 1):
        word = word | pltpu.roll(word, step, 0)
    return word


def sideways(cells, beside, oy):
    if not oy:
        return cells
    lane = lanes()
    mask = lane < oy if oy > 0 else lane >= PTS + oy
    return turn(jnp.where(mask, beside, cells), -oy)


FROM = 5


def group_masks(start):
    lane, sub = lanes(), subs()
    row = (sub + start) & (TILE_X - 1)
    col = lane & (TILE_Y - 1)
    masks, bits = {}, {}
    for o in (1, 2, 3):
        masks["col", o] = col >= TILE_Y - o
        masks["col", -o] = col < o
        masks["row", o] = row >= TILE_X - o
        masks["row", -o] = row < o
    for ox in range(-3, 4):
        bits[ox] = jnp.left_shift(jnp.int32(1), 4 * row + ((row + ox) & 7) // 2)
    return masks, bits


def group_first(cell, word, keep, start=FROM):
    masks, bits = group_masks(start)
    zero = [cell(f, 0, 0) for f in range(4)]
    fx = jnp.zeros((8, PTS), F32)
    fy = jnp.zeros((8, PTS), F32)
    plain = [word(slot(dx, 0)) for dx in (-1, 0, 1)]
    for oy in SIDEWAYS:
        words = plain
        if oy:
            words = [jnp.where(masks["col", oy], word(slot(dx, sign(oy))), plain[dx + 1]) for dx in (-1, 0, 1)]
        base_y, base_v = zero[1] - float(oy), zero[3] - float(oy)
        for number, (ox, other) in enumerate(OFFSETS):
            if other != oy:
                continue
            picked = words[1]
            if ox:
                picked = jnp.where(masks["row", ox], words[sign(ox) + 1], picked)
            intact = (picked & bits[ox]) != 0
            rest_x = cell(0, oy, ox) - (zero[0] - float(ox))
            rest_y = cell(1, oy, ox) - base_y
            now_x = cell(2, oy, ox) - (zero[2] - float(ox))
            now_y = cell(3, oy, ox) - base_v
            rest_sq = rest_x * rest_x + rest_y * rest_y + DELTA_SQ
            now_sq = now_x * now_x + now_y * now_y + DELTA_SQ
            rest_inv = lax.rsqrt(rest_sq)
            reach = jnp.maximum(1.0 - rest_sq * rest_inv * (1.0 / HORIZON), 0.0)
            weight = jnp.where(intact, reach * reach, 0.0)
            level = weight * rest_inv
            keep(number, weight, level)
            factor = level - weight * lax.rsqrt(now_sq)
            fx = fx + factor * now_x
            fy = fy + factor * now_y
    return fx, fy


def group_second(cell, kept):
    zero = [cell(f, 0, 0) for f in range(2)]
    fx = jnp.zeros((8, PTS), F32)
    fy = jnp.zeros((8, PTS), F32)
    for number, (ox, oy) in enumerate(OFFSETS):
        now_x = cell(0, oy, ox) - (zero[0] - float(ox))
        now_y = cell(1, oy, ox) - (zero[1] - float(oy))
        now_sq = now_x * now_x + now_y * now_y + DELTA_SQ
        weight, level = kept(number)
        factor = level - weight * lax.rsqrt(now_sq)
        fx = fx + factor * now_x
        fy = fy + factor * now_y
    return fx, fy


def bending_of(row):
    here = row(0)
    one, two = row(-1) + row(1), row(-2) + row(2)
    beside = 2.0 * one - 8.0 * here
    out = two - 8.0 * one + 20.0 * here
    return out + turn(beside + turn(here, 1), 1) + turn(beside + turn(here, -1), -1)


def joined(low_part, high_part):
    return jnp.left_shift(high_part.astype(I32), 16) | low_part.astype(I32)


def widen(row_of, count):
    lane, sub = lanes(), subs()
    index = sub * TILE_Y + (lane % 64) // SPLIT
    out = []
    for j in range(count):
        left, right = (
            pick_lanes(jnp.broadcast_to(row_of(b), (8, PTS)), index) for b in (2 * j, 2 * j + 1)
        )
        out.append(jnp.where(lane < 64, left, right))
    return out


def narrow(block_of, tiles):
    lane, sub = lanes(), subs()
    out = []
    for b in tiles:
        held = block_of(b // 2)
        held = held + turn(held, -1)
        held = held + turn(held, -2)
        picked = pick_lanes(held, 64 * (b % 2) + SPLIT * (lane % TILE_Y))
        out.append(jnp.sum(jnp.where(sub == lane // TILE_Y, picked, 0.0), axis=0, keepdims=True))
    return out


def lay_out(ref, at, j, block):
    for row in range(TILE_X):
        ref[at + (row, slice(None), slice(j * PTS, (j + 1) * PTS))] = jnp.broadcast_to(block[row : row + 1], (8, PTS))


class Place:
    def __init__(self, nx, ny, shell_rows, shell_cols):
        self.nx, self.ny = nx, ny
        self.gx, self.gy = lax.axis_index("gx"), lax.axis_index("gy")
        self.shell_rows, self.shell_cols = shell_rows, shell_cols
        self.width = shell_cols * ny
        self.band = shell_rows * nx // TILE_X
        self.bands = shell_rows // self.band
        self.front = self.gx == nx - 1

    def sides(self, first, second):
        even = self.gy % 2 == 0
        right = jnp.where(even, first, second)
        left = jnp.where(even, second, first)
        right = jnp.where(self.gy < self.ny - 1, right, 0.0)
        left = jnp.where(self.gy > 0, left, 0.0)
        return right, left

    def nodes(self, row, columns):
        shape = (8, columns)
        col = lax.broadcasted_iota(I32, shape, 1)
        if columns > self.shell_cols:
            col = jnp.where(col >= self.shell_cols + 64, col - columns, col)
        first = (self.gx * self.shell_rows + row) * self.width + self.gy * self.shell_cols
        return (first + lax.broadcasted_iota(I32, shape, 0) * self.width + col).astype(F32)

    def parts(self):
        inner = [list(range(p * self.band, (p + 1) * self.band, 8)) for p in range(self.bands)]
        return [[-8]] + inner + [[self.shell_rows]]

    def band_of(self, row):
        return jnp.clip((self.gx * self.shell_rows + row + self.band) // self.band - 1, 0, TILE_X - 1)


Y_ROWS = 88


def fetch(pairs, sems):
    copies = [pltpu.make_async_copy(source, target, sems.at[n]) for n, (source, target) in enumerate(pairs)]
    for copy in copies:
        copy.start()
    for copy in copies:
        copy.wait()


def pack_sides(place_args, *refs):
    sources, (first, second), held = refs[:8], refs[8:10], refs[10:16]
    shell, speed, wide_ref, sems = refs[16:]
    place = Place(*place_args)
    pairs = list(zip(sources[:6], held))
    for source, target in zip(sources[6:], (shell, speed)):
        for n, at in enumerate((0, place.shell_cols - PTS)):
            pairs.append((source.at[:, pl.ds(at, PTS)], target.at[n]))
    fetch(pairs, sems)
    disp, vel, jit, words, node, inter = held
    tiles = disp.shape[2]
    even = place.gy % 2 == 0
    blocks = place.shell_cols // PTS
    numbers = node[...].astype(F32)
    edge_blocks = (0, blocks - 1)
    for j in edge_blocks:
        lay_out(wide_ref, (), j, widen(lambda b: numbers[b : b + 1], blocks)[j])
    held = {}
    for j in edge_blocks:
        total = jnp.zeros((8, PTS), F32)
        for part in range(place.bands):
            summed = jnp.zeros((8, PTS), F32)
            for row in range(part * place.band, (part + 1) * place.band, 8):
                wanted = wide_ref[place.band_of(row), :, j * PTS : (j + 1) * PTS]
                ids = place.nodes(row, PTS) + float(j * PTS)
                summed = summed + jnp.where(wanted == ids, shell[min(j, 1), row : row + 8, :], 0.0)
            summed = jnp.sum(summed, axis=0, keepdims=True)
            total = total + jnp.where(subs() == place.band_of(part * place.band), summed, 0.0)
        held[j] = total
    met = narrow(lambda j: held[j], (0, tiles - 1))

    ends = [(jnp.transpose(x[1])[PTS - 8 :], jnp.transpose(x[0])[:8]) for x in (shell, speed)]

    def send(ref, to_right):
        edge = jnp.where(to_right, tiles - 1, 0)
        for f, source in enumerate((disp, disp, vel, vel, jit, jit)):
            ref[8 * f : 8 * f + 8, :] = jnp.where(
                to_right, source[f % 2, :, tiles - 1, :], source[f % 2, :, 0, :]
            )
        ref[48:Y_ROWS, :] = jnp.zeros((Y_ROWS - 48, PTS), F32)
        edge_words = jnp.where(to_right, words[:, tiles - 1, :], words[:, 0, :])
        ref[48:56, 0:9] = (edge_words & 65535).astype(F32)
        ref[56:64, 0:9] = jnp.right_shift(edge_words, 16).astype(F32)
        ref[64:65, :] = jnp.where(to_right, numbers[tiles - 1 : tiles], numbers[0:1])
        ref[65:66, :] = jnp.where(to_right, inter[tiles - 1 : tiles, :], inter[0:1, :])
        ref[66:67, :] = jnp.where(to_right, met[1], met[0])
        for f, source in enumerate((shell, speed)):
            ref[72 + 8 * f : 80 + 8 * f, :] = jnp.where(to_right, *ends[f])

    send(first, even)
    send(second, jnp.logical_not(even))


def own_parts(place_args, far_shell, far_speed, disp, vel, jit, words, node, *refs):
    place = Place(*place_args)
    shell, speed, lattice, lead, groups_w, ends_w, shore, tall, tall_v, wide_ref, sems = refs
    rows_a, tiles = disp.shape[1], disp.shape[2]
    rows, cols = place.shell_rows, place.shell_cols
    lane, sub = lanes(), subs()
    west, east = place.gy == 0, place.gy == place.ny - 1
    north, south = place.gx == 0, place.gx == place.nx - 1
    span = pl.ds(PAD, rows)
    copies = [
        pltpu.make_async_copy(source, target, sems.at[n])
        for n, (source, target) in enumerate(
            (
                (far_shell, shell),
                (far_speed, speed),
                (far_shell, tall.at[span, pl.ds(0, cols)]),
                (far_speed, tall_v.at[span, pl.ds(0, cols)]),
            )
        )
    ]
    for copy in copies:
        copy.start()
    for ref in (tall, tall_v):
        ref[0:PAD, :] = jnp.zeros((PAD, WIDE), F32)
        ref[PAD + rows :, :] = jnp.zeros((PAD, WIDE), F32)
        ref[PAD : PAD + rows, cols:WIDE] = jnp.zeros((rows, PTS), F32)

    for f in range(2):
        rest = [jit[f, a] for a in range(rows_a)]
        whole = [jit[f, a] + disp[f, a] for a in range(rows_a)]
        soon = [x + STEP_DT * vel[f, a] for a, x in enumerate(whole)]
        for a, (x, y, z) in enumerate(zip(flips(rest), flips(whole), flips(soon))):
            lattice[f, a] = x
            lattice[2 + f, a] = y
            lead[f, a] = z

    before = [None] * 9
    for a in range(rows_a):
        packed = words[a]
        for dx in (-1, 0, 1):
            for dy in (-1, 0, 1):
                s = slot(dx, dy)
                word = word_row(packed, s)
                if dy < 0:
                    word = jnp.where((lane < TILE_Y) & west, 0, word)
                if dy > 0:
                    word = jnp.where((lane >= PTS - TILE_Y) & east, 0, word)
                if dx < 0 and a == 0:
                    word = jnp.where(north, 0, word)
                if dx > 0 and a == rows_a - 1:
                    word = jnp.where(south, 0, word)
                if a:
                    groups_w[s, a - 1] = jnp.where(sub < TILE_X - FROM, before[s], word)
                if a in (0, rows_a - 1):
                    ends_w[s, min(a, 1)] = word
                before[s] = word

    numbers = node[...].astype(F32)
    for j, block in enumerate(widen(lambda b: numbers[b : b + 1], cols // PTS)):
        lay_out(wide_ref, (), j, block)
    for copy in copies:
        copy.wait()
    sub_wide = lax.broadcasted_iota(I32, (8, cols), 0)
    ahead = jnp.zeros((8, cols), F32)
    met = jnp.zeros((8, cols), F32)
    for part in place.parts():
        soon = jnp.zeros((8, cols), F32)
        now = jnp.zeros((8, cols), F32)
        band = place.band_of(part[0])
        for row in part:
            at = PAD + row
            hit = wide_ref[band] == place.nodes(row, cols)
            bending = bending_of(lambda o: tall[at + o : at + o + 8, :])[:, 0:cols]
            here = tall[at : at + 8, 0:cols]
            later = here + STEP_DT * (tall_v[at : at + 8, 0:cols] - (STEP_DT * BEND) * bending)
            soon = soon + jnp.where(hit, later, 0.0)
            if 0 <= row < rows:
                now = now + jnp.where(hit, here, 0.0)
        ahead = ahead + jnp.where(sub_wide == band, jnp.sum(soon, axis=0, keepdims=True), 0.0)
        if 0 <= part[0] < rows:
            met = met + jnp.where(sub_wide == band, jnp.sum(now, axis=0, keepdims=True), 0.0)
    for base, values in ((0, ahead), (tiles, met)):
        for b, row in enumerate(narrow(lambda j: values[:, j * PTS : (j + 1) * PTS], range(tiles))):
            shore[base + b : base + b + 1, :] = row


HALO_ROWS = 120
CONTACT_ROWS = 24


def shell_strip(right, left, at):
    middle = jnp.zeros((PTS - 16, PTS), F32)
    return jnp.transpose(jnp.concatenate([right[at : at + 8], middle, left[at : at + 8]], axis=0))


def pack_ends(
    place_args, shifts, disp, vel, jit, words, node, inter, shell, speed, lattice, ends_w, shore, first, second, *refs
):
    place = Place(*place_args)
    outs = refs[: len(shifts)]
    own, strip_d, strip_v, grid, tall, wide_ref = refs[len(shifts) :]
    rows_a, tiles = disp.shape[1], disp.shape[2]
    rows, cols = place.shell_rows, place.shell_cols
    right, left = place.sides(first[...], second[...])
    lane, sub = lanes(), subs()
    leftward = (lane[0:1] & (TILE_Y - 1)) >= TILE_Y // 2
    last = rows_a - 1

    for f in range(4):
        for level, a in enumerate((last - 1, last)):
            at = 32 + 8 * (f % 2) + a
            row = jnp.where(leftward, left[at : at + 1], right[at : at + 1])
            if f >= 2:
                at = 8 * (f % 2) + a
                row = row + jnp.where(leftward, left[at : at + 1], right[at : at + 1])
            near = side_columns(row)
            for n, oy in enumerate(SIDEWAYS):
                grid[f, n, 8 * level : 8 * level + 8, :] = sideways(lattice[f, a], near, oy)
        for n in range(len(SIDEWAYS)):
            grid[f, n, 16:24, :] = jnp.zeros((8, PTS), F32)
    force, _ = group_first(
        lambda f, oy, ox: grid[f, SIDEWAYS.index(oy), 8 + ox : 16 + ox, :],
        lambda s: ends_w[s, 1] if s < 6 else jnp.zeros((8, PTS), I32),
        lambda number, weight, level: None,
        start=0,
    )
    gap = disp[0, last] + inter[...]
    own[0:8, :] = gap + STEP_DT * (vel[0, last] + STEP_DT * flip(force))
    own[8:16, :] = gap
    own[16:24, :] = jnp.zeros((8, PTS), F32)
    own[16:17, :] = right[last : last + 1] + right[65:66]
    own[17:18, :] = left[last : last + 1] + left[65:66]

    halo_d = shell_strip(right, left, 72)
    halo_v = shell_strip(right, left, 80)
    strip_d[...] = halo_d
    strip_v[...] = halo_v
    for at in (0, 8, PAD + rows, PAD + rows + 8):
        tall[at : at + 8, :] = jnp.zeros((8, PTS), F32)
    tall[PAD : PAD + rows, :] = halo_d
    numbers = node[...].astype(F32)
    blocks = widen(lambda b: numbers[b : b + 1], cols // PTS)
    low = lane < PTS // 2
    lay_out(wide_ref, (), 0, jnp.where(low, blocks[0], blocks[-1]))
    far = jnp.where(low, 0.0, float(cols - PTS))
    ahead = jnp.zeros((8, PTS), F32)
    for part in place.parts():
        soon = jnp.zeros((8, PTS), F32)
        band = place.band_of(part[0])
        for row in part:
            at = PAD + row
            here = tall[at : at + 8, :]
            column = 2.0 * (tall[at - 1 : at + 7, :] + tall[at + 1 : at + 9, :]) - 8.0 * here
            from_left = turn(jnp.where(low, 0.0, column), 1) + turn(jnp.where(low, 0.0, here), 2)
            from_right = turn(jnp.where(low, column, 0.0), -1) + turn(jnp.where(low, here, 0.0), -2)
            hit = wide_ref[band] == place.nodes(row, PTS) + far
            soon = soon + jnp.where(hit, jnp.where(low, from_left, from_right), 0.0)
        ahead = ahead + jnp.where(sub == band, jnp.sum(soon, axis=0, keepdims=True), 0.0)
    base = CONTACT_ROWS
    own[base + 16 : base + 24, :] = jnp.zeros((8, PTS), F32)
    own[base : base + 16, :] = shore[...]
    for b, row in zip((0, tiles - 1), narrow(lambda j: ahead, (0, tiles - 1))):
        own[base + b : base + b + 1, :] = shore[b : b + 1, :] - (STEP_DT * STEP_DT * BEND) * row
    own[base + 16 : base + 17, :] = right[66:67]
    own[base + 17 : base + 18, :] = left[66:67]

    mine = jnp.where(place.front, own[0:CONTACT_ROWS, :], own[base : base + CONTACT_ROWS, :])
    for shift, out in zip(shifts, outs):
        at = 0
        if shift & (shift + 1) == 0:
            at = HALO_ROWS
            down = (place.gx ^ shift) > place.gx
            edge = jnp.where(down, rows_a - 1, 0)
            for f, source in enumerate((disp, disp, vel, vel, jit, jit)):
                out[8 * f : 8 * f + 8, :] = source[f % 2, edge]
            out[48:80, :] = jnp.zeros((32, PTS), F32)
            edge_words = words[edge]
            out[48:56, 0:9] = (edge_words & 65535).astype(F32)
            out[56:64, 0:9] = jnp.right_shift(edge_words, 16).astype(F32)
            for f in range(8):
                for side, values in ((64, right), (72, left)):
                    low, high = values[8 * f : 8 * f + 1], values[8 * f + rows_a - 1 : 8 * f + rows_a]
                    out[side + f : side + f + 1, :] = jnp.where(down, high, low)
            for j in range(WIDE // PTS):
                cut = slice(j * PTS, (j + 1) * PTS)
                if j < cols // PTS:
                    d_low, d_high = shell[0:4, cut], shell[rows - 4 : rows, cut]
                    v_low, v_high = speed[0:2, cut], speed[rows - 2 : rows, cut]
                else:
                    d_low, d_high = halo_d[0:4], halo_d[rows - 4 : rows]
                    v_low, v_high = halo_v[0:2], halo_v[rows - 2 : rows]
                out[80 + 8 * j : 84 + 8 * j, :] = jnp.where(down, d_high, d_low)
                out[84 + 8 * j : 86 + 8 * j, :] = jnp.where(down, v_high, v_low)
                out[86 + 8 * j : 88 + 8 * j, :] = jnp.zeros((2, PTS), F32)
        out[at : at + CONTACT_ROWS, :] = mine


def inner_rows(place_args, disp, jit, shell, speed, lattice, groups_w, first, second, strip_d, strip_v, *refs):
    place = Place(*place_args)
    win, weights, levels, flat, beside, tiles_f, mid, strips, kinds, panes = refs
    cols = place.shell_cols
    rows_a, tiles = disp.shape[1], disp.shape[2]
    right, left = place.sides(first[...], second[...])
    lane = lanes()
    leftward = (lane & (TILE_Y - 1)) >= TILE_Y // 2
    side = [jnp.where(leftward, left[8 * f : 8 * f + 8], right[8 * f : 8 * f + 8]) for f in range(6)]

    strips[...] = jnp.zeros_like(strips)
    for f in range(4):
        rest = jit[f % 2]
        whole = rest if f < 2 else rest + disp[f % 2]
        beyond = side[4 + f % 2] if f < 2 else side[4 + f % 2] + side[f % 2]
        strips[f, 0, 8:16, :] = beyond
        strips[f, 1, 8:16, :] = whole[:, 0, :]
        strips[f, 2, 8:16, :] = whole[:, tiles - 1, :]
        nears = [side_columns(beyond[a : a + 1]) for a in range(rows_a)]
        for a, near in enumerate(nears):
            cells = lattice[f, a]
            for n, oy in enumerate(SIDEWAYS):
                shifted = sideways(cells, near, oy)
                if a < rows_a - 1:
                    win[f, n, a, 0:8, :] = shifted
                if a > 0:
                    win[f, n, a - 1, 8:16, :] = shifted
    left_words = joined(left[48:56], left[56:64])
    right_words = joined(right[48:56], right[56:64])
    for s in range(9):
        kinds[s] = jnp.where(
            leftward,
            jnp.broadcast_to(left_words[:, s : s + 1], (8, PTS)),
            jnp.broadcast_to(right_words[:, s : s + 1], (8, PTS)),
        )

    flat[...] = jnp.zeros_like(flat)

    blocks = mid.shape[0]
    for n in range(blocks):
        panes[n, :, 0:cols] = shell[8 * n : 8 * n + 24, :]
        panes[n, :, cols:WIDE] = strip_d[8 * n : 8 * n + 24, :]
    each = -(-blocks // (rows_a - 1))

    def bend_block(n):
        at = pl.multiple_of(8 * n + 8, 8)
        bending = bending_of(lambda o: panes[n, 8 + o : 16 + o, :])
        mid[n, :, 0:cols] = speed[pl.ds(at, 8), :] - (STEP_DT * BEND) * bending[:, 0:cols]
        mid[n, :, cols:WIDE] = strip_v[pl.ds(at, 8), :] - (STEP_DT * BEND) * bending[:, cols:WIDE]

    @pl.loop(0, rows_a - 1)
    def _(k):
        for part in range(each):
            bend_block(jnp.minimum(each * k + part, blocks - 1))

        def cell(f, oy, ox):
            return win[f, SIDEWAYS.index(oy), k, FROM + ox : FROM + ox + 8, :]

        def keep(number, weight, level):
            weights[number, k] = weight
            levels[number, k] = level

        fx, fy = group_first(cell, lambda s: groups_w[s, k], keep)
        at = pl.multiple_of(8 * k + 16, 8)
        flat[0, pl.ds(at, 8), :] = fx
        flat[1, pl.ds(at, 8), :] = fy

    def getter(f):
        held = {}

        def get(dx, dy):
            if (dx, dy) not in held:
                held[dx, dy] = turn(strips[f, dy % 3, 8 + dx : 16 + dx, :], TILE_Y * dy)
            return held[dx, dy]

        return get

    forces = first_forces(getter(0), getter(1), getter(2), getter(3), lambda dx, dy: kinds[slot(dx, dy)])
    for f in range(2):
        moved_side = side[4 + f] + side[f] + STEP_DT * (side[2 + f] + STEP_DT * forces[f])
        for a in range(rows_a):
            beside[f, a] = side_columns(moved_side[a : a + 1])
        for a, cells in enumerate(flips([flat[f, 8 * a + 11 : 8 * a + 19, :] for a in range(1, rows_a - 1)])):
            tiles_f[f, a + 1] = cells
        tiles_f[f, 0] = jnp.zeros((8, PTS), F32)
        tiles_f[f, rows_a - 1] = jnp.zeros((8, PTS), F32)


def both_steps(place_args, shifts, *refs):
    place = Place(*place_args)
    disp, vel, node, inter, shell, speed, first, second, own, strip_d, strip_v = refs[:11]
    lead, ends_w, win, weights, levels, flat_in, beside, tiles_f, mid = refs[11:20]
    ends = refs[20 : 20 + len(shifts)]
    targets = refs[20 + len(shifts) : 24 + len(shifts)]
    scratch = refs[24 + len(shifts) :]
    out_disp, out_vel, out_shell, out_speed, gaps, halo, rim, rim_v, panes, fasts, pushed, ewin, ewords = scratch[:13]
    eweights, elevels, flat, flat2, seams, kinds, swin, sems = scratch[13:]
    outs = (out_disp, out_vel, out_shell, out_speed)
    copies = [pltpu.make_async_copy(x, y, sems.at[n]) for n, (x, y) in enumerate(zip(outs, targets))]
    rows_a, tiles = disp.shape[1], disp.shape[2]
    rows, cols = place.shell_rows, place.shell_cols
    blocks = rows // 8
    right, left = place.sides(first[...], second[...])

    halo[...] = jnp.zeros_like(halo)
    contact = jnp.where(place.front, own[0:CONTACT_ROWS, :], 0.0)
    owners = own[CONTACT_ROWS:, :]
    for shift, ref in zip(shifts, ends):
        partner = place.gx ^ shift
        at = 0
        if shift & (shift + 1) == 0:
            at = HALO_ROWS

            @pl.when(partner == place.gx - 1)
            def _():
                halo[0] = ref[0:HALO_ROWS, :]

            @pl.when(partner == place.gx + 1)
            def _():
                halo[1] = ref[0:HALO_ROWS, :]

        got = ref[at : at + CONTACT_ROWS, :]
        contact = jnp.where(partner == place.nx - 1, got, contact)
        owners = owners + got

    def wide(source, strip, row, count):
        return jnp.concatenate([source[row : row + count, :], strip[row : row + count, :]], axis=1)

    zeros = jnp.zeros((8, WIDE), F32)
    rim[0, 16:32, :] = wide(shell, strip_d, 0, 16)
    rim[1, 0:16, :] = wide(shell, strip_d, rows - 16, 16)
    rim_v[0, 8:16, :] = wide(speed, strip_v, 0, 8)
    rim_v[1, 0:8, :] = wide(speed, strip_v, rows - 8, 8)
    for ref, at in ((rim, (0, 0)), (rim, (0, 8)), (rim, (1, 16)), (rim, (1, 24)), (rim_v, (0, 0)), (rim_v, (1, 8))):
        ref[at[0], at[1] : at[1] + 8, :] = zeros
    for j in range(WIDE // PTS):
        cut = slice(j * PTS, (j + 1) * PTS)
        rim[0, 12:16, cut] = halo[0, 80 + 8 * j : 84 + 8 * j, :]
        rim_v[0, 6:8, cut] = halo[0, 84 + 8 * j : 86 + 8 * j, :]
        rim[1, 16:20, cut] = halo[1, 80 + 8 * j : 84 + 8 * j, :]
        rim_v[1, 8:10, cut] = halo[1, 84 + 8 * j : 86 + 8 * j, :]
    numbers = node[...].astype(F32)
    node_rows = [numbers[b : b + 1] for b in range(tiles)] + [right[64:65], left[64:65]]
    gap_rows = [contact[8 + b : 9 + b] for b in range(tiles)] + [contact[16:17], contact[17:18]]
    soon_rows = [contact[b : b + 1] for b in range(tiles)]
    for j, (nodes, gap) in enumerate(zip(widen(node_rows.__getitem__, 5), widen(gap_rows.__getitem__, 5))):
        lay_out(gaps, (0,), j, nodes)
        lay_out(gaps, (1,), j, gap)
    for j, soon in enumerate(widen(soon_rows.__getitem__, 4)):
        lay_out(gaps, (2,), j, soon)
    col = lax.broadcasted_iota(I32, (8, WIDE), 1)
    inside = jnp.where(col < cols, 1.0, 0.0)
    inside = jnp.where((col >= cols) & (col < cols + 64) & (place.gy < place.ny - 1), 1.0, inside)
    inside = jnp.where((col >= cols + 64) & (place.gy > 0), 1.0, inside)
    for n in range(-1, blocks + 1):
        row = 8 * n
        if 0 < n < blocks - 1:
            here, steady = wide(shell, strip_d, row, 8), mid[n - 1]
        else:
            end = 0 if n < 1 else 1
            at = row + 16 if end == 0 else row - rows + 16
            here = rim[end, at : at + 8, :]
            bending = bending_of(lambda o: rim[end, at + o : at + o + 8, :])
            steady = rim_v[end, at - 8 : at, :] - (STEP_DT * BEND) * bending
        band = place.band_of(row)
        hit = gaps[0, band] == place.nodes(row, WIDE)
        push = jnp.where(hit, PENALTY * jnp.maximum(gaps[1, band] - here, 0.0), 0.0)
        fast = steady + STEP_DT * push
        keep = inside
        if n < 0:
            keep = inside * jnp.where(place.gx > 0, 1.0, 0.0)
        elif n == blocks:
            keep = inside * jnp.where(place.gx < place.nx - 1, 1.0, 0.0)
        there = (here + STEP_DT * fast) * keep
        for part in (-1, 0, 1):
            if 0 <= n - part < blocks:
                panes[n - part, 8 + 8 * part : 16 + 8 * part, :] = there
        if 0 <= n < blocks:
            fasts[n] = fast[:, 0:cols]
            pushed[n] = push[:, 0:cols]

    lane, sub = lanes(), subs()
    west, east = place.gy == 0, place.gy == place.ny - 1
    north, south = place.gx == 0, place.gx == place.nx - 1
    leftward = (lane & (TILE_Y - 1)) >= TILE_Y // 2
    last = rows_a - 1
    high = lane >= PTS // 2
    segment = ((lane + 16) >> 5) & 3

    def side_row(end, part):
        return jnp.where(leftward[0:1], halo[end, 72 + part : 73 + part, :], halo[end, 64 + part : 65 + part, :])

    def near_row(a, part):
        at = 8 * part + a
        return jnp.where(leftward[0:1], left[at : at + 1], right[at : at + 1])

    border = (-1, 0, last, rows_a)
    sides = {}
    for part in range(6):
        for a in border:
            sides[a, part] = near_row(a, part) if 0 <= a <= last else side_row(0 if a < 0 else 1, part)
    lead_side, far_lead = {}, {}
    straight = SIDEWAYS.index(0)
    turned = flips(
        [
            piece
            for end in (0, 1)
            for f in range(2)
            for rest in (halo[end, 32 + 8 * f : 40 + 8 * f, :],)
            for whole in (rest + halo[end, 8 * f : 8 * f + 8, :],)
            for piece in (rest, whole, whole + STEP_DT * halo[end, 16 + 8 * f : 24 + 8 * f, :])
        ]
    )
    for f in range(2):
        for a in border:
            lead_side[f, a] = side_columns(sides[a, 4 + f] + sides[a, f] + STEP_DT * sides[a, 2 + f])
        for end in (0, 1):
            far_lead[f, end] = turned[6 * end + 3 * f + 2]
        for field in (f, 2 + f):
            cells, near = {}, {}
            for a in border:
                near[a] = side_columns(sides[a, 4 + f] + sides[a, f] if field >= 2 else sides[a, 4 + f])
            cells[-1], cells[rows_a] = (turned[6 * end + 3 * f + field // 2] for end in (0, 1))
            cells[0] = win[field, straight, 0, 0:8, :]
            cells[last] = win[field, straight, rows_a - 2, 8:16, :]
            for n, oy in enumerate(SIDEWAYS):
                ewin[field, n, 0, 0:8, :] = sideways(cells[-1], near[-1], oy)
                ewin[field, n, 0, 8:16, :] = win[field, n, 0, 0:8, :]
                ewin[field, n, 1, 0:8, :] = win[field, n, rows_a - 2, 8:16, :]
                ewin[field, n, 1, 8:16, :] = sideways(cells[rows_a], near[rows_a], oy)
            for half, (up, down) in enumerate(((-1, last), (0, rows_a))):
                pieces = [
                    jnp.where(high, near[up], cells[up]),
                    turn(jnp.where(high, cells[up], near[up]), 32),
                    turn(jnp.where(high, near[down], cells[down]), 64),
                    turn(jnp.where(high, cells[down], near[down]), 96),
                ]
                seam = pieces[3]
                for q in (2, 1, 0):
                    seam = jnp.where(segment == q, pieces[q], seam)
                for n, oy in enumerate(SIDEWAYS):
                    seams[field, n, 8 * half : 8 * half + 8, :] = turn(seam, -oy)
    for end in (0, 1):
        packed = joined(halo[end, 48:56, :], halo[end, 56:64, :])
        for dx in (-1, 0, 1):
            for dy in (-1, 0, 1):
                s = slot(dx, dy)
                word = word_row(packed, s)
                if dy < 0:
                    word = jnp.where((lane < TILE_Y) & west, 0, word)
                if dy > 0:
                    word = jnp.where((lane >= PTS - TILE_Y) & east, 0, word)
                pair = (word, ends_w[s, 0]) if end == 0 else (ends_w[s, 1], word)
                ewords[s, end] = jnp.where(sub < TILE_X - FROM, *pair)
    parts = []
    for at in (0, 1):
        rows_w = []
        for a in (-1, last, 0, rows_a):
            for values, part in ((left, 72), (right, 64)):
                if 0 <= a <= last:
                    rows_w.append(values[48 + 8 * at + a : 49 + 8 * at + a])
                else:
                    end = 0 if a < 0 else 1
                    rows_w.append(halo[end, part + 6 + at : part + 7 + at, :])
        parts.append(jnp.concatenate(rows_w, axis=0))
    packed = joined(*parts)
    for dx in (-1, 0, 1):
        for dy in (-1, 0, 1):
            s = slot(dx, dy)
            word = jnp.broadcast_to(packed[:, s : s + 1], (8, PTS))
            upper, lower = jnp.where(sub == segment, word, 0), jnp.where(sub == segment + 4, word, 0)
            for step in (4, 2, 1):
                upper, lower = upper | pltpu.roll(upper, step, 0), lower | pltpu.roll(lower, step, 0)
            if dx < 0:
                lower = jnp.where((segment < 2) & north, 0, lower)
            if dx > 0:
                upper = jnp.where((segment >= 2) & south, 0, upper)
            kinds[s] = jnp.where(sub < TILE_X - FROM, upper, lower)

    flat[...] = flat_in[...]
    for e in (0, 1):

        def keep_end(number, weight, level, e=e):
            eweights[number, e] = weight
            elevels[number, e] = level

        found = group_first(
            lambda f, oy, ox: ewin[f, SIDEWAYS.index(oy), e, FROM + ox : FROM + ox + 8, :],
            lambda s: ewords[s, e],
            keep_end,
        )
        for f in range(2):
            flat[f, 8 + 8 * rows_a * e : 16 + 8 * rows_a * e, :] = found[f]
    seam_f = group_first(
        lambda f, oy, ox: seams[f, SIDEWAYS.index(oy), FROM + ox : FROM + ox + 8, :],
        lambda s: kinds[s],
        lambda number, weight, level: None,
    )

    here = jnp.where(place.front, 1.0, 0.0)
    push = PENALTY * here * jnp.maximum(contact[8:18] - owners[8:18], 0.0)
    side_push = side_columns(jnp.where(leftward[0:1], push[9:10], push[8:9]))
    push = push[0:8]
    push_rows = flip(push)

    square = STEP_DT * STEP_DT
    for f in range(2):
        force = pltpu.roll(seam_f[f], FROM, 0)
        above = square * jnp.where(high, force, turn(force, -32))
        below = square * jnp.where(high, turn(force, -64), turn(force, -96))
        nears = {-1: lead_side[f, -1] + above, rows_a: lead_side[f, rows_a] + below}
        nears[0] = jnp.where(sub < FROM, lead_side[f, 0] + above, beside[f, 0])
        nears[last] = jnp.where(sub < FROM, beside[f, last], lead_side[f, last] + below)
        if f == 0:
            nears[last] = nears[last] - square * side_push
        for a in range(-1, rows_a + 1):
            cells = far_lead[f, 0 if a < 0 else 1] if a in (-1, rows_a) else lead[f, a]
            cells = cells + square * flat[f, 8 * a + 11 : 8 * a + 19, :]
            if a == last and f == 0:
                cells = cells - square * push_rows
            near = nears[a] if a in nears else beside[f, a]
            for n, oy in enumerate(SIDEWAYS):
                shifted = sideways(cells, near, oy)
                if a < rows_a:
                    swin[f, n, a + 1, 0:8, :] = shifted
                if a >= 0:
                    swin[f, n, a, 8:16, :] = shifted

    def second_group(k, kept):
        def cell(f, oy, ox):
            return swin[f, SIDEWAYS.index(oy), k, FROM + ox : FROM + ox + 8, :]

        fx, fy = group_second(cell, kept)
        at = pl.multiple_of(8 * k + 8, 8)
        flat2[0, pl.ds(at, 8), :] = fx
        flat2[1, pl.ds(at, 8), :] = fy

    def second_rows(n):
        row = pl.multiple_of(8 * n, 8)
        here = panes[n, 8:16, 0:cols]
        band = place.band_of(row)
        hit = gaps[0, band, :, 0:cols] == place.nodes(row, cols)
        gap = gaps[2, band, :, 0:cols] - square * pushed[n]
        push = jnp.where(hit, PENALTY * jnp.maximum(gap - here, 0.0), 0.0)
        bending = bending_of(lambda o: panes[n, 8 + o : 16 + o, :])[:, 0:cols]
        fast = fasts[n] + STEP_DT * (push - BEND * bending)
        out_speed[pl.ds(row, 8), :] = fast
        out_shell[pl.ds(row, 8), :] = here + STEP_DT * fast

    inner = rows_a - 1
    each = blocks // rows_a

    @pl.loop(0, inner)
    def _(k):
        second_group(k + 1, lambda number: (weights[number, k], levels[number, k]))
        for part in range(each):
            second_rows(each * k + part)

    tail = blocks - each * inner
    half = -(-tail // 2)

    @pl.loop(0, 2)
    def _(e):
        second_group(e * rows_a, lambda number: (eweights[number, e], elevels[number, e]))
        for part in range(half):
            second_rows(jnp.minimum(each * inner + half * e + part, blocks - 1))

    copies[2].start()
    copies[3].start()

    for f in range(2):
        thens = flips([flat2[f, 8 * a + 11 : 8 * a + 19, :] for a in range(rows_a)])
        end_was = flips([flat[f, 8 * a + 11 : 8 * a + 19, :] for a in (0, last)])
        for a in range(rows_a):
            was = end_was[min(a, 1)] if a in (0, last) else tiles_f[f, a]
            then = thens[a]
            if f == 0 and a == last:
                was = was - push
                gap = disp[0, last] + STEP_DT * (vel[0, last] + STEP_DT * was) + inter[...]
                reached = owners[0:8] + square * push
                then = then - PENALTY * here * jnp.maximum(gap - reached, 0.0)
            fast = vel[f, a] + STEP_DT * was
            faster = fast + STEP_DT * then
            out_vel[f, a] = faster
            out_disp[f, a] = disp[f, a] + STEP_DT * (fast + faster)
    copies[0].start()
    copies[1].start()
    for copy in copies:
        copy.wait()


def on_device(nx, ny, disp, vel, jit, words, node, inter, shell, speed):
    rows_a = disp.shape[1]
    rows, cols = shell.shape
    place_args = (nx, ny, rows, cols)
    shifts = tuple(range(1, nx))
    span, count, blocks = rows_a - 1, len(OFFSETS), rows // 8

    def call(body, out, scratch, *args, far=0, **more):
        args = [pltpu.with_memory_space_constraint(x, pltpu.MemorySpace.HBM) for x in args[:far]] + list(args[far:])
        specs = [pl.BlockSpec(memory_space=pltpu.MemorySpace.HBM)] * far
        specs += [pl.BlockSpec(memory_space=pltpu.VMEM)] * (len(args) - far)
        return pl.pallas_call(
            body,
            out_shape=out,
            in_specs=specs,
            scratch_shapes=scratch,
            **more,
            compiler_params=pltpu.CompilerParams(vmem_limit_bytes=20 * 1024 * 1024),
        )(*args)

    def shaped(*shape, dtype=F32):
        return jax.ShapeDtypeStruct(shape + (PTS,), dtype)

    def like(*arrays):
        return [jax.ShapeDtypeStruct(x.shape, x.dtype) for x in arrays]

    wide = pltpu.VMEM((TILE_X, 8, cols), F32)
    tall = pltpu.VMEM((rows + 2 * PAD, WIDE), F32)
    edges = pltpu.VMEM((2, rows, PTS), F32)
    far_shell, far_speed = shell, speed
    small = (disp, vel, jit, words, node, inter)
    first, second, *small = call(
        functools.partial(pack_sides, place_args),
        [shaped(Y_ROWS)] * 2 + like(*small),
        [edges, edges, wide, pltpu.SemaphoreType.DMA((10,))],
        *small,
        far_shell,
        far_speed,
        far=8,
    )
    disp, vel, jit, words, node, inter = small
    first = lax.ppermute(first, "gy", [(i, i ^ 1) for i in range(ny)])
    second = lax.ppermute(
        second,
        ("gx", "gy"),
        [
            (i * ny + j, i * ny + ((j - 1) ^ 1) + 1 if 0 < j < ny - 1 else (i ^ 1) * ny + j)
            for i in range(nx)
            for j in range(ny)
        ],
    )

    shell, speed, lattice, lead, groups_w, ends_w, shore = call(
        functools.partial(own_parts, place_args),
        like(far_shell, far_speed)
        + [
            shaped(4, rows_a, 8),
            shaped(2, rows_a, 8),
            shaped(9, span, 8, dtype=I32),
            shaped(9, 2, 8, dtype=I32),
            shaped(2 * disp.shape[2]),
        ],
        [tall, tall, wide, pltpu.SemaphoreType.DMA((4,))],
        far_shell,
        far_speed,
        disp,
        vel,
        jit,
        words,
        node,
        far=2,
    )

    outs = [shaped(CONTACT_ROWS + (HALO_ROWS if s & (s + 1) == 0 else 0)) for s in shifts]
    *ends, own, strip_d, strip_v = call(
        functools.partial(pack_ends, place_args, shifts),
        outs + [shaped(2 * CONTACT_ROWS), shaped(rows), shaped(rows)],
        [
            pltpu.VMEM((4, len(SIDEWAYS), 24, PTS), F32),
            pltpu.VMEM((rows + 2 * PAD, PTS), F32),
            pltpu.VMEM((TILE_X, 8, PTS), F32),
        ],
        *small,
        shell,
        speed,
        lattice,
        ends_w,
        shore,
        first,
        second,
    )
    ends = [lax.ppermute(e, "gx", [(i, i ^ s) for i in range(nx)]) for s, e in zip(shifts, ends)]

    inner = call(
        functools.partial(inner_rows, place_args),
        [
            shaped(4, len(SIDEWAYS), span, 16),
            shaped(count, span, 8),
            shaped(count, span, 8),
            shaped(2, 8 * (rows_a + 3)),
            shaped(2, rows_a, 8),
            shaped(2, rows_a, 8),
            jax.ShapeDtypeStruct((blocks - 2, 8, WIDE), F32),
        ],
        [
            pltpu.VMEM((4, 3, 24, PTS), F32),
            pltpu.VMEM((9, 8, PTS), I32),
            pltpu.VMEM((blocks - 2, 24, WIDE), F32),
        ],
        disp,
        jit,
        shell,
        speed,
        lattice,
        groups_w,
        first,
        second,
        strip_d,
        strip_v,
    )

    out = [jax.ShapeDtypeStruct(x.shape, F32) for x in (disp, vel, shell, speed)]
    scratch = [pltpu.VMEM(x.shape, F32) for x in out] + [
        pltpu.VMEM((3, TILE_X, 8, WIDE), F32),
        pltpu.VMEM((2, HALO_ROWS, PTS), F32),
        pltpu.VMEM((2, 32, WIDE), F32),
        pltpu.VMEM((2, 16, WIDE), F32),
        pltpu.VMEM((blocks, 24, WIDE), F32),
        pltpu.VMEM((blocks, 8, cols), F32),
        pltpu.VMEM((blocks, 8, cols), F32),
        pltpu.VMEM((4, len(SIDEWAYS), 2, 16, PTS), F32),
        pltpu.VMEM((9, 2, 8, PTS), I32),
        pltpu.VMEM((count, 2, 8, PTS), F32),
        pltpu.VMEM((count, 2, 8, PTS), F32),
        pltpu.VMEM((2, 8 * (rows_a + 3), PTS), F32),
        pltpu.VMEM((2, 8 * (rows_a + 3), PTS), F32),
        pltpu.VMEM((4, len(SIDEWAYS), 16, PTS), F32),
        pltpu.VMEM((9, 8, PTS), I32),
        pltpu.VMEM((2, len(SIDEWAYS), rows_a + 1, 16, PTS), F32),
        pltpu.SemaphoreType.DMA((4,)),
    ]
    return tuple(
        call(
            functools.partial(both_steps, place_args, shifts),
            out,
            scratch,
            disp,
            vel,
            node,
            inter,
            shell,
            speed,
            first,
            second,
            own,
            strip_d,
            strip_v,
            lead,
            ends_w,
            *inner,
            *ends,
            out_specs=[pl.BlockSpec(memory_space=pltpu.MemorySpace.HBM)] * 4,
        )
    )


def solution(mesh):
    in_specs = (
        P(None, "gx", "gy", None),
        P(None, "gx", "gy", None),
        P(None, "gx", "gy", None),
        P("gx", "gy", None),
        P("gy", None),
        P("gy", None),
        P("gx", "gy"),
        P("gx", "gy"),
    )
    out_specs = (P(None, "gx", "gy", None), P(None, "gx", "gy", None), P("gx", "gy"), P("gx", "gy"))
    body = functools.partial(on_device, mesh.shape["gx"], mesh.shape["gy"])
    return jax.shard_map(body, mesh=mesh, in_specs=in_specs, out_specs=out_specs, check_vma=False)
```

time: 23.1 us -> 21.8 us (0.944)
  the two profiles are of different devices: /device:TPU:1 before, /device:TPU:0 now
where the time goes in v4:
time: 21.8 us; the launch traced here: 21.6 us
  Pallas kernels  14.2 us (65%)
  starting transfers between devices  6.64 us (30%)
  between operations  0.7 us (3%)
    pallas_call x5, Pallas kernels, call(): pl.pallas_call(body, out_shape=out, in_specs=specs, scratch_shapes=scratc...  14.2 us
    ppermute x3, starting transfers between devices, on_device(): lax.ppermute(e, 'gx', [(i, i ^ s) for i in range(nx)])  3.55 us
    ppermute x1, starting transfers between devices, on_device(): lax.ppermute(second, ('gx', 'gy'), [(i * ny + j, i * ny + (j - 1 ^ 1) + 1...  2.56 us
    ppermute x1, starting transfers between devices, on_device(): first = lax.ppermute(first, 'gy', [(i, i ^ 1) for i in range(ny)])  0.52 us
  transfers between devices with their start and end apart: 5, of which 0 were waited for; matrix products, arithmetic and copies ran while one was open for 0% of the time, Pallas kernels for 33%

profile of v4, /device:TPU:0, one launch (start us, length us, event | category | flops | bytes accessed | tf_op | source)
XLA Modules:
  0.0 21.6 jit_solution(17843493792269464709)
XLA Ops:
  0.6 1.5 %shard_map.111 = (f32[88,128]{1,0:T(8,128)S(1)}, f32[88,128]{1,0:T(8,128)S(1)}, f32[2,8,8,128]{3,2,1,0:T(8,128)S(1)}, f32[2,8,8,128]{3,2,1,0:T(8,128)S(1)}, f32[...) custom-call(f32[2,8,8,128]{3,2,1,0:T(8,128)} %refs_0_.1, ...), custom_call_target="tpu_custom_call" | custom-call | tf_op jit(solution)/shard_map/pallas_call | solution.py:988
  2.2 0.5 %collective-permute-start = (f32[88,128]{1,0:T(8,128)S(1)}, f32[88,128]{1,0:T(8,128)S(1)}, u32[]{:S(2)}, u32[]{:S(2)}) collective-permute-start(f32[88,128]{1,0:T(8,128)S(1)} %get-tuple-element.40), channel_id=1, source_target_pairs={{0,1},{1,0},{2,3},{3,2},{4,5},{5,4},{6,7},{7,6},{8,9},{9,8},{10,11... | collective-permute-start | bytes 135176 | tf_op jit(solution)/shard_map/ppermute | solution.py:1018
  2.7 2.6 %collective-permute-start.1 = (f32[88,128]{1,0:T(8,128)S(1)}, f32[88,128]{1,0:T(8,128)S(1)}, u32[]{:S(2)}, u32[]{:S(2)}) collective-permute-start(f32[88,128]{1,0:T(8,128)S(1)} %get-tuple-element.41), channel_id=1, source_target_pairs={{0,8},{1,2},{2,1},{3,4},{4,3},{5,6},{6,5},{7,15},{8,0},{9,10},{10,... | collective-permute-start | bytes 135176 | tf_op jit(solution)/shard_map/ppermute | solution.py:1019
  5.3 3.4 %shard_map.112 = (f32[128,512]{1,0:T(8,128)S(1)}, f32[128,512]{1,0:T(8,128)S(1)}, f32[4,8,8,128]{3,2,1,0:T(8,128)S(1)}, f32[2,8,8,128]{3,2,1,0:T(8,128)S(1)}, s3...) custom-call(f32[128,512]{1,0:T(8,128)} %far_shell.1, f32[128,512]{1,0:T(8,128)} %far_speed.1, ...), custom_call_target="tpu_custom_call" | custom-call | tf_op jit(solution)/shard_map/pallas_call | solution.py:988
  8.7 0.0 collective-permute-done.first.refs_6_
  8.7 0.0 collective-permute-done.1.second.refs_7_
  8.7 0.7 %shard_map.113 = (f32[144,128]{1,0:T(8,128)S(1)}, f32[24,128]{1,0:T(8,128)S(1)}, f32[144,128]{1,0:T(8,128)S(1)}, f32[48,128]{1,0:T(8,128)S(1)}, f32[128,128]{1,0:T(8,128)S(1)}, /*index=5*/f32[128,128]{1,0:T(8,128)S(1)}) custom-call(f32[2,8,8,128]{3,2,1,0:T(8,128)S(1)} %get-tuple-element.32.disp.refs_0_, f32[2,8,8,128]{3,2,1,0:T(8,128)S(1)} %get-tuple-element.33.vel.refs_1_, ...), custom_call_target="tpu_custom_call" | custom-call | tf_op jit(solution)/shard_map/pallas_call | solution.py:988
  9.4 0.7 %collective-permute-start.2 = (f32[144,128]{1,0:T(8,128)S(1)}, f32[144,128]{1,0:T(8,128)S(1)}, u32[]{:S(2)}, u32[]{:S(2)}) collective-permute-start(f32[144,128]{1,0:T(8,128)S(1)} %get-tuple-element.57), channel_id=1, source_target_pairs={{0,8},{8,0},{16,24},{24,16},{1,9},{9,1},{17,25},{25,17},{2,10},{10... | collective-permute-start | bytes 221192 | tf_op jit(solution)/shard_map/ppermute | solution.py:1068
  10.1 2.4 %collective-permute-start.4 = (f32[144,128]{1,0:T(8,128)S(1)}, f32[144,128]{1,0:T(8,128)S(1)}, u32[]{:S(2)}, u32[]{:S(2)}) collective-permute-start(f32[144,128]{1,0:T(8,128)S(1)} %get-tuple-element.59), channel_id=1, source_target_pairs={{0,24},{8,16},{16,8},{24,0},{1,25},{9,17},{17,9},{25,1},{2,26},{10... | collective-permute-start | bytes 221192 | tf_op jit(solution)/shard_map/ppermute | solution.py:1068
  12.4 0.5 %collective-permute-start.3 = (f32[24,128]{1,0:T(8,128)S(1)}, f32[24,128]{1,0:T(8,128)S(1)}, u32[]{:S(2)}, u32[]{:S(2)}) collective-permute-start(f32[24,128]{1,0:T(8,128)S(1)} %get-tuple-element.58), channel_id=1, source_target_pairs={{0,16},{8,24},{16,0},{24,8},{1,17},{9,25},{17,1},{25,9},{2,18},{10... | collective-permute-start | bytes 36872 | tf_op jit(solution)/shard_map/ppermute | solution.py:1068
  13.0 3.7 %shard_map.114 = (f32[4,7,7,16,128]{4,3,2,1,0:T(8,128)S(1)}, f32[44,7,8,128]{3,2,1,0:T(8,128)S(1)}, f32[44,7,8,128]{3,2,1,0:T(8,128)S(1)}, f32[2,88,128]{2,1,0:T...) custom-call(f32[2,8,8,128]{3,2,1,0:T(8,128)S(1)} %get-tuple-element.32.disp.refs_, ...), custom_call_target="tpu_custom_call" | custom-call | tf_op jit(solution)/shard_map/pallas_call | solution.py:988
  16.7 0.0 collective-permute-done.3.refs_21_
  16.7 0.0 collective-permute-done.2.refs_20_
  16.7 0.0 collective-permute-done.4.refs_22_
  16.7 4.9 %shard_map.115 = (f32[2,8,8,128]{3,2,1,0:T(8,128)}, f32[2,8,8,128]{3,2,1,0:T(8,128)}, f32[128,512]{1,0:T(8,128)}, f32[128,512]{1,0:T(8,128)}) custom-call(f32[2,8,8,128]{3,2,1,0:T(8,128)S(1)} %get-tuple-element.32.disp.refs_0_, f32[2,8,8,128]{3,2,1,0:T(8,128)S(1)} %get-tuple-element.33.vel.refs_1_, s32[8,128]{1,0:T(8,128)S(1)} %get-tuple-element.34.node.refs_2_, ...), custom_call_target="tpu_custom_call" | custom-call | tf_op jit(solution)/shard_map/pallas_call | solution.py:988
Async XLA Ops:
  2.2 6.5 %collective-permute-start = (f32[88,128]{1,0:T(8,128)S(1)}, f32[88,128]{1,0:T(8,128)S(1)}, u32[]{:S(2)}, u32[]{:S(2)}) collective-permute-start(f32[88,128]{1,0:T(8,128)S(1)} %get-tuple-element.40), channel_id=1, source_target_pairs={{0,1},{1,0},{2,3},{3,2},{4,5},{5,4},{6,7},{7,6},{8,9},{9,8},{10,11... | collective-permute-start | bytes 135176 | tf_op jit(solution)/shard_map/ppermute | solution.py:1018
  2.7 6.0 %collective-permute-start.1 = (f32[88,128]{1,0:T(8,128)S(1)}, f32[88,128]{1,0:T(8,128)S(1)}, u32[]{:S(2)}, u32[]{:S(2)}) collective-permute-start(f32[88,128]{1,0:T(8,128)S(1)} %get-tuple-element.41), channel_id=1, source_target_pairs={{0,8},{1,2},{2,1},{3,4},{4,3},{5,6},{6,5},{7,15},{8,0},{9,10},{10,... | collective-permute-start | bytes 135176 | tf_op jit(solution)/shard_map/ppermute | solution.py:1019
  9.4 7.3 %collective-permute-start.2 = (f32[144,128]{1,0:T(8,128)S(1)}, f32[144,128]{1,0:T(8,128)S(1)}, u32[]{:S(2)}, u32[]{:S(2)}) collective-permute-start(f32[144,128]{1,0:T(8,128)S(1)} %get-tuple-element.57), channel_id=1, source_target_pairs={{0,8},{8,0},{16,24},{24,16},{1,9},{9,1},{17,25},{25,17},{2,10},{10... | collective-permute-start | bytes 221192 | tf_op jit(solution)/shard_map/ppermute | solution.py:1068
  10.1 6.6 %collective-permute-start.4 = (f32[144,128]{1,0:T(8,128)S(1)}, f32[144,128]{1,0:T(8,128)S(1)}, u32[]{:S(2)}, u32[]{:S(2)}) collective-permute-start(f32[144,128]{1,0:T(8,128)S(1)} %get-tuple-element.59), channel_id=1, source_target_pairs={{0,24},{8,16},{16,8},{24,0},{1,25},{9,17},{17,9},{25,1},{2,26},{10... | collective-permute-start | bytes 221192 | tf_op jit(solution)/shard_map/ppermute | solution.py:1068
  12.4 4.2 %collective-permute-start.3 = (f32[24,128]{1,0:T(8,128)S(1)}, f32[24,128]{1,0:T(8,128)S(1)}, u32[]{:S(2)}, u32[]{:S(2)}) collective-permute-start(f32[24,128]{1,0:T(8,128)S(1)} %get-tuple-element.58), channel_id=1, source_target_pairs={{0,16},{8,24},{16,0},{24,8},{1,17},{9,25},{17,1},{25,9},{2,18},{10... | collective-permute-start | bytes 36872 | tf_op jit(solution)/shard_map/ppermute | solution.py:1068

commit v5 on v4

--- a/solution.py
+++ b/solution.py
@@ -273,11 +273,13 @@
 
 def narrow(block_of, tiles):
     lane, sub = lanes(), subs()
-    out = []
+    out, sums = [], {}
     for b in tiles:
-        held = block_of(b // 2)
-        held = held + turn(held, -1)
-        held = held + turn(held, -2)
+        if b // 2 not in sums:
+            held = block_of(b // 2)
+            held = held + turn(held, -1)
+            sums[b // 2] = held + turn(held, -2)
+        held = sums[b // 2]
         picked = pick_lanes(held, 64 * (b % 2) + SPLIT * (lane % TILE_Y))
         out.append(jnp.sum(jnp.where(sub == lane // TILE_Y, picked, 0.0), axis=0, keepdims=True))
     return out
@@ -401,17 +403,16 @@
             (
                 (far_shell, shell),
                 (far_speed, speed),
-                (far_shell, tall.at[span, pl.ds(0, cols)]),
-                (far_speed, tall_v.at[span, pl.ds(0, cols)]),
+                (far_shell, tall.at[span]),
+                (far_speed, tall_v.at[span]),
             )
         )
     ]
     for copy in copies:
         copy.start()
     for ref in (tall, tall_v):
-        ref[0:PAD, :] = jnp.zeros((PAD, WIDE), F32)
-        ref[PAD + rows :, :] = jnp.zeros((PAD, WIDE), F32)
-        ref[PAD : PAD + rows, cols:WIDE] = jnp.zeros((rows, PTS), F32)
+        ref[0:PAD, :] = jnp.zeros((PAD, cols), F32)
+        ref[PAD + rows :, :] = jnp.zeros((PAD, cols), F32)
 
     for f in range(2):
         rest = [jit[f, a] for a in range(rows_a)]
@@ -444,29 +445,49 @@
                 before[s] = word
 
     numbers = node[...].astype(F32)
-    for j, block in enumerate(widen(lambda b: numbers[b : b + 1], cols // PTS)):
-        lay_out(wide_ref, (), j, block)
+    node_row = jnp.floor(numbers * (1.0 / place.width))
+    node_col = numbers - node_row * place.width - (place.gy * cols).astype(F32)
+    node_row = node_row - (place.gx * rows).astype(F32)
+    at_row = widen(lambda b: node_row[b : b + 1], cols // PTS)
+    at_col = jnp.concatenate(widen(lambda b: node_col[b : b + 1], cols // PTS), axis=1)
+    col = lax.broadcasted_iota(I32, (8, cols), 1)
+    split = col & (SPLIT - 1)
+    near_row = jnp.concatenate(at_row, axis=1)
+    near_row = jnp.where(split < SPLIT // 2, turn(near_row, SPLIT), turn(near_row, -SPLIT))
+    for j, block in enumerate(at_row):
+        lay_out(wide_ref, (0,), j, block)
+        lay_out(wide_ref, (1,), j, near_row[:, j * PTS : (j + 1) * PTS])
     for copy in copies:
         copy.wait()
     sub_wide = lax.broadcasted_iota(I32, (8, cols), 0)
-    ahead = jnp.zeros((8, cols), F32)
-    met = jnp.zeros((8, cols), F32)
+    row_wide = sub_wide.astype(F32)
+    square = STEP_DT * STEP_DT * BEND
+    sums = [jnp.zeros((8, cols), F32)] * 5
     for part in place.parts():
-        soon = jnp.zeros((8, cols), F32)
-        now = jnp.zeros((8, cols), F32)
+        found = [jnp.zeros((8, cols), F32)] * 5
         band = place.band_of(part[0])
         for row in part:
             at = PAD + row
-            hit = wide_ref[band] == place.nodes(row, cols)
-            bending = bending_of(lambda o: tall[at + o : at + o + 8, :])[:, 0:cols]
-            here = tall[at : at + 8, 0:cols]
-            later = here + STEP_DT * (tall_v[at : at + 8, 0:cols] - (STEP_DT * BEND) * bending)
-            soon = soon + jnp.where(hit, later, 0.0)
-            if 0 <= row < rows:
-                now = now + jnp.where(hit, here, 0.0)
-        ahead = ahead + jnp.where(sub_wide == band, jnp.sum(soon, axis=0, keepdims=True), 0.0)
-        if 0 <= part[0] < rows:
-            met = met + jnp.where(sub_wide == band, jnp.sum(now, axis=0, keepdims=True), 0.0)
+            here = tall[at : at + 8, :]
+            one = tall[at - 1 : at + 7, :] + tall[at + 1 : at + 9, :]
+            two = tall[at - 2 : at + 6, :] + tall[at + 2 : at + 10, :]
+            beside = 2.0 * one - 8.0 * here
+            later = here + STEP_DT * tall_v[at : at + 8, :] - square * (two - 8.0 * one + 20.0 * here)
+            hit = wide_ref[0, band] == row_wide + float(row)
+            near = wide_ref[1, band] == row_wide + float(row)
+            picks = ((hit, later), (hit, beside), (hit, here), (near, beside), (near, here))
+            found = [x + jnp.where(mask, value, 0.0) for x, (mask, value) in zip(found, picks)]
+        sums = [
+            x + jnp.where(sub_wide == band, jnp.sum(y, axis=0, keepdims=True), 0.0) for x, y in zip(sums, found)
+        ]
+    later, beside, here, beside_near, here_near = sums
+    spread = jnp.where(split < 3, turn(beside, -1), turn(beside_near, -1)) * (col < cols - 1).astype(F32)
+    spread += jnp.where(split > 0, turn(beside, 1), turn(beside_near, 1)) * (col > 0).astype(F32)
+    spread += jnp.where(split < 2, turn(here, -2), turn(here_near, -2)) * (col < cols - 2).astype(F32)
+    spread += jnp.where(split > 1, turn(here, 2), turn(here_near, 2)) * (col > 1).astype(F32)
+    hit = at_col == col.astype(F32)
+    ahead = jnp.where(hit, later - square * spread, 0.0)
+    met = jnp.where(hit, here, 0.0)
     for base, values in ((0, ahead), (tiles, met)):
         for b, row in enumerate(narrow(lambda j: values[:, j * PTS : (j + 1) * PTS], range(tiles))):
             shore[base + b : base + b + 1, :] = row
@@ -678,8 +699,8 @@
     ends = refs[20 : 20 + len(shifts)]
     targets = refs[20 + len(shifts) : 24 + len(shifts)]
     scratch = refs[24 + len(shifts) :]
-    out_disp, out_vel, out_shell, out_speed, gaps, halo, rim, rim_v, panes, fasts, pushed, ewin, ewords = scratch[:13]
-    eweights, elevels, flat, flat2, seams, kinds, swin, sems = scratch[13:]
+    out_disp, out_vel, out_shell, out_speed, gaps, halo, rim, rim_v, panes, fasts, hits, goals, ewin, ewords = scratch[:14]
+    eweights, elevels, flat, flat2, seams, kinds, swin, sems = scratch[14:]
     outs = (out_disp, out_vel, out_shell, out_speed)
     copies = [pltpu.make_async_copy(x, y, sems.at[n]) for n, (x, y) in enumerate(zip(outs, targets))]
     rows_a, tiles = disp.shape[1], disp.shape[2]
@@ -748,9 +769,9 @@
             bending = bending_of(lambda o: rim[end, at + o : at + o + 8, :])
             steady = rim_v[end, at - 8 : at, :] - (STEP_DT * BEND) * bending
         band = place.band_of(row)
-        hit = gaps[0, band] == place.nodes(row, WIDE)
-        push = jnp.where(hit, PENALTY * jnp.maximum(gaps[1, band] - here, 0.0), 0.0)
-        fast = steady + STEP_DT * push
+        hit = jnp.where(gaps[0, band] == place.nodes(row, WIDE), STEP_DT * PENALTY, 0.0)
+        push = hit * jnp.maximum(gaps[1, band] - here, 0.0)
+        fast = steady + push
         keep = inside
         if n < 0:
             keep = inside * jnp.where(place.gx > 0, 1.0, 0.0)
@@ -762,7 +783,8 @@
                 panes[n - part, 8 + 8 * part : 16 + 8 * part, :] = there
         if 0 <= n < blocks:
             fasts[n] = fast[:, 0:cols]
-            pushed[n] = push[:, 0:cols]
+            hits[n] = hit[:, 0:cols]
+            goals[n] = gaps[2, band, :, 0:cols] - STEP_DT * push[:, 0:cols]
 
     lane, sub = lanes(), subs()
     west, east = place.gy == 0, place.gy == place.ny - 1
@@ -923,12 +945,9 @@
     def second_rows(n):
         row = pl.multiple_of(8 * n, 8)
         here = panes[n, 8:16, 0:cols]
-        band = place.band_of(row)
-        hit = gaps[0, band, :, 0:cols] == place.nodes(row, cols)
-        gap = gaps[2, band, :, 0:cols] - square * pushed[n]
-        push = jnp.where(hit, PENALTY * jnp.maximum(gap - here, 0.0), 0.0)
+        push = hits[n] * jnp.maximum(goals[n] - here, 0.0)
         bending = bending_of(lambda o: panes[n, 8 + o : 16 + o, :])[:, 0:cols]
-        fast = fasts[n] + STEP_DT * (push - BEND * bending)
+        fast = fasts[n] + push - (STEP_DT * BEND) * bending
         out_speed[pl.ds(row, 8), :] = fast
         out_shell[pl.ds(row, 8), :] = here + STEP_DT * fast
 
@@ -1001,7 +1020,7 @@
         return [jax.ShapeDtypeStruct(x.shape, x.dtype) for x in arrays]
 
     wide = pltpu.VMEM((TILE_X, 8, cols), F32)
-    tall = pltpu.VMEM((rows + 2 * PAD, WIDE), F32)
+    tall = pltpu.VMEM((rows + 2 * PAD, cols), F32)
     edges = pltpu.VMEM((2, rows, PTS), F32)
     far_shell, far_speed = shell, speed
     small = (disp, vel, jit, words, node, inter)
@@ -1036,7 +1055,7 @@
             shaped(9, 2, 8, dtype=I32),
             shaped(2 * disp.shape[2]),
         ],
-        [tall, tall, wide, pltpu.SemaphoreType.DMA((4,))],
+        [tall, tall, pltpu.VMEM((2, TILE_X, 8, cols), F32), pltpu.SemaphoreType.DMA((4,))],
         far_shell,
         far_speed,
         disp,
@@ -1102,6 +1121,7 @@
         pltpu.VMEM((2, 32, WIDE), F32),
         pltpu.VMEM((2, 16, WIDE), F32),
         pltpu.VMEM((blocks, 24, WIDE), F32),
+        pltpu.VMEM((blocks, 8, cols), F32),
         pltpu.VMEM((blocks, 8, cols), F32),
         pltpu.VMEM((blocks, 8, cols), F32),
         pltpu.VMEM((4, len(SIDEWAYS), 2, 16, PTS), F32),

time: 21.8 us -> 20.9 us (0.959)
  Pallas kernels: 14.2 us -> 13.3 us
    pallas_call x5, Pallas kernels: 14.2 us -> 13.3 us  [call(): pl.pallas_call(body, out_shape=out, in_specs=specs, scratch_shapes=scratc...]
  transfers between devices with their start and end apart: 5 -> 5, of which waited for: 0 -> 0; matrix products, arithmetic and copies ran while one was open for 0% -> 0% of each run, Pallas kernels for 33% -> 30%
where the time goes in v5:
time: 20.9 us; the launch traced here: 20.7 us
  Pallas kernels  13.3 us (64%)
  starting transfers between devices  6.64 us (32%)
  between operations  0.7 us (3%)
    pallas_call x5, Pallas kernels, call(): pl.pallas_call(body, out_shape=out, in_specs=specs, scratch_shapes=scratc...  13.3 us
    ppermute x3, starting transfers between devices, on_device(): lax.ppermute(e, 'gx', [(i, i ^ s) for i in range(nx)])  3.55 us
    ppermute x1, starting transfers between devices, on_device(): lax.ppermute(second, ('gx', 'gy'), [(i * ny + j, i * ny + (j - 1 ^ 1) + 1...  2.56 us
    ppermute x1, starting transfers between devices, on_device(): first = lax.ppermute(first, 'gy', [(i, i ^ 1) for i in range(ny)])  0.52 us
  transfers between devices with their start and end apart: 5, of which 0 were waited for; matrix products, arithmetic and copies ran while one was open for 0% of the time, Pallas kernels for 30%

profile of v5, /device:TPU:0, one launch (start us, length us, event | category | flops | bytes accessed | tf_op | source)
XLA Modules:
  0.0 20.7 jit_solution(6879044535556695214)
XLA Ops:
  0.6 1.5 %shard_map.111 = (f32[88,128]{1,0:T(8,128)S(1)}, f32[88,128]{1,0:T(8,128)S(1)}, f32[2,8,8,128]{3,2,1,0:T(8,128)S(1)}, f32[2,8,8,128]{3,2,1,0:T(8,128)S(1)}, f32[...) custom-call(f32[2,8,8,128]{3,2,1,0:T(8,128)} %refs_0_.1, ...), custom_call_target="tpu_custom_call" | custom-call | tf_op jit(solution)/shard_map/pallas_call | solution.py:1007
  2.2 0.5 %collective-permute-start = (f32[88,128]{1,0:T(8,128)S(1)}, f32[88,128]{1,0:T(8,128)S(1)}, u32[]{:S(2)}, u32[]{:S(2)}) collective-permute-start(f32[88,128]{1,0:T(8,128)S(1)} %get-tuple-element.40), channel_id=1, source_target_pairs={{0,1},{1,0},{2,3},{3,2},{4,5},{5,4},{6,7},{7,6},{8,9},{9,8},{10,11... | collective-permute-start | bytes 135176 | tf_op jit(solution)/shard_map/ppermute | solution.py:1037
  2.7 2.6 %collective-permute-start.1 = (f32[88,128]{1,0:T(8,128)S(1)}, f32[88,128]{1,0:T(8,128)S(1)}, u32[]{:S(2)}, u32[]{:S(2)}) collective-permute-start(f32[88,128]{1,0:T(8,128)S(1)} %get-tuple-element.41), channel_id=1, source_target_pairs={{0,8},{1,2},{2,1},{3,4},{4,3},{5,6},{6,5},{7,15},{8,0},{9,10},{10,... | collective-permute-start | bytes 135176 | tf_op jit(solution)/shard_map/ppermute | solution.py:1038
  5.3 2.6 %shard_map.112 = (f32[128,512]{1,0:T(8,128)S(1)}, f32[128,512]{1,0:T(8,128)S(1)}, f32[4,8,8,128]{3,2,1,0:T(8,128)S(1)}, f32[2,8,8,128]{3,2,1,0:T(8,128)S(1)}, s3...) custom-call(f32[128,512]{1,0:T(8,128)} %far_shell.1, f32[128,512]{1,0:T(8,128)} %far_speed.1, ...), custom_call_target="tpu_custom_call" | custom-call | tf_op jit(solution)/shard_map/pallas_call | solution.py:1007
  7.8 0.0 collective-permute-done.first.refs_6_
  7.9 0.0 collective-permute-done.1.second.refs_7_
  7.9 0.7 %shard_map.113 = (f32[144,128]{1,0:T(8,128)S(1)}, f32[24,128]{1,0:T(8,128)S(1)}, f32[144,128]{1,0:T(8,128)S(1)}, f32[48,128]{1,0:T(8,128)S(1)}, f32[128,128]{1,0:T(8,128)S(1)}, /*index=5*/f32[128,128]{1,0:T(8,128)S(1)}) custom-call(f32[2,8,8,128]{3,2,1,0:T(8,128)S(1)} %get-tuple-element.32.disp.refs_0_, f32[2,8,8,128]{3,2,1,0:T(8,128)S(1)} %get-tuple-element.33.vel.refs_1_, ...), custom_call_target="tpu_custom_call" | custom-call | tf_op jit(solution)/shard_map/pallas_call | solution.py:1007
  8.6 1.5 %collective-permute-start.2 = (f32[144,128]{1,0:T(8,128)S(1)}, f32[144,128]{1,0:T(8,128)S(1)}, u32[]{:S(2)}, u32[]{:S(2)}) collective-permute-start(f32[144,128]{1,0:T(8,128)S(1)} %get-tuple-element.57), channel_id=1, source_target_pairs={{0,8},{8,0},{16,24},{24,16},{1,9},{9,1},{17,25},{25,17},{2,10},{10... | collective-permute-start | bytes 221192 | tf_op jit(solution)/shard_map/ppermute | solution.py:1087
  10.1 1.5 %collective-permute-start.4 = (f32[144,128]{1,0:T(8,128)S(1)}, f32[144,128]{1,0:T(8,128)S(1)}, u32[]{:S(2)}, u32[]{:S(2)}) collective-permute-start(f32[144,128]{1,0:T(8,128)S(1)} %get-tuple-element.59), channel_id=1, source_target_pairs={{0,24},{8,16},{16,8},{24,0},{1,25},{9,17},{17,9},{25,1},{2,26},{10... | collective-permute-start | bytes 221192 | tf_op jit(solution)/shard_map/ppermute | solution.py:1087
  11.6 0.5 %collective-permute-start.3 = (f32[24,128]{1,0:T(8,128)S(1)}, f32[24,128]{1,0:T(8,128)S(1)}, u32[]{:S(2)}, u32[]{:S(2)}) collective-permute-start(f32[24,128]{1,0:T(8,128)S(1)} %get-tuple-element.58), channel_id=1, source_target_pairs={{0,16},{8,24},{16,0},{24,8},{1,17},{9,25},{17,1},{25,9},{2,18},{10... | collective-permute-start | bytes 36872 | tf_op jit(solution)/shard_map/ppermute | solution.py:1087
  12.1 3.7 %shard_map.114 = (f32[4,7,7,16,128]{4,3,2,1,0:T(8,128)S(1)}, f32[44,7,8,128]{3,2,1,0:T(8,128)S(1)}, f32[44,7,8,128]{3,2,1,0:T(8,128)S(1)}, f32[2,88,128]{2,1,0:T...) custom-call(f32[2,8,8,128]{3,2,1,0:T(8,128)S(1)} %get-tuple-element.32.disp.refs_, ...), custom_call_target="tpu_custom_call" | custom-call | tf_op jit(solution)/shard_map/pallas_call | solution.py:1007
  15.8 0.0 collective-permute-done.3.refs_21_
  15.9 0.0 collective-permute-done.2.refs_20_
  15.9 0.0 collective-permute-done.4.refs_22_
  15.9 4.8 %shard_map.115 = (f32[2,8,8,128]{3,2,1,0:T(8,128)}, f32[2,8,8,128]{3,2,1,0:T(8,128)}, f32[128,512]{1,0:T(8,128)}, f32[128,512]{1,0:T(8,128)}) custom-call(f32[2,8,8,128]{3,2,1,0:T(8,128)S(1)} %get-tuple-element.32.disp.refs_0_, f32[2,8,8,128]{3,2,1,0:T(8,128)S(1)} %get-tuple-element.33.vel.refs_1_, s32[8,128]{1,0:T(8,128)S(1)} %get-tuple-element.34.node.refs_2_, ...), custom_call_target="tpu_custom_call" | custom-call | tf_op jit(solution)/shard_map/pallas_call | solution.py:1007
Async XLA Ops:
  2.2 5.7 %collective-permute-start = (f32[88,128]{1,0:T(8,128)S(1)}, f32[88,128]{1,0:T(8,128)S(1)}, u32[]{:S(2)}, u32[]{:S(2)}) collective-permute-start(f32[88,128]{1,0:T(8,128)S(1)} %get-tuple-element.40), channel_id=1, source_target_pairs={{0,1},{1,0},{2,3},{3,2},{4,5},{5,4},{6,7},{7,6},{8,9},{9,8},{10,11... | collective-permute-start | bytes 135176 | tf_op jit(solution)/shard_map/ppermute | solution.py:1037
  2.7 5.2 %collective-permute-start.1 = (f32[88,128]{1,0:T(8,128)S(1)}, f32[88,128]{1,0:T(8,128)S(1)}, u32[]{:S(2)}, u32[]{:S(2)}) collective-permute-start(f32[88,128]{1,0:T(8,128)S(1)} %get-tuple-element.41), channel_id=1, source_target_pairs={{0,8},{1,2},{2,1},{3,4},{4,3},{5,6},{6,5},{7,15},{8,0},{9,10},{10,... | collective-permute-start | bytes 135176 | tf_op jit(solution)/shard_map/ppermute | solution.py:1038
  8.6 7.3 %collective-permute-start.2 = (f32[144,128]{1,0:T(8,128)S(1)}, f32[144,128]{1,0:T(8,128)S(1)}, u32[]{:S(2)}, u32[]{:S(2)}) collective-permute-start(f32[144,128]{1,0:T(8,128)S(1)} %get-tuple-element.57), channel_id=1, source_target_pairs={{0,8},{8,0},{16,24},{24,16},{1,9},{9,1},{17,25},{25,17},{2,10},{10... | collective-permute-start | bytes 221192 | tf_op jit(solution)/shard_map/ppermute | solution.py:1087
  10.1 5.8 %collective-permute-start.4 = (f32[144,128]{1,0:T(8,128)S(1)}, f32[144,128]{1,0:T(8,128)S(1)}, u32[]{:S(2)}, u32[]{:S(2)}) collective-permute-start(f32[144,128]{1,0:T(8,128)S(1)} %get-tuple-element.59), channel_id=1, source_target_pairs={{0,24},{8,16},{16,8},{24,0},{1,25},{9,17},{17,9},{25,1},{2,26},{10... | collective-permute-start | bytes 221192 | tf_op jit(solution)/shard_map/ppermute | solution.py:1087
  11.6 4.2 %collective-permute-start.3 = (f32[24,128]{1,0:T(8,128)S(1)}, f32[24,128]{1,0:T(8,128)S(1)}, u32[]{:S(2)}, u32[]{:S(2)}) collective-permute-start(f32[24,128]{1,0:T(8,128)S(1)} %get-tuple-element.58), channel_id=1, source_target_pairs={{0,16},{8,24},{16,0},{24,8},{1,17},{9,25},{17,1},{25,9},{2,18},{10... | collective-permute-start | bytes 36872 | tf_op jit(solution)/shard_map/ppermute | solution.py:1087

commit v6 on v5

--- a/solution.py
+++ b/solution.py
@@ -81,59 +81,10 @@
     return masks, bits
 
 
-def moved(get, oy, masks):
-    out = {}
-    for dx in (-1, 0, 1):
-        held = get(dx, 0)
-        if oy:
-            held = turn(jnp.where(masks["col_at", oy], get(dx, sign(oy)), held), -oy)
-        out[dx] = held
-    return out
-
-
 def across(cells, ox, masks):
     if not ox:
         return cells[0]
     return turn(jnp.where(masks["row_at", ox], cells[sign(ox)], cells[0]), -TILE_Y * ox)
-
-
-def first_forces(get_jx, get_jy, get_dx, get_dy, get_words, keep=None, both=True):
-    masks, bits = lane_masks()
-    jx0, jy0, dx0, dy0 = get_jx(0, 0), get_jy(0, 0), get_dx(0, 0), get_dy(0, 0)
-    fx = jnp.zeros((8, PTS), F32)
-    fy = jnp.zeros((8, PTS), F32)
-    for oy in SIDEWAYS:
-        jxs, jys = moved(get_jx, oy, masks), moved(get_jy, oy, masks)
-        dxs, dys = moved(get_dx, oy, masks), moved(get_dy, oy, masks)
-        words = {}
-        for dx in (-1, 0, 1):
-            words[dx] = get_words(dx, 0)
-            if oy:
-                words[dx] = jnp.where(masks["col_from", oy], get_words(dx, sign(oy)), words[dx])
-        for number, (ox, other) in enumerate(OFFSETS):
-            if other != oy:
-                continue
-            word = words[0]
-            if ox:
-                word = jnp.where(masks["row_from", ox], words[sign(ox)], word)
-            intact = (word & bits[ox]) != 0
-            rest_x = across(jxs, ox, masks) - (jx0 - float(ox))
-            rest_y = across(jys, ox, masks) - (jy0 - float(oy))
-            now_x = across(dxs, ox, masks) - (dx0 - float(ox))
-            now_y = across(dys, ox, masks) - (dy0 - float(oy))
-            rest_sq = rest_x * rest_x + rest_y * rest_y + DELTA_SQ
-            now_sq = now_x * now_x + now_y * now_y + DELTA_SQ
-            rest_inv = lax.rsqrt(rest_sq)
-            reach = jnp.maximum(1.0 - rest_sq * rest_inv * (1.0 / HORIZON), 0.0)
-            weight = jnp.where(intact, reach * reach, 0.0)
-            level = weight * rest_inv
-            if keep is not None:
-                keep(number, weight, level)
-            factor = level - weight * lax.rsqrt(now_sq)
-            fx = fx + factor * now_x
-            if both:
-                fy = fy + factor * now_y
-    return fx, fy
 
 
 def pick_lanes(block, index):
@@ -390,10 +341,10 @@
 
 def own_parts(place_args, far_shell, far_speed, disp, vel, jit, words, node, *refs):
     place = Place(*place_args)
-    shell, speed, lattice, lead, groups_w, ends_w, shore, tall, tall_v, wide_ref, sems = refs
+    shell, speed, lattice, lead, rows_w, shore, tall, tall_v, wide_ref, sems = refs
     rows_a, tiles = disp.shape[1], disp.shape[2]
     rows, cols = place.shell_rows, place.shell_cols
-    lane, sub = lanes(), subs()
+    lane = lanes()
     west, east = place.gy == 0, place.gy == place.ny - 1
     north, south = place.gx == 0, place.gx == place.nx - 1
     span = pl.ds(PAD, rows)
@@ -414,7 +365,8 @@
         ref[0:PAD, :] = jnp.zeros((PAD, cols), F32)
         ref[PAD + rows :, :] = jnp.zeros((PAD, cols), F32)
 
-    for f in range(2):
+    @pl.loop(0, 2)
+    def _(f):
         rest = [jit[f, a] for a in range(rows_a)]
         whole = [jit[f, a] + disp[f, a] for a in range(rows_a)]
         soon = [x + STEP_DT * vel[f, a] for a, x in enumerate(whole)]
@@ -423,26 +375,21 @@
             lattice[2 + f, a] = y
             lead[f, a] = z
 
-    before = [None] * 9
-    for a in range(rows_a):
+    @pl.loop(0, rows_a)
+    def _(a):
         packed = words[a]
         for dx in (-1, 0, 1):
             for dy in (-1, 0, 1):
-                s = slot(dx, dy)
-                word = word_row(packed, s)
+                word = word_row(packed, slot(dx, dy))
                 if dy < 0:
                     word = jnp.where((lane < TILE_Y) & west, 0, word)
                 if dy > 0:
                     word = jnp.where((lane >= PTS - TILE_Y) & east, 0, word)
-                if dx < 0 and a == 0:
-                    word = jnp.where(north, 0, word)
-                if dx > 0 and a == rows_a - 1:
-                    word = jnp.where(south, 0, word)
-                if a:
-                    groups_w[s, a - 1] = jnp.where(sub < TILE_X - FROM, before[s], word)
-                if a in (0, rows_a - 1):
-                    ends_w[s, min(a, 1)] = word
-                before[s] = word
+                if dx < 0:
+                    word = jnp.where((a == 0) & north, 0, word)
+                if dx > 0:
+                    word = jnp.where((a == rows_a - 1) & south, 0, word)
+                rows_w[slot(dx, dy), a] = word
 
     numbers = node[...].astype(F32)
     node_row = jnp.floor(numbers * (1.0 / place.width))
@@ -493,8 +440,8 @@
             shore[base + b : base + b + 1, :] = row
 
 
-HALO_ROWS = 120
-CONTACT_ROWS = 24
+ROWS_AT, LEAD_AT, SIDE_AT, WORD_AT, SHELL_AT, HALO_ROWS = 2, 26, 32, 42, 50, 80
+CONTACT_ROWS, OWN_ROWS = 18, 24
 
 
 def shell_strip(right, left, at):
@@ -503,7 +450,7 @@
 
 
 def pack_ends(
-    place_args, shifts, disp, vel, jit, words, node, inter, shell, speed, lattice, ends_w, shore, first, second, *refs
+    place_args, shifts, disp, vel, jit, words, node, inter, shell, speed, lattice, lead, rows_w, shore, first, second, *refs
 ):
     place = Place(*place_args)
     outs = refs[: len(shifts)]
@@ -529,14 +476,13 @@
             grid[f, n, 16:24, :] = jnp.zeros((8, PTS), F32)
     force, _ = group_first(
         lambda f, oy, ox: grid[f, SIDEWAYS.index(oy), 8 + ox : 16 + ox, :],
-        lambda s: ends_w[s, 1] if s < 6 else jnp.zeros((8, PTS), I32),
+        lambda s: rows_w[s, last] if s < 6 else jnp.zeros((8, PTS), I32),
         lambda number, weight, level: None,
         start=0,
     )
     gap = disp[0, last] + inter[...]
     own[0:8, :] = gap + STEP_DT * (vel[0, last] + STEP_DT * flip(force))
     own[8:16, :] = gap
-    own[16:24, :] = jnp.zeros((8, PTS), F32)
     own[16:17, :] = right[last : last + 1] + right[65:66]
     own[17:18, :] = left[last : last + 1] + left[65:66]
 
@@ -565,8 +511,7 @@
             hit = wide_ref[band] == place.nodes(row, PTS) + far
             soon = soon + jnp.where(hit, jnp.where(low, from_left, from_right), 0.0)
         ahead = ahead + jnp.where(sub == band, jnp.sum(soon, axis=0, keepdims=True), 0.0)
-    base = CONTACT_ROWS
-    own[base + 16 : base + 24, :] = jnp.zeros((8, PTS), F32)
+    base = OWN_ROWS
     own[base : base + 16, :] = shore[...]
     for b, row in zip((0, tiles - 1), narrow(lambda j: ahead, (0, tiles - 1))):
         own[base + b : base + b + 1, :] = shore[b : b + 1, :] - (STEP_DT * STEP_DT * BEND) * row
@@ -579,17 +524,30 @@
         if shift & (shift + 1) == 0:
             at = HALO_ROWS
             down = (place.gx ^ shift) > place.gx
-            edge = jnp.where(down, rows_a - 1, 0)
-            for f, source in enumerate((disp, disp, vel, vel, jit, jit)):
-                out[8 * f : 8 * f + 8, :] = source[f % 2, edge]
-            out[48:80, :] = jnp.zeros((32, PTS), F32)
-            edge_words = words[edge]
-            out[48:56, 0:9] = (edge_words & 65535).astype(F32)
-            out[56:64, 0:9] = jnp.right_shift(edge_words, 16).astype(F32)
-            for f in range(8):
-                for side, values in ((64, right), (72, left)):
-                    low, high = values[8 * f : 8 * f + 1], values[8 * f + rows_a - 1 : 8 * f + rows_a]
-                    out[side + f : side + f + 1, :] = jnp.where(down, high, low)
+            out[0:ROWS_AT, :] = jnp.zeros((ROWS_AT, PTS), F32)
+            for f in range(4):
+                to = ROWS_AT + 6 * f
+                out[to : to + 6, :] = jnp.where(down, lattice[f, last, 2:8, :], lattice[f, 0, 0:6, :])
+            for f in range(2):
+                to = LEAD_AT + 3 * f
+                out[to : to + 3, :] = jnp.where(down, lead[f, last, 5:8, :], lead[f, 0, 0:3, :])
+
+                def merged(part):
+                    rows_of = [x[8 * part + a : 8 * part + a + 1] for a in (last, 0) for x in (left, right)]
+                    return jnp.where(leftward, jnp.where(down, rows_of[0], rows_of[2]), jnp.where(down, rows_of[1], rows_of[3]))
+
+                rest = merged(4 + f)
+                whole = rest + merged(f)
+                for n, values in enumerate((rest, whole, whole + STEP_DT * merged(2 + f))):
+                    out[SIDE_AT + 2 * n + f : SIDE_AT + 2 * n + f + 1, :] = values
+            for n, values in enumerate((left, right)):
+                for part in range(2):
+                    to, row = SIDE_AT + 6 + 2 * n + part, 48 + 8 * part
+                    out[to : to + 1, :] = jnp.where(down, values[row + last : row + last + 1], values[row : row + 1])
+            out[WORD_AT : WORD_AT + 8, :] = jnp.zeros((8, PTS), F32)
+            edge_words = jnp.where(down, words[last], words[0])
+            out[WORD_AT : WORD_AT + 8, 0:9] = (edge_words & 65535).astype(F32)
+            out[WORD_AT : WORD_AT + 8, 16:25] = jnp.right_shift(edge_words, 16).astype(F32)
             for j in range(WIDE // PTS):
                 cut = slice(j * PTS, (j + 1) * PTS)
                 if j < cols // PTS:
@@ -598,39 +556,44 @@
                 else:
                     d_low, d_high = halo_d[0:4], halo_d[rows - 4 : rows]
                     v_low, v_high = halo_v[0:2], halo_v[rows - 2 : rows]
-                out[80 + 8 * j : 84 + 8 * j, :] = jnp.where(down, d_high, d_low)
-                out[84 + 8 * j : 86 + 8 * j, :] = jnp.where(down, v_high, v_low)
-                out[86 + 8 * j : 88 + 8 * j, :] = jnp.zeros((2, PTS), F32)
+                to = SHELL_AT + 6 * j
+                out[to : to + 4, :] = jnp.where(down, d_high, d_low)
+                out[to + 4 : to + 6, :] = jnp.where(down, v_high, v_low)
         out[at : at + CONTACT_ROWS, :] = mine
 
 
-def inner_rows(place_args, disp, jit, shell, speed, lattice, groups_w, first, second, strip_d, strip_v, *refs):
+def inner_rows(place_args, disp, jit, shell, speed, lattice, rows_w, first, second, strip_d, strip_v, *refs):
     place = Place(*place_args)
-    win, weights, levels, flat, beside, tiles_f, mid, strips, kinds, panes = refs
+    win, weights, levels, flat, beside, mid, strips, kinds, panes, hold, side = refs
     cols = place.shell_cols
     rows_a, tiles = disp.shape[1], disp.shape[2]
     right, left = place.sides(first[...], second[...])
     lane = lanes()
     leftward = (lane & (TILE_Y - 1)) >= TILE_Y // 2
-    side = [jnp.where(leftward, left[8 * f : 8 * f + 8], right[8 * f : 8 * f + 8]) for f in range(6)]
+    for f in range(6):
+        side[f] = jnp.where(leftward, left[8 * f : 8 * f + 8], right[8 * f : 8 * f + 8])
 
     strips[...] = jnp.zeros_like(strips)
-    for f in range(4):
-        rest = jit[f % 2]
-        whole = rest if f < 2 else rest + disp[f % 2]
-        beyond = side[4 + f % 2] if f < 2 else side[4 + f % 2] + side[f % 2]
-        strips[f, 0, 8:16, :] = beyond
-        strips[f, 1, 8:16, :] = whole[:, 0, :]
-        strips[f, 2, 8:16, :] = whole[:, tiles - 1, :]
-        nears = [side_columns(beyond[a : a + 1]) for a in range(rows_a)]
-        for a, near in enumerate(nears):
-            cells = lattice[f, a]
-            for n, oy in enumerate(SIDEWAYS):
-                shifted = sideways(cells, near, oy)
-                if a < rows_a - 1:
-                    win[f, n, a, 0:8, :] = shifted
-                if a > 0:
-                    win[f, n, a - 1, 8:16, :] = shifted
+
+    @pl.loop(0, 2)
+    def _(c):
+        for part in range(2):
+            f = c + 2 * part
+            whole = jit[c] + disp[c] if part else jit[c]
+            beyond = side[4 + c] + side[c] if part else side[4 + c]
+            strips[f, 0, 8:16, :] = beyond
+            strips[f, 1, 8:16, :] = turn(whole[:, 0, :], TILE_Y)
+            strips[f, 2, 8:16, :] = turn(whole[:, tiles - 1, :], -TILE_Y)
+            nears = [side_columns(beyond[a : a + 1]) for a in range(rows_a)]
+            for a, near in enumerate(nears):
+                cells = lattice[f, a]
+                for n, oy in enumerate(SIDEWAYS):
+                    shifted = sideways(cells, near, oy)
+                    if a < rows_a - 1:
+                        win[f, n, a, 0:8, :] = shifted
+                    if a > 0:
+                        win[f, n, a - 1, 8:16, :] = shifted
+
     left_words = joined(left[48:56], left[56:64])
     right_words = joined(right[48:56], right[56:64])
     for s in range(9):
@@ -643,9 +606,11 @@
     flat[...] = jnp.zeros_like(flat)
 
     blocks = mid.shape[0]
+
     for n in range(blocks):
         panes[n, :, 0:cols] = shell[8 * n : 8 * n + 24, :]
         panes[n, :, cols:WIDE] = strip_d[8 * n : 8 * n + 24, :]
+
     each = -(-blocks // (rows_a - 1))
 
     def bend_block(n):
@@ -654,8 +619,57 @@
         mid[n, :, 0:cols] = speed[pl.ds(at, 8), :] - (STEP_DT * BEND) * bending[:, 0:cols]
         mid[n, :, cols:WIDE] = strip_v[pl.ds(at, 8), :] - (STEP_DT * BEND) * bending[:, cols:WIDE]
 
+    hold[...] = jnp.zeros_like(hold)
+    reach_y = len(SIDEWAYS) // 2
+
+    def side_bonds(k):
+        masks, bits = lane_masks()
+        oy = k - reach_y
+        at = jnp.where(oy > 0, 1, jnp.where(oy < 0, 2, 0))
+        towards = jnp.where(oy > 0, 1, jnp.where(oy < 0, -1, 0)) + 1
+        col = lane & (TILE_Y - 1)
+        crossed = (col < oy) | (col >= TILE_Y + oy)
+        crossing = (col >= TILE_Y - oy) | (col < -oy)
+        cells = [
+            {
+                dx: pltpu.roll(
+                    jnp.where(crossed, strips[f, at, 8 + dx : 16 + dx, :], strips[f, 0, 8 + dx : 16 + dx, :]),
+                    (PTS - oy) & (PTS - 1),
+                    1,
+                )
+                for dx in (-1, 0, 1)
+            }
+            for f in range(4)
+        ]
+        words = [jnp.where(crossing, kinds[3 * dx + towards], kinds[3 * dx + 1]) for dx in range(3)]
+        zero = [strips[f, 0, 8:16, :] for f in range(4)]
+        step = oy.astype(F32)
+        base_y, base_v = zero[1] - step, zero[3] - step
+        fx, fy = hold[0], hold[1]
+        for ox in range(-3, 4):
+            word = words[1]
+            if ox:
+                word = jnp.where(masks["row_from", ox], words[sign(ox) + 1], word)
+            rest_x = across(cells[0], ox, masks) - (zero[0] - float(ox))
+            rest_y = across(cells[1], ox, masks) - base_y
+            now_x = across(cells[2], ox, masks) - (zero[2] - float(ox))
+            now_y = across(cells[3], ox, masks) - base_v
+            rest_sq = rest_x * rest_x + rest_y * rest_y + DELTA_SQ
+            now_sq = now_x * now_x + now_y * now_y + DELTA_SQ
+            rest_inv = lax.rsqrt(rest_sq)
+            reach = jnp.maximum(1.0 - rest_sq * rest_inv * (1.0 / HORIZON), 0.0)
+            weight = jnp.where((word & bits[ox]) != 0, reach * reach, 0.0)
+            factor = weight * (rest_inv - lax.rsqrt(now_sq))
+            fx, fy = fx + factor * now_x, fy + factor * now_y
+        hold[0], hold[1] = fx, fy
+
+    if rows_a - 1 != len(SIDEWAYS):
+        pl.loop(0, len(SIDEWAYS))(side_bonds)
+
     @pl.loop(0, rows_a - 1)
     def _(k):
+        if rows_a - 1 == len(SIDEWAYS):
+            side_bonds(k)
         for part in range(each):
             bend_block(jnp.minimum(each * k + part, blocks - 1))
 
@@ -666,39 +680,26 @@
             weights[number, k] = weight
             levels[number, k] = level
 
-        fx, fy = group_first(cell, lambda s: groups_w[s, k], keep)
+        upper = subs() < TILE_X - FROM
+        grouped = [jnp.where(upper, rows_w[s, k], rows_w[s, k + 1]) for s in range(9)]
+        fx, fy = group_first(cell, grouped.__getitem__, keep)
         at = pl.multiple_of(8 * k + 16, 8)
         flat[0, pl.ds(at, 8), :] = fx
         flat[1, pl.ds(at, 8), :] = fy
 
-    def getter(f):
-        held = {}
-
-        def get(dx, dy):
-            if (dx, dy) not in held:
-                held[dx, dy] = turn(strips[f, dy % 3, 8 + dx : 16 + dx, :], TILE_Y * dy)
-            return held[dx, dy]
-
-        return get
-
-    forces = first_forces(getter(0), getter(1), getter(2), getter(3), lambda dx, dy: kinds[slot(dx, dy)])
     for f in range(2):
-        moved_side = side[4 + f] + side[f] + STEP_DT * (side[2 + f] + STEP_DT * forces[f])
+        moved_side = side[4 + f] + side[f] + STEP_DT * (side[2 + f] + STEP_DT * hold[f])
         for a in range(rows_a):
             beside[f, a] = side_columns(moved_side[a : a + 1])
-        for a, cells in enumerate(flips([flat[f, 8 * a + 11 : 8 * a + 19, :] for a in range(1, rows_a - 1)])):
-            tiles_f[f, a + 1] = cells
-        tiles_f[f, 0] = jnp.zeros((8, PTS), F32)
-        tiles_f[f, rows_a - 1] = jnp.zeros((8, PTS), F32)
 
 
 def both_steps(place_args, shifts, *refs):
     place = Place(*place_args)
     disp, vel, node, inter, shell, speed, first, second, own, strip_d, strip_v = refs[:11]
-    lead, ends_w, win, weights, levels, flat_in, beside, tiles_f, mid = refs[11:20]
-    ends = refs[20 : 20 + len(shifts)]
-    targets = refs[20 + len(shifts) : 24 + len(shifts)]
-    scratch = refs[24 + len(shifts) :]
+    lead, rows_w, win, weights, levels, flat_in, beside, mid = refs[11:19]
+    ends = refs[19 : 19 + len(shifts)]
+    targets = refs[19 + len(shifts) : 23 + len(shifts)]
+    scratch = refs[23 + len(shifts) :]
     out_disp, out_vel, out_shell, out_speed, gaps, halo, rim, rim_v, panes, fasts, hits, goals, ewin, ewords = scratch[:14]
     eweights, elevels, flat, flat2, seams, kinds, swin, sems = scratch[14:]
     outs = (out_disp, out_vel, out_shell, out_speed)
@@ -710,7 +711,7 @@
 
     halo[...] = jnp.zeros_like(halo)
     contact = jnp.where(place.front, own[0:CONTACT_ROWS, :], 0.0)
-    owners = own[CONTACT_ROWS:, :]
+    owners = own[OWN_ROWS : OWN_ROWS + CONTACT_ROWS, :]
     for shift, ref in zip(shifts, ends):
         partner = place.gx ^ shift
         at = 0
@@ -741,10 +742,11 @@
         ref[at[0], at[1] : at[1] + 8, :] = zeros
     for j in range(WIDE // PTS):
         cut = slice(j * PTS, (j + 1) * PTS)
-        rim[0, 12:16, cut] = halo[0, 80 + 8 * j : 84 + 8 * j, :]
-        rim_v[0, 6:8, cut] = halo[0, 84 + 8 * j : 86 + 8 * j, :]
-        rim[1, 16:20, cut] = halo[1, 80 + 8 * j : 84 + 8 * j, :]
-        rim_v[1, 8:10, cut] = halo[1, 84 + 8 * j : 86 + 8 * j, :]
+        at = SHELL_AT + 6 * j
+        rim[0, 12:16, cut] = halo[0, at : at + 4, :]
+        rim_v[0, 6:8, cut] = halo[0, at + 4 : at + 6, :]
+        rim[1, 16:20, cut] = halo[1, at : at + 4, :]
+        rim_v[1, 8:10, cut] = halo[1, at + 4 : at + 6, :]
     numbers = node[...].astype(F32)
     node_rows = [numbers[b : b + 1] for b in range(tiles)] + [right[64:65], left[64:65]]
     gap_rows = [contact[8 + b : 9 + b] for b in range(tiles)] + [contact[16:17], contact[17:18]]
@@ -758,33 +760,43 @@
     inside = jnp.where(col < cols, 1.0, 0.0)
     inside = jnp.where((col >= cols) & (col < cols + 64) & (place.gy < place.ny - 1), 1.0, inside)
     inside = jnp.where((col >= cols + 64) & (place.gy > 0), 1.0, inside)
-    for n in range(-1, blocks + 1):
-        row = 8 * n
-        if 0 < n < blocks - 1:
-            here, steady = wide(shell, strip_d, row, 8), mid[n - 1]
-        else:
-            end = 0 if n < 1 else 1
-            at = row + 16 if end == 0 else row - rows + 16
-            here = rim[end, at : at + 8, :]
-            bending = bending_of(lambda o: rim[end, at + o : at + o + 8, :])
-            steady = rim_v[end, at - 8 : at, :] - (STEP_DT * BEND) * bending
-        band = place.band_of(row)
-        hit = jnp.where(gaps[0, band] == place.nodes(row, WIDE), STEP_DT * PENALTY, 0.0)
+
+    def first_rows(n, here, steady, keep=None):
+        band = place.band_of(8 * n)
+        hit = jnp.where(gaps[0, band] == place.nodes(8 * n, WIDE), STEP_DT * PENALTY, 0.0)
         push = hit * jnp.maximum(gaps[1, band] - here, 0.0)
         fast = steady + push
-        keep = inside
+        there = (here + STEP_DT * fast) * (inside if keep is None else inside * keep)
+        return there, fast[:, 0:cols], hit[:, 0:cols], gaps[2, band, :, 0:cols] - STEP_DT * push[:, 0:cols]
+
+    for n in (-1, 0, blocks - 1, blocks):
+        end = 0 if n < 1 else 1
+        at = 8 * n + 16 if end == 0 else 8 * n - rows + 16
+        bending = bending_of(lambda o: rim[end, at + o : at + o + 8, :])
+        steady = rim_v[end, at - 8 : at, :] - (STEP_DT * BEND) * bending
+        keep = None
         if n < 0:
-            keep = inside * jnp.where(place.gx > 0, 1.0, 0.0)
+            keep = jnp.where(place.gx > 0, 1.0, 0.0)
         elif n == blocks:
-            keep = inside * jnp.where(place.gx < place.nx - 1, 1.0, 0.0)
-        there = (here + STEP_DT * fast) * keep
+            keep = jnp.where(place.gx < place.nx - 1, 1.0, 0.0)
+        there, *rest = first_rows(n, rim[end, at : at + 8, :], steady, keep)
         for part in (-1, 0, 1):
             if 0 <= n - part < blocks:
                 panes[n - part, 8 + 8 * part : 16 + 8 * part, :] = there
         if 0 <= n < blocks:
-            fasts[n] = fast[:, 0:cols]
-            hits[n] = hit[:, 0:cols]
-            goals[n] = gaps[2, band, :, 0:cols] - STEP_DT * push[:, 0:cols]
+            fasts[n], hits[n], goals[n] = rest
+
+    def inner_block(n):
+        at = pl.ds(pl.multiple_of(8 * n, 8), 8)
+        there, *rest = first_rows(n, jnp.concatenate([shell[at, :], strip_d[at, :]], axis=1), mid[n - 1])
+        for part in (-1, 0, 1):
+            panes[n - part, 8 + 8 * part : 16 + 8 * part, :] = there
+        fasts[n], hits[n], goals[n] = rest
+
+    @pl.loop(0, (blocks - 2) // 2)
+    def _(k):
+        inner_block(2 * k + 1)
+        inner_block(2 * k + 2)
 
     lane, sub = lanes(), subs()
     west, east = place.gy == 0, place.gy == place.ny - 1
@@ -794,40 +806,32 @@
     high = lane >= PTS // 2
     segment = ((lane + 16) >> 5) & 3
 
-    def side_row(end, part):
-        return jnp.where(leftward[0:1], halo[end, 72 + part : 73 + part, :], halo[end, 64 + part : 65 + part, :])
-
     def near_row(a, part):
         at = 8 * part + a
         return jnp.where(leftward[0:1], left[at : at + 1], right[at : at + 1])
 
     border = (-1, 0, last, rows_a)
     sides = {}
-    for part in range(6):
-        for a in border:
-            sides[a, part] = near_row(a, part) if 0 <= a <= last else side_row(0 if a < 0 else 1, part)
+    for f in range(2):
+        for a in (0, last):
+            rest = near_row(a, 4 + f)
+            whole = rest + near_row(a, f)
+            sides[a, f] = (rest, whole, whole + STEP_DT * near_row(a, 2 + f))
+        for a, end in ((-1, 0), (rows_a, 1)):
+            sides[a, f] = [halo[end, SIDE_AT + 2 * n + f : SIDE_AT + 2 * n + f + 1, :] for n in range(3)]
     lead_side, far_lead = {}, {}
     straight = SIDEWAYS.index(0)
-    turned = flips(
-        [
-            piece
-            for end in (0, 1)
-            for f in range(2)
-            for rest in (halo[end, 32 + 8 * f : 40 + 8 * f, :],)
-            for whole in (rest + halo[end, 8 * f : 8 * f + 8, :],)
-            for piece in (rest, whole, whole + STEP_DT * halo[end, 16 + 8 * f : 24 + 8 * f, :])
-        ]
-    )
     for f in range(2):
         for a in border:
-            lead_side[f, a] = side_columns(sides[a, 4 + f] + sides[a, f] + STEP_DT * sides[a, 2 + f])
-        for end in (0, 1):
-            far_lead[f, end] = turned[6 * end + 3 * f + 2]
+            lead_side[f, a] = side_columns(sides[a, f][2])
+        at = LEAD_AT + 3 * f
+        far_lead[f, 0], far_lead[f, 1] = halo[0, at - 5 : at + 3, :], halo[1, at : at + 8, :]
         for field in (f, 2 + f):
             cells, near = {}, {}
             for a in border:
-                near[a] = side_columns(sides[a, 4 + f] + sides[a, f] if field >= 2 else sides[a, 4 + f])
-            cells[-1], cells[rows_a] = (turned[6 * end + 3 * f + field // 2] for end in (0, 1))
+                near[a] = side_columns(sides[a, f][field // 2])
+            at = ROWS_AT + 6 * field
+            cells[-1], cells[rows_a] = halo[0, at - 2 : at + 6, :], halo[1, at : at + 8, :]
             cells[0] = win[field, straight, 0, 0:8, :]
             cells[last] = win[field, straight, rows_a - 2, 8:16, :]
             for n, oy in enumerate(SIDEWAYS):
@@ -848,7 +852,8 @@
                 for n, oy in enumerate(SIDEWAYS):
                     seams[field, n, 8 * half : 8 * half + 8, :] = turn(seam, -oy)
     for end in (0, 1):
-        packed = joined(halo[end, 48:56, :], halo[end, 56:64, :])
+        packed = halo[end, WORD_AT : WORD_AT + 8, :]
+        packed = joined(packed, turn(packed, -16))
         for dx in (-1, 0, 1):
             for dy in (-1, 0, 1):
                 s = slot(dx, dy)
@@ -857,18 +862,18 @@
                     word = jnp.where((lane < TILE_Y) & west, 0, word)
                 if dy > 0:
                     word = jnp.where((lane >= PTS - TILE_Y) & east, 0, word)
-                pair = (word, ends_w[s, 0]) if end == 0 else (ends_w[s, 1], word)
+                pair = (word, rows_w[s, 0]) if end == 0 else (rows_w[s, last], word)
                 ewords[s, end] = jnp.where(sub < TILE_X - FROM, *pair)
     parts = []
     for at in (0, 1):
         rows_w = []
         for a in (-1, last, 0, rows_a):
-            for values, part in ((left, 72), (right, 64)):
+            for n, values in enumerate((left, right)):
                 if 0 <= a <= last:
                     rows_w.append(values[48 + 8 * at + a : 49 + 8 * at + a])
                 else:
-                    end = 0 if a < 0 else 1
-                    rows_w.append(halo[end, part + 6 + at : part + 7 + at, :])
+                    row = SIDE_AT + 6 + 2 * n + at
+                    rows_w.append(halo[0 if a < 0 else 1, row : row + 1, :])
         parts.append(jnp.concatenate(rows_w, axis=0))
     packed = joined(*parts)
     for dx in (-1, 0, 1):
@@ -954,11 +959,18 @@
     inner = rows_a - 1
     each = blocks // rows_a
 
-    @pl.loop(0, inner)
-    def _(k):
-        second_group(k + 1, lambda number: (weights[number, k], levels[number, k]))
-        for part in range(each):
-            second_rows(each * k + part)
+    @pl.loop(0, inner // 2)
+    def _(j):
+        for h in range(2):
+            k = 2 * j + h
+            second_group(k + 1, lambda number: (weights[number, k], levels[number, k]))
+            for part in range(each):
+                second_rows(each * k + part)
+
+    k = inner - 1
+    second_group(k + 1, lambda number: (weights[number, k], levels[number, k]))
+    for part in range(each):
+        second_rows(each * k + part)
 
     tail = blocks - each * inner
     half = -(-tail // 2)
@@ -974,9 +986,9 @@
 
     for f in range(2):
         thens = flips([flat2[f, 8 * a + 11 : 8 * a + 19, :] for a in range(rows_a)])
-        end_was = flips([flat[f, 8 * a + 11 : 8 * a + 19, :] for a in (0, last)])
+        wases = flips([flat[f, 8 * a + 11 : 8 * a + 19, :] for a in range(rows_a)])
         for a in range(rows_a):
-            was = end_was[min(a, 1)] if a in (0, last) else tiles_f[f, a]
+            was = wases[a]
             then = thens[a]
             if f == 0 and a == last:
                 was = was - push
@@ -1045,14 +1057,13 @@
         ],
     )
 
-    shell, speed, lattice, lead, groups_w, ends_w, shore = call(
+    shell, speed, lattice, lead, rows_w, shore = call(
         functools.partial(own_parts, place_args),
         like(far_shell, far_speed)
         + [
             shaped(4, rows_a, 8),
             shaped(2, rows_a, 8),
-            shaped(9, span, 8, dtype=I32),
-            shaped(9, 2, 8, dtype=I32),
+            shaped(9, rows_a, 8, dtype=I32),
             shaped(2 * disp.shape[2]),
         ],
         [tall, tall, pltpu.VMEM((2, TILE_X, 8, cols), F32), pltpu.SemaphoreType.DMA((4,))],
@@ -1069,7 +1080,7 @@
     outs = [shaped(CONTACT_ROWS + (HALO_ROWS if s & (s + 1) == 0 else 0)) for s in shifts]
     *ends, own, strip_d, strip_v = call(
         functools.partial(pack_ends, place_args, shifts),
-        outs + [shaped(2 * CONTACT_ROWS), shaped(rows), shaped(rows)],
+        outs + [shaped(2 * OWN_ROWS), shaped(rows), shaped(rows)],
         [
             pltpu.VMEM((4, len(SIDEWAYS), 24, PTS), F32),
             pltpu.VMEM((rows + 2 * PAD, PTS), F32),
@@ -1079,7 +1090,8 @@
         shell,
         speed,
         lattice,
-        ends_w,
+        lead,
+        rows_w,
         shore,
         first,
         second,
@@ -1094,20 +1106,21 @@
             shaped(count, span, 8),
             shaped(2, 8 * (rows_a + 3)),
             shaped(2, rows_a, 8),
-            shaped(2, rows_a, 8),
             jax.ShapeDtypeStruct((blocks - 2, 8, WIDE), F32),
         ],
         [
             pltpu.VMEM((4, 3, 24, PTS), F32),
             pltpu.VMEM((9, 8, PTS), I32),
             pltpu.VMEM((blocks - 2, 24, WIDE), F32),
+            pltpu.VMEM((2, 8, PTS), F32),
+            pltpu.VMEM((6, 8, PTS), F32),
         ],
         disp,
         jit,
         shell,
         speed,
         lattice,
-        groups_w,
+        rows_w,
         first,
         second,
         strip_d,
@@ -1152,7 +1165,7 @@
             strip_d,
             strip_v,
             lead,
-            ends_w,
+            rows_w,
             *inner,
             *ends,
             out_specs=[pl.BlockSpec(memory_space=pltpu.MemorySpace.HBM)] * 4,

time: 20.9 us -> 20 us (0.957)
  Pallas kernels: 13.3 us -> 12.5 us
    pallas_call x5, Pallas kernels: 13.3 us -> 12.5 us  [call(): pl.pallas_call(body, out_shape=out, in_specs=specs, scratch_shapes=scratc...]
  transfers between devices with their start and end apart: 5 -> 5, of which waited for: 0 -> 0; matrix products, arithmetic and copies ran while one was open for 0% -> 0% of each run, Pallas kernels for 30% -> 29%
where the time goes in v6:
time: 20 us; the launch traced here: 19.8 us
  Pallas kernels  12.5 us (62%)
  starting transfers between devices  6.64 us (33%)
  between operations  0.7 us (4%)
    pallas_call x5, Pallas kernels, call(): pl.pallas_call(body, out_shape=out, in_specs=specs, scratch_shapes=scratc...  12.5 us
    ppermute x3, starting transfers between devices, on_device(): lax.ppermute(e, 'gx', [(i, i ^ s) for i in range(nx)])  3.55 us
    ppermute x1, starting transfers between devices, on_device(): lax.ppermute(second, ('gx', 'gy'), [(i * ny + j, i * ny + (j - 1 ^ 1) + 1...  2.56 us
    ppermute x1, starting transfers between devices, on_device(): first = lax.ppermute(first, 'gy', [(i, i ^ 1) for i in range(ny)])  0.52 us
  transfers between devices with their start and end apart: 5, of which 0 were waited for; matrix products, arithmetic and copies ran while one was open for 0% of the time, Pallas kernels for 29%

profile of v6, /device:TPU:0, one launch (start us, length us, event | category | flops | bytes accessed | tf_op | source)
XLA Modules:
  0.0 19.8 jit_solution(11044422417320165338)
XLA Ops:
  0.6 1.5 %shard_map.111 = (f32[88,128]{1,0:T(8,128)S(1)}, f32[88,128]{1,0:T(8,128)S(1)}, f32[2,8,8,128]{3,2,1,0:T(8,128)S(1)}, f32[2,8,8,128]{3,2,1,0:T(8,128)S(1)}, f32[...) custom-call(f32[2,8,8,128]{3,2,1,0:T(8,128)} %refs_0_.1, ...), custom_call_target="tpu_custom_call" | custom-call | tf_op jit(solution)/shard_map/pallas_call | solution.py:1019
  2.2 0.5 %collective-permute-start = (f32[88,128]{1,0:T(8,128)S(1)}, f32[88,128]{1,0:T(8,128)S(1)}, u32[]{:S(2)}, u32[]{:S(2)}) collective-permute-start(f32[88,128]{1,0:T(8,128)S(1)} %get-tuple-element.38), channel_id=1, source_target_pairs={{0,1},{1,0},{2,3},{3,2},{4,5},{5,4},{6,7},{7,6},{8,9},{9,8},{10,11... | collective-permute-start | bytes 135176 | tf_op jit(solution)/shard_map/ppermute | solution.py:1049
  2.7 2.6 %collective-permute-start.1 = (f32[88,128]{1,0:T(8,128)S(1)}, f32[88,128]{1,0:T(8,128)S(1)}, u32[]{:S(2)}, u32[]{:S(2)}) collective-permute-start(f32[88,128]{1,0:T(8,128)S(1)} %get-tuple-element.39), channel_id=1, source_target_pairs={{0,8},{1,2},{2,1},{3,4},{4,3},{5,6},{6,5},{7,15},{8,0},{9,10},{10,... | collective-permute-start | bytes 135176 | tf_op jit(solution)/shard_map/ppermute | solution.py:1050
  5.3 2.3 %shard_map.112 = (f32[128,512]{1,0:T(8,128)S(1)}, f32[128,512]{1,0:T(8,128)S(1)}, f32[4,8,8,128]{3,2,1,0:T(8,128)S(1)}, f32[2,8,8,128]{3,2,1,0:T(8,128)S(1)}, s3...) custom-call(f32[128,512]{1,0:T(8,128)} %far_shell.1, f32[128,512]{1,0:T(8,128)} %far_speed.1, ...), custom_call_target="tpu_custom_call" | custom-call | tf_op jit(solution)/shard_map/pallas_call | solution.py:1019
  7.5 0.0 collective-permute-done.first.refs_6_
  7.6 0.0 collective-permute-done.1.second.refs_7_
  7.6 0.7 %shard_map.113 = (f32[98,128]{1,0:T(8,128)S(1)}, f32[18,128]{1,0:T(8,128)S(1)}, f32[98,128]{1,0:T(8,128)S(1)}, f32[48,128]{1,0:T(8,128)S(1)}, f32[128,128]{1,0:T(8,128)S(1)}, /*index=5*/f32[128,128]{1,0:T(8,128)S(1)}) custom-call(f32[2,8,8,128]{3,2,1,0:T(8,128)S(1)} %get-tuple-element.30.disp.refs_0_, f32[2,8,8,128]{3,2,1,0:T(8,128)S(1)} %get-tuple-element.31.vel.refs_1_, ...), custom_call_target="tpu_custom_call" | custom-call | tf_op jit(solution)/shard_map/pallas_call | solution.py:1019
  8.3 1.8 %collective-permute-start.2 = (f32[98,128]{1,0:T(8,128)S(1)}, f32[98,128]{1,0:T(8,128)S(1)}, u32[]{:S(2)}, u32[]{:S(2)}) collective-permute-start(f32[98,128]{1,0:T(8,128)S(1)} %get-tuple-element.53), channel_id=1, source_target_pairs={{0,8},{8,0},{16,24},{24,16},{1,9},{9,1},{17,25},{25,17},{2,10},{10... | collective-permute-start | bytes 150536 | tf_op jit(solution)/shard_map/ppermute | solution.py:1099
  10.1 1.5 %collective-permute-start.4 = (f32[98,128]{1,0:T(8,128)S(1)}, f32[98,128]{1,0:T(8,128)S(1)}, u32[]{:S(2)}, u32[]{:S(2)}) collective-permute-start(f32[98,128]{1,0:T(8,128)S(1)} %get-tuple-element.55), channel_id=1, source_target_pairs={{0,24},{8,16},{16,8},{24,0},{1,25},{9,17},{17,9},{25,1},{2,26},{10... | collective-permute-start | bytes 150536 | tf_op jit(solution)/shard_map/ppermute | solution.py:1099
  11.6 0.3 %collective-permute-start.3 = (f32[18,128]{1,0:T(8,128)S(1)}, f32[18,128]{1,0:T(8,128)S(1)}, u32[]{:S(2)}, u32[]{:S(2)}) collective-permute-start(f32[18,128]{1,0:T(8,128)S(1)} %get-tuple-element.54), channel_id=1, source_target_pairs={{0,16},{8,24},{16,0},{24,8},{1,17},{9,25},{17,1},{25,9},{2,18},{10... | collective-permute-start | bytes 27656 | tf_op jit(solution)/shard_map/ppermute | solution.py:1099
  11.8 3.5 %shard_map.114 = (f32[4,7,7,16,128]{4,3,2,1,0:T(8,128)S(1)}, f32[44,7,8,128]{3,2,1,0:T(8,128)S(1)}, f32[44,7,8,128]{3,2,1,0:T(8,128)S(1)}, f32[2,88,128]{2,1,0:T...) custom-call(f32[2,8,8,128]{3,2,1,0:T(8,128)S(1)} %get-tuple-element.30.disp.refs_0_, ...), custom_call_target="tpu_custom_call" | custom-call | tf_op jit(solution)/shard_map/pallas_call | solution.py:1019
  15.3 0.0 collective-permute-done.3.refs_20_
  15.3 0.0 collective-permute-done.2.refs_19_
  15.3 0.0 collective-permute-done.4.refs_21_
  15.3 4.5 %shard_map.115 = (f32[2,8,8,128]{3,2,1,0:T(8,128)}, f32[2,8,8,128]{3,2,1,0:T(8,128)}, f32[128,512]{1,0:T(8,128)}, f32[128,512]{1,0:T(8,128)}) custom-call(f32[2,8,8,128]{3,2,1,0:T(8,128)S(1)} %get-tuple-element.30.disp.refs_0_, f32[2,8,8,128]{3,2,1,0:T(8,128)S(1)} %get-tuple-element.31.vel.refs_1_, s32[8,128]{1,0:T(8,128)S(1)} %get-tuple-element.32.node.refs_2_, ...), custom_call_target="tpu_custom_call" | custom-call | tf_op jit(solution)/shard_map/pallas_call | solution.py:1019
Async XLA Ops:
  2.2 5.4 %collective-permute-start = (f32[88,128]{1,0:T(8,128)S(1)}, f32[88,128]{1,0:T(8,128)S(1)}, u32[]{:S(2)}, u32[]{:S(2)}) collective-permute-start(f32[88,128]{1,0:T(8,128)S(1)} %get-tuple-element.38), channel_id=1, source_target_pairs={{0,1},{1,0},{2,3},{3,2},{4,5},{5,4},{6,7},{7,6},{8,9},{9,8},{10,11... | collective-permute-start | bytes 135176 | tf_op jit(solution)/shard_map/ppermute | solution.py:1049
  2.7 4.9 %collective-permute-start.1 = (f32[88,128]{1,0:T(8,128)S(1)}, f32[88,128]{1,0:T(8,128)S(1)}, u32[]{:S(2)}, u32[]{:S(2)}) collective-permute-start(f32[88,128]{1,0:T(8,128)S(1)} %get-tuple-element.39), channel_id=1, source_target_pairs={{0,8},{1,2},{2,1},{3,4},{4,3},{5,6},{6,5},{7,15},{8,0},{9,10},{10,... | collective-permute-start | bytes 135176 | tf_op jit(solution)/shard_map/ppermute | solution.py:1050
  8.3 7.0 %collective-permute-start.2 = (f32[98,128]{1,0:T(8,128)S(1)}, f32[98,128]{1,0:T(8,128)S(1)}, u32[]{:S(2)}, u32[]{:S(2)}) collective-permute-start(f32[98,128]{1,0:T(8,128)S(1)} %get-tuple-element.53), channel_id=1, source_target_pairs={{0,8},{8,0},{16,24},{24,16},{1,9},{9,1},{17,25},{25,17},{2,10},{10... | collective-permute-start | bytes 150536 | tf_op jit(solution)/shard_map/ppermute | solution.py:1099
  10.1 5.2 %collective-permute-start.4 = (f32[98,128]{1,0:T(8,128)S(1)}, f32[98,128]{1,0:T(8,128)S(1)}, u32[]{:S(2)}, u32[]{:S(2)}) collective-permute-start(f32[98,128]{1,0:T(8,128)S(1)} %get-tuple-element.55), channel_id=1, source_target_pairs={{0,24},{8,16},{16,8},{24,0},{1,25},{9,17},{17,9},{25,1},{2,26},{10... | collective-permute-start | bytes 150536 | tf_op jit(solution)/shard_map/ppermute | solution.py:1099
  11.6 3.7 %collective-permute-start.3 = (f32[18,128]{1,0:T(8,128)S(1)}, f32[18,128]{1,0:T(8,128)S(1)}, u32[]{:S(2)}, u32[]{:S(2)}) collective-permute-start(f32[18,128]{1,0:T(8,128)S(1)} %get-tuple-element.54), channel_id=1, source_target_pairs={{0,16},{8,24},{16,0},{24,8},{1,17},{9,25},{17,1},{25,9},{2,18},{10... | collective-permute-start | bytes 27656 | tf_op jit(solution)/shard_map/ppermute | solution.py:1099

commit v7 on v6

--- a/solution.py
+++ b/solution.py
@@ -701,9 +701,10 @@
     targets = refs[19 + len(shifts) : 23 + len(shifts)]
     scratch = refs[23 + len(shifts) :]
     out_disp, out_vel, out_shell, out_speed, gaps, halo, rim, rim_v, panes, fasts, hits, goals, ewin, ewords = scratch[:14]
-    eweights, elevels, flat, flat2, seams, kinds, swin, sems = scratch[14:]
+    eweights, elevels, flat, flat2, seams, kinds, swin, cast, sems = scratch[14:]
     outs = (out_disp, out_vel, out_shell, out_speed)
-    copies = [pltpu.make_async_copy(x, y, sems.at[n]) for n, (x, y) in enumerate(zip(outs, targets))]
+    pairs = [(x.at[f], y.at[f]) for x, y in zip(outs[:2], targets[:2]) for f in range(2)] + list(zip(outs[2:], targets[2:]))
+    copies = [pltpu.make_async_copy(x, y, sems.at[n]) for n, (x, y) in enumerate(pairs)]
     rows_a, tiles = disp.shape[1], disp.shape[2]
     rows, cols = place.shell_rows, place.shell_cols
     blocks = rows // 8
@@ -930,7 +931,13 @@
             cells = cells + square * flat[f, 8 * a + 11 : 8 * a + 19, :]
             if a == last and f == 0:
                 cells = cells - square * push_rows
-            near = nears[a] if a in nears else beside[f, a]
+            cast[f, 0, a + 1] = cells
+            cast[f, 1, a + 1] = nears[a] if a in nears else beside[f, a]
+
+    @pl.loop(0, 2)
+    def _(f):
+        for a in range(-1, rows_a + 1):
+            cells, near = cast[f, 0, a + 1], cast[f, 1, a + 1]
             for n, oy in enumerate(SIDEWAYS):
                 shifted = sideways(cells, near, oy)
                 if a < rows_a:
@@ -981,8 +988,8 @@
         for part in range(half):
             second_rows(jnp.minimum(each * inner + half * e + part, blocks - 1))
 
-    copies[2].start()
-    copies[3].start()
+    copies[4].start()
+    copies[5].start()
 
     for f in range(2):
         thens = flips([flat2[f, 8 * a + 11 : 8 * a + 19, :] for a in range(rows_a)])
@@ -999,8 +1006,8 @@
             faster = fast + STEP_DT * then
             out_vel[f, a] = faster
             out_disp[f, a] = disp[f, a] + STEP_DT * (fast + faster)
-    copies[0].start()
-    copies[1].start()
+        copies[f].start()
+        copies[2 + f].start()
     for copy in copies:
         copy.wait()
 
@@ -1096,7 +1103,18 @@
         first,
         second,
     )
-    ends = [lax.ppermute(e, "gx", [(i, i ^ s) for i in range(nx)]) for s, e in zip(shifts, ends)]
+    ends = [
+        lax.ppermute(
+            e,
+            ("gx", "gy"),
+            [
+                (i * ny + j, i * ny + (j ^ 1) if s & (s + 1) and nx - 1 not in (i, i ^ s) else (i ^ s) * ny + j)
+                for i in range(nx)
+                for j in range(ny)
+            ],
+        )
+        for s, e in zip(shifts, ends)
+    ]
 
     inner = call(
         functools.partial(inner_rows, place_args),
@@ -1146,7 +1164,8 @@
         pltpu.VMEM((4, len(SIDEWAYS), 16, PTS), F32),
         pltpu.VMEM((9, 8, PTS), I32),
         pltpu.VMEM((2, len(SIDEWAYS), rows_a + 1, 16, PTS), F32),
-        pltpu.SemaphoreType.DMA((4,)),
+        pltpu.VMEM((2, 2, rows_a + 2, 8, PTS), F32),
+        pltpu.SemaphoreType.DMA((6,)),
     ]
     return tuple(
         call(

time: 20 us -> 19.7 us (0.985)
  starting transfers between devices: 6.64 us -> 6.37 us
    ppermute x3, starting transfers between devices: 3.55 us -> 3.29 us  [on_device(): lax.ppermute(e, ('gx', 'gy'), [(i * ny + j, i * ny + (j ^ 1) if s & s + 1...]
  transfers between devices with their start and end apart: 5 -> 5, of which waited for: 0 -> 1; matrix products, arithmetic and copies ran while one was open for 0% -> 0% of each run, Pallas kernels for 29% -> 29%
where the time goes in v7:
time: 19.7 us; the launch traced here: 19.5 us
  Pallas kernels  12.4 us (63%)
  starting transfers between devices  6.37 us (32%)
  between operations  0.69 us (4%)
    pallas_call x5, Pallas kernels, call(): pl.pallas_call(body, out_shape=out, in_specs=specs, scratch_shapes=scratc...  12.4 us
    ppermute x3, starting transfers between devices, on_device(): lax.ppermute(e, ('gx', 'gy'), [(i * ny + j, i * ny + (j ^ 1) if s & s + 1...  3.29 us
    ppermute x1, starting transfers between devices, on_device(): lax.ppermute(second, ('gx', 'gy'), [(i * ny + j, i * ny + (j - 1 ^ 1) + 1...  2.56 us
    ppermute x1, starting transfers between devices, on_device(): first = lax.ppermute(first, 'gy', [(i, i ^ 1) for i in range(ny)])  0.52 us
  transfers between devices with their start and end apart: 5, of which 1 were waited for; matrix products, arithmetic and copies ran while one was open for 0% of the time, Pallas kernels for 29%

profile of v7, /device:TPU:0, one launch (start us, length us, event | category | flops | bytes accessed | tf_op | source)
XLA Modules:
  0.0 19.5 jit_solution(6213521739538945611)
XLA Ops:
  0.6 1.5 %shard_map.111 = (f32[88,128]{1,0:T(8,128)S(1)}, f32[88,128]{1,0:T(8,128)S(1)}, f32[2,8,8,128]{3,2,1,0:T(8,128)S(1)}, f32[2,8,8,128]{3,2,1,0:T(8,128)S(1)}, f32[...) custom-call(f32[2,8,8,128]{3,2,1,0:T(8,128)} %refs_0_.1, ...), custom_call_target="tpu_custom_call" | custom-call | tf_op jit(solution)/shard_map/pallas_call | solution.py:1026
  2.2 0.5 %collective-permute-start = (f32[88,128]{1,0:T(8,128)S(1)}, f32[88,128]{1,0:T(8,128)S(1)}, u32[]{:S(2)}, u32[]{:S(2)}) collective-permute-start(f32[88,128]{1,0:T(8,128)S(1)} %get-tuple-element.38), channel_id=1, source_target_pairs={{0,1},{1,0},{2,3},{3,2},{4,5},{5,4},{6,7},{7,6},{8,9},{9,8},{10,11... | collective-permute-start | bytes 135176 | tf_op jit(solution)/shard_map/ppermute | solution.py:1056
  2.7 2.6 %collective-permute-start.1 = (f32[88,128]{1,0:T(8,128)S(1)}, f32[88,128]{1,0:T(8,128)S(1)}, u32[]{:S(2)}, u32[]{:S(2)}) collective-permute-start(f32[88,128]{1,0:T(8,128)S(1)} %get-tuple-element.39), channel_id=1, source_target_pairs={{0,8},{1,2},{2,1},{3,4},{4,3},{5,6},{6,5},{7,15},{8,0},{9,10},{10,... | collective-permute-start | bytes 135176 | tf_op jit(solution)/shard_map/ppermute | solution.py:1057
  5.3 2.3 %shard_map.112 = (f32[128,512]{1,0:T(8,128)S(1)}, f32[128,512]{1,0:T(8,128)S(1)}, f32[4,8,8,128]{3,2,1,0:T(8,128)S(1)}, f32[2,8,8,128]{3,2,1,0:T(8,128)S(1)}, s3...) custom-call(f32[128,512]{1,0:T(8,128)} %far_shell.1, f32[128,512]{1,0:T(8,128)} %far_speed.1, ...), custom_call_target="tpu_custom_call" | custom-call | tf_op jit(solution)/shard_map/pallas_call | solution.py:1026
  7.5 0.0 collective-permute-done.first.refs_6_
  7.6 0.0 collective-permute-done.1.second.refs_7_
  7.6 0.7 %shard_map.113 = (f32[98,128]{1,0:T(8,128)S(1)}, f32[18,128]{1,0:T(8,128)S(1)}, f32[98,128]{1,0:T(8,128)S(1)}, f32[48,128]{1,0:T(8,128)S(1)}, f32[128,128]{1,0:T(8,128)S(1)}, /*index=5*/f32[128,128]{1,0:T(8,128)S(1)}) custom-call(f32[2,8,8,128]{3,2,1,0:T(8,128)S(1)} %get-tuple-element.30.disp.refs_0_, f32[2,8,8,128]{3,2,1,0:T(8,128)S(1)} %get-tuple-element.31.vel.refs_1_, ...), custom_call_target="tpu_custom_call" | custom-call | tf_op jit(solution)/shard_map/pallas_call | solution.py:1026
  8.3 1.8 %collective-permute-start.2 = (f32[98,128]{1,0:T(8,128)S(1)}, f32[98,128]{1,0:T(8,128)S(1)}, u32[]{:S(2)}, u32[]{:S(2)}) collective-permute-start(f32[98,128]{1,0:T(8,128)S(1)} %get-tuple-element.53), channel_id=1, source_target_pairs={{0,8},{1,9},{2,10},{3,11},{4,12},{5,13},{6,14},{7,15},{8,0},{9,1},... | collective-permute-start | bytes 150536 | tf_op jit(solution)/shard_map/ppermute | solution.py:1107
  10.1 1.5 %collective-permute-start.4 = (f32[98,128]{1,0:T(8,128)S(1)}, f32[98,128]{1,0:T(8,128)S(1)}, u32[]{:S(2)}, u32[]{:S(2)}) collective-permute-start(f32[98,128]{1,0:T(8,128)S(1)} %get-tuple-element.55), channel_id=1, source_target_pairs={{0,24},{1,25},{2,26},{3,27},{4,28},{5,29},{6,30},{7,31},{8,16},{9,... | collective-permute-start | bytes 150536 | tf_op jit(solution)/shard_map/ppermute | solution.py:1107
  11.6 0.0 collective-permute-start.3
  11.6 3.5 %shard_map.114 = (f32[4,7,7,16,128]{4,3,2,1,0:T(8,128)S(1)}, f32[44,7,8,128]{3,2,1,0:T(8,128)S(1)}, f32[44,7,8,128]{3,2,1,0:T(8,128)S(1)}, f32[2,88,128]{2,1,0:T...) custom-call(f32[2,8,8,128]{3,2,1,0:T(8,128)S(1)} %get-tuple-element.30.disp.refs_0_, ...), custom_call_target="tpu_custom_call" | custom-call | tf_op jit(solution)/shard_map/pallas_call | solution.py:1026
  15.0 0.0 collective-permute-done.3.refs_20_
  15.1 0.0 collective-permute-done.2.refs_19_
  15.1 0.1 collective-permute-done.4.refs_21_
  15.1 4.4 %shard_map.115 = (f32[2,8,8,128]{3,2,1,0:T(8,128)}, f32[2,8,8,128]{3,2,1,0:T(8,128)}, f32[128,512]{1,0:T(8,128)}, f32[128,512]{1,0:T(8,128)}) custom-call(f32[2,8,8,128]{3,2,1,0:T(8,128)S(1)} %get-tuple-element.30.disp.refs_0_, f32[2,8,8,128]{3,2,1,0:T(8,128)S(1)} %get-tuple-element.31.vel.refs_1_, s32[8,128]{1,0:T(8,128)S(1)} %get-tuple-element.32.node.refs_2_, ...), custom_call_target="tpu_custom_call" | custom-call | tf_op jit(solution)/shard_map/pallas_call | solution.py:1026
Async XLA Ops:
  2.2 5.4 %collective-permute-start = (f32[88,128]{1,0:T(8,128)S(1)}, f32[88,128]{1,0:T(8,128)S(1)}, u32[]{:S(2)}, u32[]{:S(2)}) collective-permute-start(f32[88,128]{1,0:T(8,128)S(1)} %get-tuple-element.38), channel_id=1, source_target_pairs={{0,1},{1,0},{2,3},{3,2},{4,5},{5,4},{6,7},{7,6},{8,9},{9,8},{10,11... | collective-permute-start | bytes 135176 | tf_op jit(solution)/shard_map/ppermute | solution.py:1056
  2.7 4.9 %collective-permute-start.1 = (f32[88,128]{1,0:T(8,128)S(1)}, f32[88,128]{1,0:T(8,128)S(1)}, u32[]{:S(2)}, u32[]{:S(2)}) collective-permute-start(f32[88,128]{1,0:T(8,128)S(1)} %get-tuple-element.39), channel_id=1, source_target_pairs={{0,8},{1,2},{2,1},{3,4},{4,3},{5,6},{6,5},{7,15},{8,0},{9,10},{10,... | collective-permute-start | bytes 135176 | tf_op jit(solution)/shard_map/ppermute | solution.py:1057
  8.3 6.8 %collective-permute-start.2 = (f32[98,128]{1,0:T(8,128)S(1)}, f32[98,128]{1,0:T(8,128)S(1)}, u32[]{:S(2)}, u32[]{:S(2)}) collective-permute-start(f32[98,128]{1,0:T(8,128)S(1)} %get-tuple-element.53), channel_id=1, source_target_pairs={{0,8},{1,9},{2,10},{3,11},{4,12},{5,13},{6,14},{7,15},{8,0},{9,1},... | collective-permute-start | bytes 150536 | tf_op jit(solution)/shard_map/ppermute | solution.py:1107
  10.1 5.0 %collective-permute-start.4 = (f32[98,128]{1,0:T(8,128)S(1)}, f32[98,128]{1,0:T(8,128)S(1)}, u32[]{:S(2)}, u32[]{:S(2)}) collective-permute-start(f32[98,128]{1,0:T(8,128)S(1)} %get-tuple-element.55), channel_id=1, source_target_pairs={{0,24},{1,25},{2,26},{3,27},{4,28},{5,29},{6,30},{7,31},{8,16},{9,... | collective-permute-start | bytes 150536 | tf_op jit(solution)/shard_map/ppermute | solution.py:1107
  11.6 3.5 %collective-permute-start.3 = (f32[18,128]{1,0:T(8,128)S(1)}, f32[18,128]{1,0:T(8,128)S(1)}, u32[]{:S(2)}, u32[]{:S(2)}) collective-permute-start(f32[18,128]{1,0:T(8,128)S(1)} %get-tuple-element.54), channel_id=1, source_target_pairs={{0,1},{1,0},{2,3},{3,2},{4,5},{5,4},{6,7},{7,6},{8,24},{9,25},{10,... | collective-permute-start | bytes 27656 | tf_op jit(solution)/shard_map/ppermute | solution.py:1107

commit v8 on v7

--- a/solution.py
+++ b/solution.py
@@ -236,8 +236,8 @@
     return out
 
 
-def lay_out(ref, at, j, block):
-    for row in range(TILE_X):
+def lay_out(ref, at, j, block, count=TILE_X):
+    for row in range(count):
         ref[at + (row, slice(None), slice(j * PTS, (j + 1) * PTS))] = jnp.broadcast_to(block[row : row + 1], (8, PTS))
 
 
@@ -270,6 +270,12 @@
     def parts(self):
         inner = [list(range(p * self.band, (p + 1) * self.band, 8)) for p in range(self.bands)]
         return [[-8]] + inner + [[self.shell_rows]]
+
+    def met_bands(self, block):
+        return pltpu.roll(block, (TILE_X + 1 - self.gx * self.bands) & (TILE_X - 1), 0)
+
+    def met_band(self, row):
+        return (row + self.band) // self.band
 
     def band_of(self, row):
         return jnp.clip((self.gx * self.shell_rows + row + self.band) // self.band - 1, 0, TILE_X - 1)
@@ -402,8 +408,8 @@
     near_row = jnp.concatenate(at_row, axis=1)
     near_row = jnp.where(split < SPLIT // 2, turn(near_row, SPLIT), turn(near_row, -SPLIT))
     for j, block in enumerate(at_row):
-        lay_out(wide_ref, (0,), j, block)
-        lay_out(wide_ref, (1,), j, near_row[:, j * PTS : (j + 1) * PTS])
+        lay_out(wide_ref, (0,), j, place.met_bands(block), place.bands + 2)
+        lay_out(wide_ref, (1,), j, place.met_bands(near_row[:, j * PTS : (j + 1) * PTS]), place.bands + 2)
     for copy in copies:
         copy.wait()
     sub_wide = lax.broadcasted_iota(I32, (8, cols), 0)
@@ -420,8 +426,8 @@
             two = tall[at - 2 : at + 6, :] + tall[at + 2 : at + 10, :]
             beside = 2.0 * one - 8.0 * here
             later = here + STEP_DT * tall_v[at : at + 8, :] - square * (two - 8.0 * one + 20.0 * here)
-            hit = wide_ref[0, band] == row_wide + float(row)
-            near = wide_ref[1, band] == row_wide + float(row)
+            hit = wide_ref[0, place.met_band(row)] == row_wide + float(row)
+            near = wide_ref[1, place.met_band(row)] == row_wide + float(row)
             picks = ((hit, later), (hit, beside), (hit, here), (near, beside), (near, here))
             found = [x + jnp.where(mask, value, 0.0) for x, (mask, value) in zip(found, picks)]
         sums = [
@@ -753,17 +759,17 @@
     gap_rows = [contact[8 + b : 9 + b] for b in range(tiles)] + [contact[16:17], contact[17:18]]
     soon_rows = [contact[b : b + 1] for b in range(tiles)]
     for j, (nodes, gap) in enumerate(zip(widen(node_rows.__getitem__, 5), widen(gap_rows.__getitem__, 5))):
-        lay_out(gaps, (0,), j, nodes)
-        lay_out(gaps, (1,), j, gap)
+        lay_out(gaps, (0,), j, place.met_bands(nodes), place.bands + 2)
+        lay_out(gaps, (1,), j, place.met_bands(gap), place.bands + 2)
     for j, soon in enumerate(widen(soon_rows.__getitem__, 4)):
-        lay_out(gaps, (2,), j, soon)
+        lay_out(gaps, (2,), j, place.met_bands(soon), place.bands + 2)
     col = lax.broadcasted_iota(I32, (8, WIDE), 1)
     inside = jnp.where(col < cols, 1.0, 0.0)
     inside = jnp.where((col >= cols) & (col < cols + 64) & (place.gy < place.ny - 1), 1.0, inside)
     inside = jnp.where((col >= cols + 64) & (place.gy > 0), 1.0, inside)
 
     def first_rows(n, here, steady, keep=None):
-        band = place.band_of(8 * n)
+        band = place.met_band(8 * n)
         hit = jnp.where(gaps[0, band] == place.nodes(8 * n, WIDE), STEP_DT * PENALTY, 0.0)
         push = hit * jnp.maximum(gaps[1, band] - here, 0.0)
         fast = steady + push

time: 19.7 us -> 19.7 us (level)
  no operation moved by 1% of the time
where the time goes in v8:
time: 19.7 us; the launch traced here: 19.5 us
  Pallas kernels  12.3 us (62%)
  starting transfers between devices  6.38 us (32%)
  between operations  0.69 us (4%)
    pallas_call x5, Pallas kernels, call(): pl.pallas_call(body, out_shape=out, in_specs=specs, scratch_shapes=scratc...  12.3 us
    ppermute x3, starting transfers between devices, on_device(): lax.ppermute(e, ('gx', 'gy'), [(i * ny + j, i * ny + (j ^ 1) if s & s + 1...  3.3 us
    ppermute x1, starting transfers between devices, on_device(): lax.ppermute(second, ('gx', 'gy'), [(i * ny + j, i * ny + (j - 1 ^ 1) + 1...  2.56 us
    ppermute x1, starting transfers between devices, on_device(): first = lax.ppermute(first, 'gy', [(i, i ^ 1) for i in range(ny)])  0.52 us
  transfers between devices with their start and end apart: 5, of which 1 were waited for; matrix products, arithmetic and copies ran while one was open for 0% of the time, Pallas kernels for 29%

profile of v8, /device:TPU:0, one launch (start us, length us, event | category | flops | bytes accessed | tf_op | source)
XLA Modules:
  0.0 19.5 jit_solution(10183355645100169906)
XLA Ops:
  0.6 1.5 %shard_map.111 = (f32[88,128]{1,0:T(8,128)S(1)}, f32[88,128]{1,0:T(8,128)S(1)}, f32[2,8,8,128]{3,2,1,0:T(8,128)S(1)}, f32[2,8,8,128]{3,2,1,0:T(8,128)S(1)}, f32[...) custom-call(f32[2,8,8,128]{3,2,1,0:T(8,128)} %refs_0_.1, ...), custom_call_target="tpu_custom_call" | custom-call | tf_op jit(solution)/shard_map/pallas_call | solution.py:1032
  2.2 0.5 %collective-permute-start = (f32[88,128]{1,0:T(8,128)S(1)}, f32[88,128]{1,0:T(8,128)S(1)}, u32[]{:S(2)}, u32[]{:S(2)}) collective-permute-start(f32[88,128]{1,0:T(8,128)S(1)} %get-tuple-element.38), channel_id=1, source_target_pairs={{0,1},{1,0},{2,3},{3,2},{4,5},{5,4},{6,7},{7,6},{8,9},{9,8},{10,11... | collective-permute-start | bytes 135176 | tf_op jit(solution)/shard_map/ppermute | solution.py:1062
  2.7 2.6 %collective-permute-start.1 = (f32[88,128]{1,0:T(8,128)S(1)}, f32[88,128]{1,0:T(8,128)S(1)}, u32[]{:S(2)}, u32[]{:S(2)}) collective-permute-start(f32[88,128]{1,0:T(8,128)S(1)} %get-tuple-element.39), channel_id=1, source_target_pairs={{0,8},{1,2},{2,1},{3,4},{4,3},{5,6},{6,5},{7,15},{8,0},{9,10},{10,... | collective-permute-start | bytes 135176 | tf_op jit(solution)/shard_map/ppermute | solution.py:1063
  5.3 2.3 %shard_map.112 = (f32[128,512]{1,0:T(8,128)S(1)}, f32[128,512]{1,0:T(8,128)S(1)}, f32[4,8,8,128]{3,2,1,0:T(8,128)S(1)}, f32[2,8,8,128]{3,2,1,0:T(8,128)S(1)}, s3...) custom-call(f32[128,512]{1,0:T(8,128)} %far_shell.1, f32[128,512]{1,0:T(8,128)} %far_speed.1, ...), custom_call_target="tpu_custom_call" | custom-call | tf_op jit(solution)/shard_map/pallas_call | solution.py:1032
  7.5 0.0 collective-permute-done.first.refs_6_
  7.5 0.0 collective-permute-done.1.second.refs_7_
  7.6 0.7 %shard_map.113 = (f32[98,128]{1,0:T(8,128)S(1)}, f32[18,128]{1,0:T(8,128)S(1)}, f32[98,128]{1,0:T(8,128)S(1)}, f32[48,128]{1,0:T(8,128)S(1)}, f32[128,128]{1,0:T(8,128)S(1)}, /*index=5*/f32[128,128]{1,0:T(8,128)S(1)}) custom-call(f32[2,8,8,128]{3,2,1,0:T(8,128)S(1)} %get-tuple-element.30.disp.refs_0_, f32[2,8,8,128]{3,2,1,0:T(8,128)S(1)} %get-tuple-element.31.vel.refs_1_, ...), custom_call_target="tpu_custom_call" | custom-call | tf_op jit(solution)/shard_map/pallas_call | solution.py:1032
  8.3 1.8 %collective-permute-start.2 = (f32[98,128]{1,0:T(8,128)S(1)}, f32[98,128]{1,0:T(8,128)S(1)}, u32[]{:S(2)}, u32[]{:S(2)}) collective-permute-start(f32[98,128]{1,0:T(8,128)S(1)} %get-tuple-element.53), channel_id=1, source_target_pairs={{0,8},{1,9},{2,10},{3,11},{4,12},{5,13},{6,14},{7,15},{8,0},{9,1},... | collective-permute-start | bytes 150536 | tf_op jit(solution)/shard_map/ppermute | solution.py:1113
  10.1 1.5 %collective-permute-start.4 = (f32[98,128]{1,0:T(8,128)S(1)}, f32[98,128]{1,0:T(8,128)S(1)}, u32[]{:S(2)}, u32[]{:S(2)}) collective-permute-start(f32[98,128]{1,0:T(8,128)S(1)} %get-tuple-element.55), channel_id=1, source_target_pairs={{0,24},{1,25},{2,26},{3,27},{4,28},{5,29},{6,30},{7,31},{8,16},{9,... | collective-permute-start | bytes 150536 | tf_op jit(solution)/shard_map/ppermute | solution.py:1113
  11.6 0.0 collective-permute-start.3
  11.6 3.5 %shard_map.114 = (f32[4,7,7,16,128]{4,3,2,1,0:T(8,128)S(1)}, f32[44,7,8,128]{3,2,1,0:T(8,128)S(1)}, f32[44,7,8,128]{3,2,1,0:T(8,128)S(1)}, f32[2,88,128]{2,1,0:T...) custom-call(f32[2,8,8,128]{3,2,1,0:T(8,128)S(1)} %get-tuple-element.30.disp.refs_0_, ...), custom_call_target="tpu_custom_call" | custom-call | tf_op jit(solution)/shard_map/pallas_call | solution.py:1032
  15.0 0.0 collective-permute-done.3.refs_20_
  15.1 0.0 collective-permute-done.2.refs_19_
  15.1 0.1 collective-permute-done.4.refs_21_
  15.1 4.3 %shard_map.115 = (f32[2,8,8,128]{3,2,1,0:T(8,128)}, f32[2,8,8,128]{3,2,1,0:T(8,128)}, f32[128,512]{1,0:T(8,128)}, f32[128,512]{1,0:T(8,128)}) custom-call(f32[2,8,8,128]{3,2,1,0:T(8,128)S(1)} %get-tuple-element.30.disp.refs_0_, f32[2,8,8,128]{3,2,1,0:T(8,128)S(1)} %get-tuple-element.31.vel.refs_1_, s32[8,128]{1,0:T(8,128)S(1)} %get-tuple-element.32.node.refs_2_, ...), custom_call_target="tpu_custom_call" | custom-call | tf_op jit(solution)/shard_map/pallas_call | solution.py:1032
Async XLA Ops:
  2.2 5.4 %collective-permute-start = (f32[88,128]{1,0:T(8,128)S(1)}, f32[88,128]{1,0:T(8,128)S(1)}, u32[]{:S(2)}, u32[]{:S(2)}) collective-permute-start(f32[88,128]{1,0:T(8,128)S(1)} %get-tuple-element.38), channel_id=1, source_target_pairs={{0,1},{1,0},{2,3},{3,2},{4,5},{5,4},{6,7},{7,6},{8,9},{9,8},{10,11... | collective-permute-start | bytes 135176 | tf_op jit(solution)/shard_map/ppermute | solution.py:1062
  2.7 4.9 %collective-permute-start.1 = (f32[88,128]{1,0:T(8,128)S(1)}, f32[88,128]{1,0:T(8,128)S(1)}, u32[]{:S(2)}, u32[]{:S(2)}) collective-permute-start(f32[88,128]{1,0:T(8,128)S(1)} %get-tuple-element.39), channel_id=1, source_target_pairs={{0,8},{1,2},{2,1},{3,4},{4,3},{5,6},{6,5},{7,15},{8,0},{9,10},{10,... | collective-permute-start | bytes 135176 | tf_op jit(solution)/shard_map/ppermute | solution.py:1063
  8.3 6.8 %collective-permute-start.2 = (f32[98,128]{1,0:T(8,128)S(1)}, f32[98,128]{1,0:T(8,128)S(1)}, u32[]{:S(2)}, u32[]{:S(2)}) collective-permute-start(f32[98,128]{1,0:T(8,128)S(1)} %get-tuple-element.53), channel_id=1, source_target_pairs={{0,8},{1,9},{2,10},{3,11},{4,12},{5,13},{6,14},{7,15},{8,0},{9,1},... | collective-permute-start | bytes 150536 | tf_op jit(solution)/shard_map/ppermute | solution.py:1113
  10.1 5.0 %collective-permute-start.4 = (f32[98,128]{1,0:T(8,128)S(1)}, f32[98,128]{1,0:T(8,128)S(1)}, u32[]{:S(2)}, u32[]{:S(2)}) collective-permute-start(f32[98,128]{1,0:T(8,128)S(1)} %get-tuple-element.55), channel_id=1, source_target_pairs={{0,24},{1,25},{2,26},{3,27},{4,28},{5,29},{6,30},{7,31},{8,16},{9,... | collective-permute-start | bytes 150536 | tf_op jit(solution)/shard_map/ppermute | solution.py:1113
  11.6 3.5 %collective-permute-start.3 = (f32[18,128]{1,0:T(8,128)S(1)}, f32[18,128]{1,0:T(8,128)S(1)}, u32[]{:S(2)}, u32[]{:S(2)}) collective-permute-start(f32[18,128]{1,0:T(8,128)S(1)} %get-tuple-element.54), channel_id=1, source_target_pairs={{0,1},{1,0},{2,3},{3,2},{4,5},{5,4},{6,7},{7,6},{8,24},{9,25},{10,... | collective-permute-start | bytes 27656 | tf_op jit(solution)/shard_map/ppermute | solution.py:1113

commit v9 on v8

--- a/solution.py
+++ b/solution.py
@@ -308,14 +308,14 @@
     numbers = node[...].astype(F32)
     edge_blocks = (0, blocks - 1)
     for j in edge_blocks:
-        lay_out(wide_ref, (), j, widen(lambda b: numbers[b : b + 1], blocks)[j])
+        lay_out(wide_ref, (), j, place.met_bands(widen(lambda b: numbers[b : b + 1], blocks)[j]), place.bands + 2)
     held = {}
     for j in edge_blocks:
         total = jnp.zeros((8, PTS), F32)
         for part in range(place.bands):
             summed = jnp.zeros((8, PTS), F32)
             for row in range(part * place.band, (part + 1) * place.band, 8):
-                wanted = wide_ref[place.band_of(row), :, j * PTS : (j + 1) * PTS]
+                wanted = wide_ref[place.met_band(row), :, j * PTS : (j + 1) * PTS]
                 ids = place.nodes(row, PTS) + float(j * PTS)
                 summed = summed + jnp.where(wanted == ids, shell[min(j, 1), row : row + 8, :], 0.0)
             summed = jnp.sum(summed, axis=0, keepdims=True)
@@ -502,7 +502,7 @@
     numbers = node[...].astype(F32)
     blocks = widen(lambda b: numbers[b : b + 1], cols // PTS)
     low = lane < PTS // 2
-    lay_out(wide_ref, (), 0, jnp.where(low, blocks[0], blocks[-1]))
+    lay_out(wide_ref, (), 0, place.met_bands(jnp.where(low, blocks[0], blocks[-1])), place.bands + 2)
     far = jnp.where(low, 0.0, float(cols - PTS))
     ahead = jnp.zeros((8, PTS), F32)
     for part in place.parts():
@@ -514,7 +514,7 @@
             column = 2.0 * (tall[at - 1 : at + 7, :] + tall[at + 1 : at + 9, :]) - 8.0 * here
             from_left = turn(jnp.where(low, 0.0, column), 1) + turn(jnp.where(low, 0.0, here), 2)
             from_right = turn(jnp.where(low, column, 0.0), -1) + turn(jnp.where(low, here, 0.0), -2)
-            hit = wide_ref[band] == place.nodes(row, PTS) + far
+            hit = wide_ref[place.met_band(row)] == place.nodes(row, PTS) + far
             soon = soon + jnp.where(hit, jnp.where(low, from_left, from_right), 0.0)
         ahead = ahead + jnp.where(sub == band, jnp.sum(soon, axis=0, keepdims=True), 0.0)
     base = OWN_ROWS

time: 19.7 us -> 19.6 us (level)
  no operation moved by 1% of the time
where the time goes in v9:
time: 19.6 us; the launch traced here: 19.5 us
  Pallas kernels  12.3 us (63%)
  starting transfers between devices  6.38 us (33%)
  between operations  0.69 us (4%)
    pallas_call x5, Pallas kernels, call(): pl.pallas_call(body, out_shape=out, in_specs=specs, scratch_shapes=scratc...  12.3 us
    ppermute x3, starting transfers between devices, on_device(): lax.ppermute(e, ('gx', 'gy'), [(i * ny + j, i * ny + (j ^ 1) if s & s + 1...  3.3 us
    ppermute x1, starting transfers between devices, on_device(): lax.ppermute(second, ('gx', 'gy'), [(i * ny + j, i * ny + (j - 1 ^ 1) + 1...  2.56 us
    ppermute x1, starting transfers between devices, on_device(): first = lax.ppermute(first, 'gy', [(i, i ^ 1) for i in range(ny)])  0.52 us
  transfers between devices with their start and end apart: 5, of which 1 were waited for; matrix products, arithmetic and copies ran while one was open for 0% of the time, Pallas kernels for 29%

profile of v9, /device:TPU:0, one launch (start us, length us, event | category | flops | bytes accessed | tf_op | source)
XLA Modules:
  0.0 19.5 jit_solution(17129728136640983991)
XLA Ops:
  0.6 1.5 %shard_map.111 = (f32[88,128]{1,0:T(8,128)S(1)}, f32[88,128]{1,0:T(8,128)S(1)}, f32[2,8,8,128]{3,2,1,0:T(8,128)S(1)}, f32[2,8,8,128]{3,2,1,0:T(8,128)S(1)}, f32[...) custom-call(f32[2,8,8,128]{3,2,1,0:T(8,128)} %refs_0_.1, ...), custom_call_target="tpu_custom_call" | custom-call | tf_op jit(solution)/shard_map/pallas_call | solution.py:1032
  2.2 0.5 %collective-permute-start = (f32[88,128]{1,0:T(8,128)S(1)}, f32[88,128]{1,0:T(8,128)S(1)}, u32[]{:S(2)}, u32[]{:S(2)}) collective-permute-start(f32[88,128]{1,0:T(8,128)S(1)} %get-tuple-element.38), channel_id=1, source_target_pairs={{0,1},{1,0},{2,3},{3,2},{4,5},{5,4},{6,7},{7,6},{8,9},{9,8},{10,11... | collective-permute-start | bytes 135176 | tf_op jit(solution)/shard_map/ppermute | solution.py:1062
  2.7 2.6 %collective-permute-start.1 = (f32[88,128]{1,0:T(8,128)S(1)}, f32[88,128]{1,0:T(8,128)S(1)}, u32[]{:S(2)}, u32[]{:S(2)}) collective-permute-start(f32[88,128]{1,0:T(8,128)S(1)} %get-tuple-element.39), channel_id=1, source_target_pairs={{0,8},{1,2},{2,1},{3,4},{4,3},{5,6},{6,5},{7,15},{8,0},{9,10},{10,... | collective-permute-start | bytes 135176 | tf_op jit(solution)/shard_map/ppermute | solution.py:1063
  5.2 2.3 %shard_map.112 = (f32[128,512]{1,0:T(8,128)S(1)}, f32[128,512]{1,0:T(8,128)S(1)}, f32[4,8,8,128]{3,2,1,0:T(8,128)S(1)}, f32[2,8,8,128]{3,2,1,0:T(8,128)S(1)}, s3...) custom-call(f32[128,512]{1,0:T(8,128)} %far_shell.1, f32[128,512]{1,0:T(8,128)} %far_speed.1, ...), custom_call_target="tpu_custom_call" | custom-call | tf_op jit(solution)/shard_map/pallas_call | solution.py:1032
  7.5 0.0 collective-permute-done.first.refs_6_
  7.5 0.0 collective-permute-done.1.second.refs_7_
  7.5 0.7 %shard_map.113 = (f32[98,128]{1,0:T(8,128)S(1)}, f32[18,128]{1,0:T(8,128)S(1)}, f32[98,128]{1,0:T(8,128)S(1)}, f32[48,128]{1,0:T(8,128)S(1)}, f32[128,128]{1,0:T(8,128)S(1)}, /*index=5*/f32[128,128]{1,0:T(8,128)S(1)}) custom-call(f32[2,8,8,128]{3,2,1,0:T(8,128)S(1)} %get-tuple-element.30.disp.refs_0_, f32[2,8,8,128]{3,2,1,0:T(8,128)S(1)} %get-tuple-element.31.vel.refs_1_, ...), custom_call_target="tpu_custom_call" | custom-call | tf_op jit(solution)/shard_map/pallas_call | solution.py:1032
  8.3 1.8 %collective-permute-start.2 = (f32[98,128]{1,0:T(8,128)S(1)}, f32[98,128]{1,0:T(8,128)S(1)}, u32[]{:S(2)}, u32[]{:S(2)}) collective-permute-start(f32[98,128]{1,0:T(8,128)S(1)} %get-tuple-element.53), channel_id=1, source_target_pairs={{0,8},{1,9},{2,10},{3,11},{4,12},{5,13},{6,14},{7,15},{8,0},{9,1},... | collective-permute-start | bytes 150536 | tf_op jit(solution)/shard_map/ppermute | solution.py:1113
  10.1 1.5 %collective-permute-start.4 = (f32[98,128]{1,0:T(8,128)S(1)}, f32[98,128]{1,0:T(8,128)S(1)}, u32[]{:S(2)}, u32[]{:S(2)}) collective-permute-start(f32[98,128]{1,0:T(8,128)S(1)} %get-tuple-element.55), channel_id=1, source_target_pairs={{0,24},{1,25},{2,26},{3,27},{4,28},{5,29},{6,30},{7,31},{8,16},{9,... | collective-permute-start | bytes 150536 | tf_op jit(solution)/shard_map/ppermute | solution.py:1113
  11.6 0.0 collective-permute-start.3
  11.6 3.5 %shard_map.114 = (f32[4,7,7,16,128]{4,3,2,1,0:T(8,128)S(1)}, f32[44,7,8,128]{3,2,1,0:T(8,128)S(1)}, f32[44,7,8,128]{3,2,1,0:T(8,128)S(1)}, f32[2,88,128]{2,1,0:T...) custom-call(f32[2,8,8,128]{3,2,1,0:T(8,128)S(1)} %get-tuple-element.30.disp.refs_0_, ...), custom_call_target="tpu_custom_call" | custom-call | tf_op jit(solution)/shard_map/pallas_call | solution.py:1032
  15.0 0.0 collective-permute-done.3.refs_20_
  15.0 0.0 collective-permute-done.2.refs_19_
  15.0 0.1 collective-permute-done.4.refs_21_
  15.1 4.3 %shard_map.115 = (f32[2,8,8,128]{3,2,1,0:T(8,128)}, f32[2,8,8,128]{3,2,1,0:T(8,128)}, f32[128,512]{1,0:T(8,128)}, f32[128,512]{1,0:T(8,128)}) custom-call(f32[2,8,8,128]{3,2,1,0:T(8,128)S(1)} %get-tuple-element.30.disp.refs_0_, f32[2,8,8,128]{3,2,1,0:T(8,128)S(1)} %get-tuple-element.31.vel.refs_1_, s32[8,128]{1,0:T(8,128)S(1)} %get-tuple-element.32.node.refs_2_, ...), custom_call_target="tpu_custom_call" | custom-call | tf_op jit(solution)/shard_map/pallas_call | solution.py:1032
Async XLA Ops:
  2.2 5.4 %collective-permute-start = (f32[88,128]{1,0:T(8,128)S(1)}, f32[88,128]{1,0:T(8,128)S(1)}, u32[]{:S(2)}, u32[]{:S(2)}) collective-permute-start(f32[88,128]{1,0:T(8,128)S(1)} %get-tuple-element.38), channel_id=1, source_target_pairs={{0,1},{1,0},{2,3},{3,2},{4,5},{5,4},{6,7},{7,6},{8,9},{9,8},{10,11... | collective-permute-start | bytes 135176 | tf_op jit(solution)/shard_map/ppermute | solution.py:1062
  2.7 4.9 %collective-permute-start.1 = (f32[88,128]{1,0:T(8,128)S(1)}, f32[88,128]{1,0:T(8,128)S(1)}, u32[]{:S(2)}, u32[]{:S(2)}) collective-permute-start(f32[88,128]{1,0:T(8,128)S(1)} %get-tuple-element.39), channel_id=1, source_target_pairs={{0,8},{1,2},{2,1},{3,4},{4,3},{5,6},{6,5},{7,15},{8,0},{9,10},{10,... | collective-permute-start | bytes 135176 | tf_op jit(solution)/shard_map/ppermute | solution.py:1063
  8.3 6.8 %collective-permute-start.2 = (f32[98,128]{1,0:T(8,128)S(1)}, f32[98,128]{1,0:T(8,128)S(1)}, u32[]{:S(2)}, u32[]{:S(2)}) collective-permute-start(f32[98,128]{1,0:T(8,128)S(1)} %get-tuple-element.53), channel_id=1, source_target_pairs={{0,8},{1,9},{2,10},{3,11},{4,12},{5,13},{6,14},{7,15},{8,0},{9,1},... | collective-permute-start | bytes 150536 | tf_op jit(solution)/shard_map/ppermute | solution.py:1113
  10.1 5.0 %collective-permute-start.4 = (f32[98,128]{1,0:T(8,128)S(1)}, f32[98,128]{1,0:T(8,128)S(1)}, u32[]{:S(2)}, u32[]{:S(2)}) collective-permute-start(f32[98,128]{1,0:T(8,128)S(1)} %get-tuple-element.55), channel_id=1, source_target_pairs={{0,24},{1,25},{2,26},{3,27},{4,28},{5,29},{6,30},{7,31},{8,16},{9,... | collective-permute-start | bytes 150536 | tf_op jit(solution)/shard_map/ppermute | solution.py:1113
  11.6 3.5 %collective-permute-start.3 = (f32[18,128]{1,0:T(8,128)S(1)}, f32[18,128]{1,0:T(8,128)S(1)}, u32[]{:S(2)}, u32[]{:S(2)}) collective-permute-start(f32[18,128]{1,0:T(8,128)S(1)} %get-tuple-element.54), channel_id=1, source_target_pairs={{0,1},{1,0},{2,3},{3,2},{4,5},{5,4},{6,7},{7,6},{8,24},{9,25},{10,... | collective-permute-start | bytes 27656 | tf_op jit(solution)/shard_map/ppermute | solution.py:1113
